TPU v7x, 32 devices: a whole 2x2x4 slice. The times are simulated.
32 devices in a mesh: learn: 4 (over y, x), act: 8 (over z, core).
Axes of the slice: x: 2, y: 2, z: 4, core: 2. Of those that a mesh axis runs over, the one named last changes fastest.
Arguments:
- positions: int32 [2, 32, 361], P(None, ('learn', 'act')), may hold values from 0 to 2
- to_move: int32 [2, 32], P(None, ('learn', 'act')), may hold values from 0 to 1
- legal_moves: int32 [2, 32, 361], P(None, ('learn', 'act')), may hold values 0 or 1
- master: float32 [4, 2, 2304, 256], P('learn', None, 'act'), may hold values from -0.125 to 0.125
- gradients: float32 [4, 4, 2, 2304, 256], P('learn', None, None, 'act'), may hold values from -0.4375 to 0.4375
- stem_weight: bfloat16 [36, 256], replicated, may hold values from -1 to 1
- policy_weight: float32 [256], replicated, may hold values from -2 to 2
- pass_weight: float32 [256], replicated, may hold values from -2 to 2
- value_weight: float32 [256], replicated, may hold values from -0.375 to 0.375
Outputs:
- updated: float32 [4, 2, 2304, 256], P('learn', None, 'act')
- policy_logp: float32 [2, 32, 362], P(None, ('learn', 'act'))
- value: float32 [2, 32], P(None, ('learn', 'act'))
All inputs are finite; a program needn't handle non-finite values. No bound on the sum of `legal_moves` on one device may be relied on, other than what follows from the above.
Results may differ from a plain program's by a relative error of at most 0.008.
Values may be sent and summed in bfloat16 or wider, within the bound.
No kernel may reach another device: no remote copies, remote signals or barrier semaphores. Data moves between devices by JAX's collectives and lax.ppermute only.
A program may use at most 128 MiB of HBM per device.

v0:
```python
import jax
import jax.numpy as jnp
from jax import lax
from jax.sharding import PartitionSpec as P

BOARD = 19
CELLS = 361
PLANES = 4


def convolve(planes_in, kernel):
    padded = jnp.pad(planes_in, ((0, 0), (1, 1), (1, 1), (0, 0)))
    shifted = [
        padded[:, row_off : row_off + BOARD, col_off : col_off + BOARD, :]
        for row_off in range(3)
        for col_off in range(3)
    ]
    stacked = jnp.concatenate(shifted, axis=-1)
    unrolled = stacked.reshape(-1, stacked.shape[-1])
    result = jnp.dot(unrolled, kernel, preferred_element_type=jnp.float32)
    return result.reshape(planes_in.shape[0], BOARD, BOARD, kernel.shape[1])


def make_planes(boards, sides):
    side_move = sides[:, None]
    own_stones = boards == 1 + side_move
    foe_stones = boards == 2 - side_move
    vacant = boards == 0
    filled = jnp.ones_like(own_stones)
    stacked = jnp.stack([own_stones, foe_stones, vacant, filled], axis=-1).astype(jnp.bfloat16)
    return stacked.reshape(boards.shape[0], BOARD, BOARD, PLANES)


def heads(stream, legal_rows, policy_weight, pass_weight, value_weight):
    number = stream.shape[0]
    trunk_out = jax.nn.relu(stream).reshape(number, CELLS, stream.shape[-1])
    board_raw = jnp.einsum("pcd,d->pc", trunk_out, policy_weight, precision=lax.Precision.HIGHEST)
    pooled = jnp.mean(trunk_out, axis=1)
    pass_raw = jnp.dot(pooled, pass_weight, precision=lax.Precision.HIGHEST)
    value_raw = jnp.dot(pooled, value_weight, precision=lax.Precision.HIGHEST)
    logits = 10.0 * jnp.tanh(jnp.concatenate([board_raw, pass_raw[:, None]], axis=1) / 10.0)
    allowed = jnp.concatenate([legal_rows, jnp.ones((number, 1), jnp.int32)], axis=1) > 0
    exponent = jnp.where(allowed, jnp.exp(logits), 0.0)
    denominator = jnp.sum(exponent, axis=1, keepdims=True)
    logp = jnp.where(allowed, logits - jnp.log(denominator), 0.0)
    return (logp, jnp.tanh(value_raw))


def per_device(
    positions,
    to_move,
    legal_moves,
    master,
    gradients,
    stem_weight,
    policy_weight,
    pass_weight,
    value_weight,
):
    learner_part = gradients[0]
    gradient_sum = lax.psum_scatter(learner_part, "learn", scatter_dimension=0, tiled=True)
    learners = lax.axis_size("learn")
    updated = master - gradient_sum / learners
    sending = updated.astype(jnp.bfloat16)
    stacked = lax.all_gather(sending, "learn", axis=0, tiled=True)
    complete = lax.all_gather(stacked, "act", axis=2, tiled=True)
    steps_here = positions.shape[0]
    local_count = positions.shape[1]
    boards = positions.reshape(-1, CELLS)
    sides = to_move.reshape(-1)
    legal_flat = legal_moves.reshape(-1, CELLS)
    planes = make_planes(boards, sides)
    stream = convolve(planes, stem_weight)
    for layer in range(learners):
        kernels = complete[layer]
        activ = jax.nn.relu(stream).astype(jnp.bfloat16)
        middle = jax.nn.relu(convolve(activ, kernels[0])).astype(jnp.bfloat16)
        stream = stream + convolve(middle, kernels[1])
    logp, value_flat = heads(stream, legal_flat, policy_weight, pass_weight, value_weight)
    return (
        updated,
        logp.reshape(steps_here, local_count, CELLS + 1),
        value_flat.reshape(steps_here, local_count),
    )


def solution(mesh):
    in_specs = (
        P(None, ("learn", "act"), None),
        P(None, ("learn", "act")),
        P(None, ("learn", "act"), None),
        P("learn", None, "act", None),
        P("learn", None, None, "act", None),
        P(),
        P(),
        P(),
        P(),
    )
    out_specs = (
        P("learn", None, "act", None),
        P(None, ("learn", "act"), None),
        P(None, ("learn", "act")),
    )
    return jax.shard_map(
        per_device, mesh=mesh, in_specs=in_specs, out_specs=out_specs, check_vma=False
    )
```

profile of v0, /device:TPU:0, one launch (start us, length us, event | category | flops | bytes accessed | tf_op | source)
XLA Modules:
  0.0 204.4 jit_solution(7149888384381159362)
XLA Ops:
  7.3 0.7 reduce-scatter.4.cloned.1.call-update
  8.0 43.2 %reduce-scatter.4.cloned.1.call-done = f32[1,2,288,256]{3,2,1,0:T(8,128)} async-done(((f32[4,2,288,256]{3,2,1,0:T(8,128)}), f32[1,2,288,256]{3,2,1,0:T(8,128)}) %reduce-scatter.4.cloned.1.call-update) | async-done | bytes 589840
  51.2 2.2 %fusion.20 = (bf16[1,2,288,256]{3,2,1,0:T(8,128)(2,1)}, f32[1,2,288,256]{3,2,1,0:T(8,128)}) fusion(f32[1,2,288,256]{3,2,1,0:T(8,128)} %param.12, f32[1,2,288,256]{3,2,1,0:T(8,128)} %reduce-scatter.4.cloned.1.call-done), kind=kLoop, calls=%fused_computation.136 | loop fusion | flops 442368 | bytes 2064384 | tf_op jit(solution)/shard_map/convert_element_type | solution.py:64
  53.5 27.8 %all-gather.3.cloned.1.call-done = bf16[4,2,288,256]{3,2,1,0:T(8,128)(2,1)} async-done(((bf16[1,2,288,256]{3,2,1,0:T(8,128)(2,1)}), bf16[4,2,288,256]{3,2,1,0:T(8,128)(2,1)}) %all-gather.3.cloned.1.call-update) | async-done | bytes 1179664 | tf_op jit(solution)/shard_map/all_gather | solution.py:65
  82.8 0.3 maximum_convert_fusion.3
  83.2 0.9 slice_dynamic-update-slice_fusion.63
  84.1 0.9 slice_dynamic-update-slice_fusion.62
  85.0 1.0 slice_dynamic-update-slice_fusion.61
  86.0 1.0 slice_dynamic-update-slice_fusion.60
  86.9 0.8 constant_dynamic-update-slice_fusion.9
  87.8 1.0 slice_dynamic-update-slice_fusion.59
  88.8 1.0 slice_dynamic-update-slice_fusion.58
  89.8 0.8 slice_dynamic-update-slice_fusion.57
  90.7 1.0 slice_dynamic-update-slice_fusion.56
  91.7 82.1 %all-gather.5.cloned.1.call-done = bf16[4,2,2304,256]{3,2,1,0:T(8,128)(2,1)} async-done(((bf16[4,2,288,256]{3,2,1,0:T(8,128)(2,1)}), bf16[4,2,2304,256]{3,2,1,0:T(8,128)(2,1)}) %all-gather.5.cloned.1.call-update) | async-done | bytes 9437200 | tf_op jit(solution)/shard_map/all_gather | solution.py:66
  173.7 4.0 %fusion.1 = bf16[2,19,19,256]{3,2,1,0:T(8,128)(2,1)S(1)} fusion(bf16[2,19,19,2304]{3,2,1,0:T(8,128)(2,1)} %slice_dynamic-update-slice_fusion.56, bf16[4,2,2304,256]{3,2,1,0:T(8,128)(2,1)} %all-gather.5.cloned.1.call-done), kind=kOutput, calls=%fused_computation.9 | convolution fusion | flops 852075520 | bytes 5751808 | tf_op jit(solution)/shard_map/dot_general | solution.py:20
  178.8 0.2 copy-done.4
  179.0 1.3 maximum_convert_fusion.2
  180.7 0.2 slice_dynamic-update-slice_fusion.44
  181.4 1.3 fusion.2
  183.1 0.2 slice_dynamic-update-slice_fusion.36
  183.9 1.3 maximum_convert_fusion.1
  185.5 0.2 slice_dynamic-update-slice_fusion.28
  186.3 1.5 fusion.3
  188.9 1.3 maximum_convert_fusion
  191.3 1.3 fusion.4
  193.7 1.3 fusion.21
  195.1 0.4 copy.33
  195.5 0.7 fusion.7
  196.3 0.2 select_reduce_fusion
  196.6 0.6 reshape.189
  197.2 0.7 fusion.6
  (100 shorter events, 8.4 us)
Async XLA Ops:
  7.2 75.7 %copy-start = (bf16[36,256]{1,0:T(8,128)(2,1)S(1)}, bf16[36,256]{1,0:T(8,128)(2,1)}, u32[]{:S(2)}) copy-start(bf16[36,256]{1,0:T(8,128)(2,1)} %param.14) | copy-start | bytes 55300
  7.2 74.2 %copy-start.2 = (s32[2,1,361]{2,1,0:T(1,128)S(1)}, s32[2,1,361]{2,1,0:T(1,128)}, u32[]{:S(2)}) copy-start(s32[2,1,361]{2,1,0:T(1,128)} %param.9) | copy-start | bytes 8668
  7.2 74.3 %copy-start.1 = (s32[2,1,361]{2,1,0:T(1,128)S(1)}, s32[2,1,361]{2,1,0:T(1,128)}, u32[]{:S(2)}) copy-start(s32[2,1,361]{2,1,0:T(1,128)} %param.11) | copy-start | bytes 8668
  7.2 74.4 %copy-start.7 = (s32[2,1]{0,1:T(1,128)S(1)}, s32[2,1]{0,1:T(1,128)}, u32[]{:S(2)}) copy-start(s32[2,1]{0,1:T(1,128)} %param.10) | copy-start | bytes 28
  7.2 44.0 %reduce-scatter.4.cloned.1.call-start = ((), (), s32[]{:S(2)}) async-start(), calls=%async_computation.3 | async-start | bytes 2949120
  7.9 73.4 %all-gather.3.cloned.1.call-start = ((), (), s32[]{:S(2)}) async-start(), calls=%async_computation.1 | async-start | bytes 1474560 | tf_op jit(solution)/shard_map/all_gather | solution.py:65
  53.5 120.3 %all-gather.5.cloned.1.call-start = ((), (), s32[]{:S(2)}) async-start(), calls=%async_computation.2 | async-start | bytes 10616832 | tf_op jit(solution)/shard_map/all_gather | solution.py:66
  173.7 5.3 %copy-start.4 = (bf16[4,2,2304,256]{3,2,1,0:T(8,128)(2,1)S(1)}, bf16[4,2,2304,256]{3,2,1,0:T(8,128)(2,1)}, u32[]{:S(2)}) copy-start(bf16[4,2,2304,256]{3,2,1,0:T(8,128)(2,1)} %all-gather.5.cloned.1.call-done) | copy-start | bytes 28311556
  193.7 1.8 copy-start.3
  193.7 2.5 %copy-start.5 = (f32[256]{0:T(256)S(1)}, f32[256]{0:T(256)}, u32[]{:S(2)}) copy-start(f32[256]{0:T(256)} %param.16) | copy-start | bytes 3076
  193.7 3.5 %copy-start.6 = (f32[256]{0:T(256)S(1)}, f32[256]{0:T(256)}, u32[]{:S(2)}) copy-start(f32[256]{0:T(256)} %param.17) | copy-start | bytes 3076
Sparse Core Ops, SparseCore 0:
  11.1 40.0 reduce-scatter.3
  53.6 27.7 all-gather.2
  83.0 90.7 all-gather.4
where the time goes:
time: 205 us; the launch traced here: 204 us
  waiting for transfers between devices  154 us (75%)
  local copies, waits for them, and re-layouts  18 us (9%)
  matrix products  15.3 us (7%)
  between operations  14.3 us (7%)
  other arithmetic  2.86 us (1%)
    all_gather x1, waiting for transfers between devices, per_device(): complete = lax.all_gather(stacked, 'act', axis=2, tiled=True)  82.1 us
    unnamed x4, waiting for transfers between devices  43.9 us
    all_gather x1, waiting for transfers between devices, per_device(): stacked = lax.all_gather(sending, 'learn', axis=0, tiled=True)  27.8 us
    unnamed x88, local copies, waits for them, and re-layouts  14.8 us
    dot_general x9, matrix products, convolve(): result = jnp.dot(unrolled, kernel, preferred_element_type=jnp.float32)  13.7 us
  transfers between devices with their start and end apart: 3, of which 3 were waited for; matrix products, arithmetic and copies ran while one was open for 5% of the time, Pallas kernels for 0%

commit v1 on v0

v1 whole, which is shorter than its diff:
```python
import functools

import jax
import jax.numpy as jnp
from jax import lax
from jax.experimental import pallas as pl
from jax.experimental.pallas import tpu as pltpu
from jax.sharding import PartitionSpec as P

BOARD = 19
CELLS = 361
PLANES = 4
PITCH = BOARD + 1
AXES = ("learn", "act")


def pairs(learners, actors, target):
    out = []
    for learner in range(learners):
        for actor in range(actors):
            to_learner, to_actor = target(learner, actor)
            out.append((learner * actors + actor, to_learner * actors + to_actor))
    return out


def route_mask(core, subset, bits):
    mask = 0
    for step in range(bits):
        if subset >> step & 1:
            mask |= 1 << (step if core == 0 else bits - 1 - step)
    return mask


def plane_route(learners, actors, step):
    low, high = 1 << step, learners >> (step + 1)
    return pairs(learners, actors, lambda l, a: (l ^ (low if a % 2 == 0 else high), a))


def reduce_gradients(gradients, learners, actors):
    bits = learners.bit_length() - 1
    me, core = lax.axis_index("learn"), lax.axis_index("act") % 2
    held = {}
    for subset in range(learners):
        layer = me ^ jnp.where(core == 0, route_mask(0, subset, bits), route_mask(1, subset, bits))
        held[subset] = lax.dynamic_index_in_dim(gradients, layer, 0, keepdims=False)
    for step in range(bits):
        route = plane_route(learners, actors, step)
        for subset in sorted(held, reverse=True):
            if subset >> step & 1:
                kept = subset ^ 1 << step
                held[kept] = held[kept] + lax.ppermute(held.pop(subset), AXES, route)
    return held[0]


def gather_blocks(own, learners, actors):
    bits = learners.bit_length() - 1
    chips = actors // 2

    def along_z(block, away):
        return lax.ppermute(block, AXES, pairs(learners, actors, lambda l, a: (l, a ^ (2 * away))))

    def along_plane(block, step):
        return lax.ppermute(block, AXES, plane_route(learners, actors, step))

    def swapped(block):
        return lax.ppermute(block, AXES, pairs(learners, actors, lambda l, a: (l, a ^ 1)))

    def label(away, subset):
        masks = (route_mask(0, subset, bits), route_mask(1, subset, bits))
        return masks, 2 * away

    def other_label(away, subset):
        masks, actor_mask = label(away, subset)
        return masks[::-1], actor_mask + 1

    found = []
    starts = {0: own}
    for away in range(1, chips):
        starts[away] = along_z(starts[away - 1], 1) if away % 2 and away > 1 else along_z(own, away)
    for away in range(chips):
        held = {0: starts[away]}
        for step in range(bits):
            for subset in sorted(held):
                held[subset | 1 << step] = along_plane(held[subset], step)
        groups = [sorted(held)] if away < chips - 1 else [sorted(held)[:-1], [learners - 1]]
        for group in groups:
            joined = jnp.concatenate([held[subset] for subset in group], axis=0) if len(group) > 1 else held[group[0]]
            found.append((swapped(joined), [other_label(away, subset) for subset in group]))
        found.extend((held[subset], [label(away, subset)]) for subset in sorted(held))
    return found


def place_of(masks, actor_mask):
    actor = lax.axis_index("act")
    mask = jnp.where(actor % 2 == 0, masks[0], masks[1])
    return lax.axis_index("learn") ^ mask, actor ^ actor_mask


def tower(places, layers, rows, number, width, cuts, *refs):
    blocks = refs[: len(places)]
    stem, legal, policy, passing, valuing, logp, extra = refs[len(places) : len(places) + 7]
    weights, field, stream, mask, arrived = refs[len(places) + 7 :]
    points = BOARD * width
    for labels, block in zip(places, blocks):
        if labels is None:
            for layer in range(layers):
                pltpu.make_async_copy(block.at[layer], weights.at[layer], arrived.at[layer]).start()
            continue
        for entry, label in enumerate(labels):
            layer, actor = place_of(*label)
            spot = pl.ds(pl.multiple_of(actor * rows, rows), rows)
            pltpu.make_async_copy(
                block.at[2 * entry : 2 * entry + 2], weights.at[layer, :, spot, :], arrived.at[layer]
            ).start()
    for half in range(2):
        field[half, :width, :] = jnp.zeros((width, field.shape[2]), jnp.bfloat16)
        field[half, width + points :, :] = jnp.zeros((width, field.shape[2]), jnp.bfloat16)
    column = lax.rem(lax.broadcasted_iota(jnp.int32, mask.shape, 0), width)
    on_board = (lax.rem(column, PITCH) < BOARD) & (column < PITCH * number)
    mask[...] = jnp.where(on_board, 1.0, 0.0)

    def rectified(low, high, values):
        keep = mask[low:high, :]
        keep = jnp.concatenate([keep] * (values.shape[1] // keep.shape[1]), axis=1)
        return jnp.maximum(values, 0.0) * keep

    def spread(half, low, high, values):
        values = rectified(low, high, values)
        depth = values.shape[1]
        spot = slice(width + low, width + high)
        field[half, spot, depth : 2 * depth] = values.astype(jnp.bfloat16)
        field[half, spot, :depth] = pltpu.roll(values, 1, 0).astype(jnp.bfloat16)
        field[half, spot, 2 * depth :] = pltpu.roll(values, high - low - 1, 0).astype(jnp.bfloat16)

    def convolve(half, layer, which, low, high):
        lines = [field[half, low + row * width : high + row * width, :] for row in range(3)]
        return jnp.dot(
            jnp.concatenate(lines, axis=1), weights[layer, which], preferred_element_type=jnp.float32
        )

    for low, high in cuts:
        values = stem[low:high, :]
        stream[low:high, :] = values
        spread(0, low, high, values)
    for layer in range(layers):
        pltpu.make_async_copy(weights.at[layer], weights.at[layer], arrived.at[layer]).wait()
        for low, high in cuts:
            spread(1, low, high, convolve(0, layer, 0, low, high))
        for low, high in cuts:
            values = stream[low:high, :] + convolve(1, layer, 1, low, high)
            if layer == layers - 1:
                stream[low:high, :] = rectified(low, high, values)
            else:
                stream[low:high, :] = values
                spread(0, low, high, values)

    trunk = stream[...]
    column = lax.rem(lax.broadcasted_iota(jnp.int32, (8, points), 1), width)
    owner = lax.broadcasted_iota(jnp.int32, (8, points), 0)
    inside = (column >= owner * PITCH) & (column < owner * PITCH + BOARD) & (owner < number)
    exact = functools.partial(
        lax.dot_general, precision=lax.Precision.HIGHEST, preferred_element_type=jnp.float32
    )
    per_point = jnp.broadcast_to(policy[...], (8, policy.shape[1]))
    raw = exact(per_point, trunk, (((1,), (1,)), ((), ())))
    pooled = exact(jnp.where(inside, 1.0, 0.0), trunk, (((1,), (0,)), ((), ()))) / CELLS
    pass_raw = jnp.sum(pooled * passing[...], axis=1, keepdims=True)
    value = jnp.tanh(jnp.sum(pooled * valuing[...], axis=1, keepdims=True))
    logits = 10.0 * jnp.tanh(raw / 10.0)
    pass_logit = 10.0 * jnp.tanh(pass_raw / 10.0)
    allowed = inside & (legal[...] > 0)
    shares = jnp.sum(jnp.where(allowed, jnp.exp(logits), 0.0), axis=1, keepdims=True)
    scale = jnp.log(shares + jnp.exp(pass_logit))
    logp[...] = jnp.where(allowed, logits - scale, 0.0)
    lane = lax.broadcasted_iota(jnp.int32, extra.shape, 1)
    extra[...] = jnp.where(lane == 0, pass_logit - scale, value)


def run_tower(found, layers, rows, depth, stem, legal, policy, passing, valuing, number, width):
    points = BOARD * width
    channels = stem.shape[1]
    places = [labels for _, labels in found]
    steps = [0, 7, 13, BOARD]
    cuts = [(low * width, high * width) for low, high in zip(steps, steps[1:])]
    anywhere = pl.BlockSpec(memory_space=pl.ANY)
    inside = pl.BlockSpec(memory_space=pltpu.VMEM)
    return pl.pallas_call(
        functools.partial(tower, places, layers, rows, number, width, cuts),
        out_shape=(
            jax.ShapeDtypeStruct((8, points), jnp.float32),
            jax.ShapeDtypeStruct((8, 128), jnp.float32),
        ),
        in_specs=[anywhere] * len(found) + [inside] * 5,
        out_specs=(inside, inside),
        scratch_shapes=[
            pltpu.VMEM((layers, 2, depth, channels), jnp.bfloat16),
            pltpu.VMEM((2, points + 2 * width, 3 * channels), jnp.bfloat16),
            pltpu.VMEM((points, channels), jnp.float32),
            pltpu.VMEM((points, 128), jnp.float32),
            pltpu.SemaphoreType.DMA((layers,)),
        ],
        compiler_params=pltpu.CompilerParams(vmem_limit_bytes=36 * 2**20),
        name="tower",
    )(*[block for block, _ in found], stem, legal, policy, passing, valuing)


def padded_boards(rows, width):
    number = rows.shape[0]
    boards = jnp.pad(rows.reshape(number, BOARD, BOARD), ((0, 0), (0, 0), (0, PITCH - BOARD)))
    side_by_side = jnp.swapaxes(boards, 0, 1).reshape(BOARD, number * PITCH)
    return jnp.pad(side_by_side, ((0, 0), (0, width - number * PITCH)))


def stem_stream(boards, sides, stem_weight, width):
    side_move = sides[:, None]
    planes = [boards == 1 + side_move, boards == 2 - side_move, boards == 0, jnp.ones_like(boards)]
    planes = [padded_boards(plane.astype(jnp.bfloat16), width) for plane in planes]
    field = jnp.stack(planes, axis=-1)[None]
    kernel = stem_weight.reshape(3, 3, PLANES, -1)
    out = lax.conv_general_dilated(
        field,
        kernel,
        (1, 1),
        ((1, 1), (1, 1)),
        dimension_numbers=("NHWC", "HWIO", "NHWC"),
        preferred_element_type=jnp.float32,
    )
    return out.reshape(BOARD * width, kernel.shape[-1])


def per_device(
    positions,
    to_move,
    legal_moves,
    master,
    gradients,
    stem_weight,
    policy_weight,
    pass_weight,
    value_weight,
):
    learners, actors = lax.axis_size("learn"), lax.axis_size("act")
    steps_here, local_count = positions.shape[:2]
    number = steps_here * local_count
    width = -(-number * PITCH // 8) * 8
    rows, channels = master.shape[2:]
    depth = rows * actors

    boards = positions.reshape(number, CELLS)
    stem = stem_stream(boards, to_move.reshape(number), stem_weight, width)
    legal = padded_boards(legal_moves.reshape(number, CELLS), width).reshape(1, BOARD * width)

    total = reduce_gradients(gradients[0], learners, actors)
    total, stem, legal = lax.optimization_barrier((total, stem, legal))
    updated = master[0] - total / learners
    found = gather_blocks(updated.astype(jnp.bfloat16), learners, actors)
    if rows % 16:
        whole = jnp.zeros((learners, 2, depth, channels), jnp.bfloat16)
        for block, labels in found:
            for entry, label in enumerate(labels):
                layer, actor = place_of(*label)
                piece = block[2 * entry : 2 * entry + 2]
                whole = lax.dynamic_update_slice(whole, piece[None], (layer, 0, actor * rows, 0))
        found = [(whole, None)]
    logp, extra = run_tower(
        found,
        learners,
        rows,
        depth,
        stem,
        legal,
        policy_weight[None],
        pass_weight[None],
        value_weight[None],
        number,
        width,
    )
    boards_out = logp[:number].reshape(number, BOARD, width)
    moves = [
        boards_out[board, :, board * PITCH : board * PITCH + BOARD].reshape(1, CELLS)
        for board in range(number)
    ]
    moves = jnp.concatenate([jnp.concatenate(moves, axis=0), extra[:number, :1]], axis=1)
    return (
        updated[None],
        moves.reshape(steps_here, local_count, CELLS + 1),
        extra[:number, 1].reshape(steps_here, local_count),
    )


def solution(mesh):
    in_specs = (
        P(None, ("learn", "act"), None),
        P(None, ("learn", "act")),
        P(None, ("learn", "act"), None),
        P("learn", None, "act", None),
        P("learn", None, None, "act", None),
        P(),
        P(),
        P(),
        P(),
    )
    out_specs = (
        P("learn", None, "act", None),
        P(None, ("learn", "act"), None),
        P(None, ("learn", "act")),
    )
    return jax.shard_map(
        per_device, mesh=mesh, in_specs=in_specs, out_specs=out_specs, check_vma=False
    )
```

time: 205 us -> 97.3 us (0.47)
  waiting for transfers between devices: 154 us -> 35.7 us
  starting transfers between devices: 0.12 us -> 33.4 us
  between operations: 14.3 us -> 1 us
  Pallas kernels: 0 us -> 12.2 us
  local copies, waits for them, and re-layouts: 18 us -> 6.13 us
  matrix products: 15.3 us -> 3.73 us
  other arithmetic: 2.86 us -> 5 us
    all_gather x2 -> x0, waiting for transfers between devices: 110 us -> none  [the longest x1 82.1 us: per_device(): complete = lax.all_gather(stacked, 'act', axis=2, tiled=True)]
    unnamed x4 -> x0, waiting for transfers between devices: 43.9 us -> none
    ppermute x0 -> x23, waiting for transfers between devices: none -> 35.7 us  [the longest x12 16.6 us: along_plane(): return lax.ppermute(block, AXES, plane_route(learners, actors, step))]
    ppermute x0 -> x23, starting transfers between devices: none -> 33.4 us  [the longest x12 21.2 us: along_plane(): return lax.ppermute(block, AXES, plane_route(learners, actors, step))]
    dot_general x12 -> x0, matrix products: 15.3 us -> none  [the longest x9 13.7 us: convolve(): result = jnp.dot(unrolled, kernel, preferred_element_type=jnp.float32)]
    unnamed x88 -> x21, local copies, waits for them, and re-layouts: 14.8 us -> 1.9 us
    pallas_call x0 -> x1, Pallas kernels: none -> 12.2 us  [run_tower(): pl.pallas_call(functools.partial(tower, places, layers, rows, number, wid...]
    conv_general_dilated x0 -> x1, matrix products: none -> 3.73 us  [stem_stream(): lax.conv_general_dilated(field, kernel, (1, 1), ((1, 1), (1, 1)), dimensi...]
  transfers between devices with their start and end apart: 3 -> 23, of which waited for: 3 -> 11; matrix products, arithmetic and copies ran while one was open for 5% -> 8% of each run, Pallas kernels for 0% -> 0%
where the time goes in v1:
time: 97.3 us; the launch traced here: 97.1 us
  waiting for transfers between devices  35.7 us (37%)
  starting transfers between devices  33.4 us (34%)
  Pallas kernels  12.2 us (13%)
  local copies, waits for them, and re-layouts  6.13 us (6%)
  other arithmetic  5 us (5%)
  matrix products  3.73 us (4%)
  between operations  1 us (1%)
    ppermute x12, starting transfers between devices, along_plane(): return lax.ppermute(block, AXES, plane_route(learners, actors, step))  21.2 us
    ppermute x12, waiting for transfers between devices, along_plane(): return lax.ppermute(block, AXES, plane_route(learners, actors, step))  16.6 us
    pallas_call x1, Pallas kernels, run_tower(): pl.pallas_call(functools.partial(tower, places, layers, rows, number, wid...  12.2 us
    ppermute x3, waiting for transfers between devices, reduce_gradients(): held[kept] = held[kept] + lax.ppermute(held.pop(subset), AXES, route)  9.89 us
    ppermute x3, waiting for transfers between devices, along_z(): lax.ppermute(block, AXES, pairs(learners, actors, lambda l, a: (l, a ^ 2...  7.64 us
    ppermute x3, starting transfers between devices, reduce_gradients(): held[kept] = held[kept] + lax.ppermute(held.pop(subset), AXES, route)  5.02 us
    ppermute x3, starting transfers between devices, along_z(): lax.ppermute(block, AXES, pairs(learners, actors, lambda l, a: (l, a ^ 2...  4.89 us
    conv_general_dilated x1, matrix products, stem_stream(): lax.conv_general_dilated(field, kernel, (1, 1), ((1, 1), (1, 1)), dimensi...  3.73 us
  transfers between devices with their start and end apart: 23, of which 11 were waited for; matrix products, arithmetic and copies ran while one was open for 8% of the time, Pallas kernels for 0%

profile of v1, /device:TPU:0, one launch (start us, length us, event | category | flops | bytes accessed | tf_op | source)
XLA Modules:
  0.0 97.1 jit_solution(12234244427259996024)
XLA Ops:
  0.7 2.3 %dynamic-slice_bitcast_fusion.1 = (f32[2,288,256]{2,1,0:T(8,128)}, f32[2,288,256]{2,1,0:T(8,128)S(1)}) fusion(f32[1,4,2,288,256]{4,3,2,1,0:T(8,128)} %param.13, s32[]{:T(128)S(6)} %select_n.32, s32[]{:T(128)S(6)} %select_n.35), kind=kLoop, calls=%fused_computation.9 | loop fusion | bytes 2359304 | tf_op jit(solution)/shard_map/jit(dynamic_index_in_dim)/squeeze | solution.py:45
  3.0 2.9 %collective-permute-start.1 = (f32[2,288,256]{2,1,0:T(8,128)S(1)}, f32[2,288,256]{2,1,0:T(8,128)}, u32[]{:S(2)}, u32[]{:S(2)}) collective-permute-start(f32[2,288,256]{2,1,0:T(8,128)S(1)} %get-tuple-element.20), channel_id=1, source_target_pairs={{0,8},{1,17},{2,10},{3,19},{4,12},{5,21},{6,14},{7,23},{8,0},{9,25... | collective-permute-start | bytes 1769480 | tf_op jit(solution)/shard_map/ppermute | solution.py:51
  6.4 7.5 %collective-permute-done.1 = f32[2,288,256]{2,1,0:T(8,128)} collective-permute-done((f32[2,288,256]{2,1,0:T(8,128)S(1)}, f32[2,288,256]{2,1,0:T(8,128)}, u32[]{:S(2)}, u32[]{:S(2)}) %collective-permute-start.1) | collective-permute-done | bytes 589856 | tf_op jit(solution)/shard_map/ppermute | solution.py:51
  13.9 2.0 %bitcast_add_fusion = f32[2,288,256]{2,1,0:T(8,128)} fusion(f32[2,288,256]{2,1,0:T(8,128)} %collective-permute-done.1, f32[1,4,2,288,256]{4,3,2,1,0:T(8,128)S(1)} %copy-done.3, s32[]{:T(128)S(6)} %select_n.34), kind=kLoop, calls=%fused_computation.4 | loop fusion | flops 147456 | bytes 1769476 | tf_op jit(solution)/shard_map/add | solution.py:51
  15.9 2.1 %collective-permute-start.2 = (f32[2,288,256]{2,1,0:T(8,128)}, f32[2,288,256]{2,1,0:T(8,128)}, u32[]{:S(2)}, u32[]{:S(2)}) collective-permute-start(f32[2,288,256]{2,1,0:T(8,128)} %bitcast_add_fusion), channel_id=1, source_target_pairs={{0,16},{1,9},{2,18},{3,11},{4,20},{5,13},{6,22},{7,15},{8,24},{9,1... | collective-permute-start | bytes 1769480 | tf_op jit(solution)/shard_map/ppermute | solution.py:51
  19.0 3.7 %fusion.8 = f32[1,19,40,256]{3,0,2,1:T(1,128)S(1)} fusion(bf16[1,19,40,4]{3,0,2,1:T(2,128)(2,1)S(1)} %copy.21, bf16[3,3,4,256]{3,2,1,0:T(4,128)(2,1)S(1)} %reshape.64), kind=kOutput, calls=%fused_computation.28 | convolution fusion | flops 13291520 | bytes 802752 | tf_op jit(solution)/shard_map/conv_general_dilated | solution.py:220
  23.7 2.4 %collective-permute-done.2 = f32[2,288,256]{2,1,0:T(8,128)} collective-permute-done((f32[2,288,256]{2,1,0:T(8,128)}, f32[2,288,256]{2,1,0:T(8,128)}, u32[]{:S(2)}, u32[]{:S(2)}) %collective-permute-start.2) | collective-permute-done | bytes 589856 | tf_op jit(solution)/shard_map/ppermute | solution.py:51
  26.1 1.4 %fusion = f32[2,288,256]{2,1,0:T(8,128)S(1)} fusion(f32[2,288,256]{2,1,0:T(8,128)} %collective-permute-done.2, f32[2,288,256]{2,1,0:T(8,128)} %collective-permute-done, f32[1,4,2,288,256]{4,3,2,1,0:T(8,128)S(1)} %copy-done.3, s32[]{:T(128)S(6)} %select_n.29), kind=kLoop, calls=%fused_computation.6 | loop fusion | flops 294912 | bytes 2359300 | tf_op jit(solution)/shard_map/add | solution.py:51
  27.5 0.9 fusion.1
  28.4 2.1 %collective-permute-start.7 = (bf16[2,288,256]{2,1,0:T(8,128)(2,1)S(1)}, bf16[2,288,256]{2,1,0:T(8,128)(2,1)S(1)}, u32[]{:S(2)}, u32[]{:S(2)}) collective-permute-start(bf16[2,288,256]{2,1,0:T(8,128)(2,1)S(1)} %get-tuple-element.21.refs_1_), channel_id=1, source_target_pairs={{0,2},{1,3},{2,0},{3,1},{4,6},{5,7},{6,4},{7,5},{8,10},{9,11},{10,... | collective-permute-start | bytes 884744 | tf_op jit(solution)/shard_map/ppermute | solution.py:60
  30.5 1.5 %collective-permute-start.3 = (bf16[2,288,256]{2,1,0:T(8,128)(2,1)S(1)}, bf16[2,288,256]{2,1,0:T(8,128)(2,1)S(1)}, u32[]{:S(2)}, u32[]{:S(2)}) collective-permute-start(bf16[2,288,256]{2,1,0:T(8,128)(2,1)S(1)} %get-tuple-element.21.refs_1_), channel_id=1, source_target_pairs={{0,8},{1,17},{2,10},{3,19},{4,12},{5,21},{6,14},{7,23},{8,0},{9,25... | collective-permute-start | bytes 884744 | tf_op jit(solution)/shard_map/ppermute | solution.py:63
  32.0 2.6 %collective-permute-start.12 = (bf16[2,288,256]{2,1,0:T(8,128)(2,1)S(1)}, bf16[2,288,256]{2,1,0:T(8,128)(2,1)S(1)}, u32[]{:S(2)}, u32[]{:S(2)}) collective-permute-start(bf16[2,288,256]{2,1,0:T(8,128)(2,1)S(1)} %get-tuple-element.21.refs_1_), channel_id=1, source_target_pairs={{0,4},{1,5},{2,6},{3,7},{4,0},{5,1},{6,2},{7,3},{8,12},{9,13},{10,... | collective-permute-start | bytes 884744 | tf_op jit(solution)/shard_map/ppermute | solution.py:60
  34.5 1.5 %collective-permute-start.4 = (bf16[2,288,256]{2,1,0:T(8,128)(2,1)S(1)}, bf16[2,288,256]{2,1,0:T(8,128)(2,1)S(1)}, u32[]{:S(2)}, u32[]{:S(2)}) collective-permute-start(bf16[2,288,256]{2,1,0:T(8,128)(2,1)S(1)} %get-tuple-element.21.refs_1_), channel_id=1, source_target_pairs={{0,16},{1,9},{2,18},{3,11},{4,20},{5,13},{6,22},{7,15},{8,24},{9,1... | collective-permute-start | bytes 884744 | tf_op jit(solution)/shard_map/ppermute | solution.py:63
  36.1 6.8 %collective-permute-done.7.refs_6_ = bf16[2,288,256]{2,1,0:T(8,128)(2,1)S(1)} collective-permute-done((bf16[2,288,256]{2,1,0:T(8,128)(2,1)S(1)}, bf16[2,288,256]{2,1,0:T(8,128)(2,1)S(1)}, u32[]{:S(2)}, u32[]{:S(2)}) %collective-permute-start.7) | collective-permute-done | bytes 294944 | tf_op jit(solution)/shard_map/ppermute | solution.py:60
  42.9 1.7 %collective-permute-start.8 = (bf16[2,288,256]{2,1,0:T(8,128)(2,1)S(1)}, bf16[2,288,256]{2,1,0:T(8,128)(2,1)S(1)}, u32[]{:S(2)}, u32[]{:S(2)}) collective-permute-start(bf16[2,288,256]{2,1,0:T(8,128)(2,1)S(1)} %collective-permute-done.7.refs_6_), channel_id=1, source_target_pairs={{0,8},{1,17},{2,10},{3,19},{4,12},{5,21},{6,14},{7,23},{8,0},{9,25... | collective-permute-start | bytes 884744 | tf_op jit(solution)/shard_map/ppermute | solution.py:63
  44.6 2.5 %collective-permute-start.5 = (bf16[2,288,256]{2,1,0:T(8,128)(2,1)S(1)}, bf16[2,288,256]{2,1,0:T(8,128)(2,1)S(1)}, u32[]{:S(2)}, u32[]{:S(2)}) collective-permute-start(bf16[2,288,256]{2,1,0:T(8,128)(2,1)S(1)} %collective-permute-done.3.refs_2_), channel_id=1, source_target_pairs={{0,16},{1,9},{2,18},{3,11},{4,20},{5,13},{6,22},{7,15},{8,24},{9,1... | collective-permute-start | bytes 884744 | tf_op jit(solution)/shard_map/ppermute | solution.py:63
  47.1 0.8 collective-permute-done.12.refs_11_
  47.9 1.5 %collective-permute-start.13 = (bf16[2,288,256]{2,1,0:T(8,128)(2,1)S(1)}, bf16[2,288,256]{2,1,0:T(8,128)(2,1)S(1)}, u32[]{:S(2)}, u32[]{:S(2)}) collective-permute-start(bf16[2,288,256]{2,1,0:T(8,128)(2,1)S(1)} %collective-permute-done.12.refs_11_), channel_id=1, source_target_pairs={{0,8},{1,17},{2,10},{3,19},{4,12},{5,21},{6,14},{7,23},{8,0},{9,25... | collective-permute-start | bytes 884744 | tf_op jit(solution)/shard_map/ppermute | solution.py:63
  50.1 1.7 %collective-permute-done.8.refs_7_ = bf16[2,288,256]{2,1,0:T(8,128)(2,1)S(1)} collective-permute-done((bf16[2,288,256]{2,1,0:T(8,128)(2,1)S(1)}, bf16[2,288,256]{2,1,0:T(8,128)(2,1)S(1)}, u32[]{:S(2)}, u32[]{:S(2)}) %collective-permute-start.8) | collective-permute-done | bytes 294944 | tf_op jit(solution)/shard_map/ppermute | solution.py:63
  51.8 3.7 %collective-permute-start.10 = (bf16[2,288,256]{2,1,0:T(8,128)(2,1)S(1)}, bf16[2,288,256]{2,1,0:T(8,128)(2,1)S(1)}, u32[]{:S(2)}, u32[]{:S(2)}) collective-permute-start(bf16[2,288,256]{2,1,0:T(8,128)(2,1)S(1)} %collective-permute-done.8.refs_7_), channel_id=1, source_target_pairs={{0,16},{1,9},{2,18},{3,11},{4,20},{5,13},{6,22},{7,15},{8,24},{9,1... | collective-permute-start | bytes 884744 | tf_op jit(solution)/shard_map/ppermute | solution.py:63
  55.5 1.5 %collective-permute-start.14 = (bf16[2,288,256]{2,1,0:T(8,128)(2,1)S(1)}, bf16[2,288,256]{2,1,0:T(8,128)(2,1)S(1)}, u32[]{:S(2)}, u32[]{:S(2)}) collective-permute-start(bf16[2,288,256]{2,1,0:T(8,128)(2,1)S(1)} %collective-permute-done.12.refs_11_), channel_id=1, source_target_pairs={{0,16},{1,9},{2,18},{3,11},{4,20},{5,13},{6,22},{7,15},{8,24},{9,1... | collective-permute-start | bytes 884744 | tf_op jit(solution)/shard_map/ppermute | solution.py:63
  57.0 1.1 %collective-permute-done.13.refs_12_ = bf16[2,288,256]{2,1,0:T(8,128)(2,1)S(1)} collective-permute-done((bf16[2,288,256]{2,1,0:T(8,128)(2,1)S(1)}, bf16[2,288,256]{2,1,0:T(8,128)(2,1)S(1)}, u32[]{:S(2)}, u32[]{:S(2)}) %collective-permute-start.13) | collective-permute-done | bytes 294944 | tf_op jit(solution)/shard_map/ppermute | solution.py:63
  58.2 3.7 %collective-permute-start.15 = (bf16[2,288,256]{2,1,0:T(8,128)(2,1)S(1)}, bf16[2,288,256]{2,1,0:T(8,128)(2,1)S(1)}, u32[]{:S(2)}, u32[]{:S(2)}) collective-permute-start(bf16[2,288,256]{2,1,0:T(8,128)(2,1)S(1)} %collective-permute-done.13.refs_12_), channel_id=1, source_target_pairs={{0,16},{1,9},{2,18},{3,11},{4,20},{5,13},{6,22},{7,15},{8,24},{9,1... | collective-permute-start | bytes 884744 | tf_op jit(solution)/shard_map/ppermute | solution.py:63
  62.2 1.6 %collective-permute-start.18 = (bf16[2,288,256]{2,1,0:T(8,128)(2,1)S(1)}, bf16[2,288,256]{2,1,0:T(8,128)(2,1)S(1)}, u32[]{:S(2)}, u32[]{:S(2)}) collective-permute-start(bf16[2,288,256]{2,1,0:T(8,128)(2,1)S(1)} %collective-permute-done.17.refs_17_), channel_id=1, source_target_pairs={{0,8},{1,17},{2,10},{3,19},{4,12},{5,21},{6,14},{7,23},{8,0},{9,25... | collective-permute-start | bytes 884744 | tf_op jit(solution)/shard_map/ppermute | solution.py:63
  63.9 1.0 %collective-permute-done.14.refs_13_ = bf16[2,288,256]{2,1,0:T(8,128)(2,1)S(1)} collective-permute-done((bf16[2,288,256]{2,1,0:T(8,128)(2,1)S(1)}, bf16[2,288,256]{2,1,0:T(8,128)(2,1)S(1)}, u32[]{:S(2)}, u32[]{:S(2)}) %collective-permute-start.14) | collective-permute-done | bytes 294944 | tf_op jit(solution)/shard_map/ppermute | solution.py:63
  65.5 4.8 %collective-permute-done.15.refs_14_ = bf16[2,288,256]{2,1,0:T(8,128)(2,1)S(1)} collective-permute-done((bf16[2,288,256]{2,1,0:T(8,128)(2,1)S(1)}, bf16[2,288,256]{2,1,0:T(8,128)(2,1)S(1)}, u32[]{:S(2)}, u32[]{:S(2)}) %collective-permute-start.15) | collective-permute-done | bytes 294944 | tf_op jit(solution)/shard_map/ppermute | solution.py:63
  70.5 1.1 %collective-permute-start.16 = (bf16[8,288,256]{2,1,0:T(8,128)(2,1)S(1)}, bf16[8,288,256]{2,1,0:T(8,128)(2,1)S(1)}, u32[]{:S(2)}, u32[]{:S(2)}) collective-permute-start(bf16[8,288,256]{2,1,0:T(8,128)(2,1)S(1)} %pad_maximum_fusion.2), channel_id=1, source_target_pairs={{0,1},{1,0},{2,3},{3,2},{4,5},{5,4},{6,7},{7,6},{8,9},{9,8},{10,11... | collective-permute-start | bytes 3538952 | tf_op jit(solution)/shard_map/ppermute | solution.py:66
  71.6 2.8 %collective-permute-done.19.refs_19_ = bf16[2,288,256]{2,1,0:T(8,128)(2,1)S(1)} collective-permute-done((bf16[2,288,256]{2,1,0:T(8,128)(2,1)S(1)}, bf16[2,288,256]{2,1,0:T(8,128)(2,1)S(1)}, u32[]{:S(2)}, u32[]{:S(2)}) %collective-permute-start.19) | collective-permute-done | bytes 294944 | tf_op jit(solution)/shard_map/ppermute | solution.py:63
  74.9 1.5 %collective-permute-start.21 = (bf16[2,288,256]{2,1,0:T(8,128)(2,1)S(1)}, bf16[2,288,256]{2,1,0:T(8,128)(2,1)S(1)}, u32[]{:S(2)}, u32[]{:S(2)}) collective-permute-start(bf16[2,288,256]{2,1,0:T(8,128)(2,1)S(1)} %collective-permute-done.18.refs_18_), channel_id=1, source_target_pairs={{0,16},{1,9},{2,18},{3,11},{4,20},{5,13},{6,22},{7,15},{8,24},{9,1... | collective-permute-start | bytes 884744 | tf_op jit(solution)/shard_map/ppermute | solution.py:63
  76.4 5.2 %collective-permute-done.21.refs_20_ = bf16[2,288,256]{2,1,0:T(8,128)(2,1)S(1)} collective-permute-done((bf16[2,288,256]{2,1,0:T(8,128)(2,1)S(1)}, bf16[2,288,256]{2,1,0:T(8,128)(2,1)S(1)}, u32[]{:S(2)}, u32[]{:S(2)}) %collective-permute-start.21) | collective-permute-done | bytes 294944 | tf_op jit(solution)/shard_map/ppermute | solution.py:63
  81.6 1.6 %collective-permute-done.22.refs_16_ = bf16[2,288,256]{2,1,0:T(8,128)(2,1)S(1)} collective-permute-done((bf16[2,288,256]{2,1,0:T(8,128)(2,1)S(1)}, bf16[2,288,256]{2,1,0:T(8,128)(2,1)S(1)}, u32[]{:S(2)}, u32[]{:S(2)}) %collective-permute-start.22) | collective-permute-done | bytes 294944 | tf_op jit(solution)/shard_map/ppermute | solution.py:66
  83.2 12.2 %tower.1 = (f32[8,760]{1,0:T(8,128)S(1)}, f32[8,128]{1,0:T(8,128)S(1)}) custom-call(bf16[8,288,256]{2,1,0:T(8,128)(2,1)S(1)} %collective-permute-done.6.refs_0_, bf16[2,288,256]{2,1,0:T(8,128)(2,1)S(1)} %get-tuple-element.21.refs_1_, bf16[2,288,256]{2,1,0:T(8,128)(2,1)S(1)} %collective-permute-done.3.refs_2_, ...), custom_call_target="tpu_custom_call" | custom-call | tf_op jit(solution)/shard_map/tower/pallas_call | solution.py:187
  (77 shorter events, 6.6 us)
Async XLA Ops:
  0.7 5.4 %copy-start.6 = (s32[2,1,361]{2,1,0:T(1,128)S(1)}, s32[2,1,361]{2,1,0:T(1,128)}, u32[]{:S(2)}) copy-start(s32[2,1,361]{2,1,0:T(1,128)} %param.9) | copy-start | bytes 8668
  0.7 5.5 %copy-start.8 = (s32[2,1]{0,1:T(1,128)S(1)}, s32[2,1]{0,1:T(1,128)}, u32[]{:S(2)}) copy-start(s32[2,1]{0,1:T(1,128)} %param.10) | copy-start | bytes 28
  0.7 13.2 %copy-start.3 = (f32[1,4,2,288,256]{4,3,2,1,0:T(8,128)S(1)}, f32[1,4,2,288,256]{4,3,2,1,0:T(8,128)}, u32[]{:S(2)}) copy-start(f32[1,4,2,288,256]{4,3,2,1,0:T(8,128)} %param.13) | copy-start | bytes 7077892
  3.0 10.9 %collective-permute-start.1 = (f32[2,288,256]{2,1,0:T(8,128)S(1)}, f32[2,288,256]{2,1,0:T(8,128)}, u32[]{:S(2)}, u32[]{:S(2)}) collective-permute-start(f32[2,288,256]{2,1,0:T(8,128)S(1)} %get-tuple-element.20), channel_id=1, source_target_pairs={{0,8},{1,17},{2,10},{3,19},{4,12},{5,21},{6,14},{7,23},{8,0},{9,25... | collective-permute-start | bytes 1769480 | tf_op jit(solution)/shard_map/ppermute | solution.py:51
  5.9 17.7 %collective-permute-start = (f32[2,288,256]{2,1,0:T(8,128)}, f32[2,288,256]{2,1,0:T(8,128)}, u32[]{:S(2)}, u32[]{:S(2)}) collective-permute-start(f32[2,288,256]{2,1,0:T(8,128)} %get-tuple-element.19), channel_id=1, source_target_pairs={{0,8},{1,17},{2,10},{3,19},{4,12},{5,21},{6,14},{7,23},{8,0},{9,25... | collective-permute-start | bytes 1769480 | tf_op jit(solution)/shard_map/ppermute | solution.py:51
  6.4 12.5 %copy-start.5 = (bf16[36,256]{1,0:T(8,128)(2,1)S(1)}, bf16[36,256]{1,0:T(8,128)(2,1)}, u32[]{:S(2)}) copy-start(bf16[36,256]{1,0:T(8,128)(2,1)} %param.14) | copy-start | bytes 55300
  15.9 10.2 %collective-permute-start.2 = (f32[2,288,256]{2,1,0:T(8,128)}, f32[2,288,256]{2,1,0:T(8,128)}, u32[]{:S(2)}, u32[]{:S(2)}) collective-permute-start(f32[2,288,256]{2,1,0:T(8,128)} %bitcast_add_fusion), channel_id=1, source_target_pairs={{0,16},{1,9},{2,18},{3,11},{4,20},{5,13},{6,22},{7,15},{8,24},{9,1... | collective-permute-start | bytes 1769480 | tf_op jit(solution)/shard_map/ppermute | solution.py:51
  22.7 0.7 copy-start.7
  23.7 3.8 %copy-start.4 = (f32[1,2,288,256]{3,2,1,0:T(8,128)S(1)}, f32[1,2,288,256]{3,2,1,0:T(8,128)}, u32[]{:S(2)}) copy-start(f32[1,2,288,256]{3,2,1,0:T(8,128)} %param.12) | copy-start | bytes 1769476
  28.4 14.5 %collective-permute-start.7 = (bf16[2,288,256]{2,1,0:T(8,128)(2,1)S(1)}, bf16[2,288,256]{2,1,0:T(8,128)(2,1)S(1)}, u32[]{:S(2)}, u32[]{:S(2)}) collective-permute-start(bf16[2,288,256]{2,1,0:T(8,128)(2,1)S(1)} %get-tuple-element.21.refs_1_), channel_id=1, source_target_pairs={{0,2},{1,3},{2,0},{3,1},{4,6},{5,7},{6,4},{7,5},{8,10},{9,11},{10,... | collective-permute-start | bytes 884744 | tf_op jit(solution)/shard_map/ppermute | solution.py:60
  30.5 14.1 %collective-permute-start.3 = (bf16[2,288,256]{2,1,0:T(8,128)(2,1)S(1)}, bf16[2,288,256]{2,1,0:T(8,128)(2,1)S(1)}, u32[]{:S(2)}, u32[]{:S(2)}) collective-permute-start(bf16[2,288,256]{2,1,0:T(8,128)(2,1)S(1)} %get-tuple-element.21.refs_1_), channel_id=1, source_target_pairs={{0,8},{1,17},{2,10},{3,19},{4,12},{5,21},{6,14},{7,23},{8,0},{9,25... | collective-permute-start | bytes 884744 | tf_op jit(solution)/shard_map/ppermute | solution.py:63
  32.0 15.9 %collective-permute-start.12 = (bf16[2,288,256]{2,1,0:T(8,128)(2,1)S(1)}, bf16[2,288,256]{2,1,0:T(8,128)(2,1)S(1)}, u32[]{:S(2)}, u32[]{:S(2)}) collective-permute-start(bf16[2,288,256]{2,1,0:T(8,128)(2,1)S(1)} %get-tuple-element.21.refs_1_), channel_id=1, source_target_pairs={{0,4},{1,5},{2,6},{3,7},{4,0},{5,1},{6,2},{7,3},{8,12},{9,13},{10,... | collective-permute-start | bytes 884744 | tf_op jit(solution)/shard_map/ppermute | solution.py:60
  34.5 15.4 %collective-permute-start.4 = (bf16[2,288,256]{2,1,0:T(8,128)(2,1)S(1)}, bf16[2,288,256]{2,1,0:T(8,128)(2,1)S(1)}, u32[]{:S(2)}, u32[]{:S(2)}) collective-permute-start(bf16[2,288,256]{2,1,0:T(8,128)(2,1)S(1)} %get-tuple-element.21.refs_1_), channel_id=1, source_target_pairs={{0,16},{1,9},{2,18},{3,11},{4,20},{5,13},{6,22},{7,15},{8,24},{9,1... | collective-permute-start | bytes 884744 | tf_op jit(solution)/shard_map/ppermute | solution.py:63
  42.9 8.9 %collective-permute-start.8 = (bf16[2,288,256]{2,1,0:T(8,128)(2,1)S(1)}, bf16[2,288,256]{2,1,0:T(8,128)(2,1)S(1)}, u32[]{:S(2)}, u32[]{:S(2)}) collective-permute-start(bf16[2,288,256]{2,1,0:T(8,128)(2,1)S(1)} %collective-permute-done.7.refs_6_), channel_id=1, source_target_pairs={{0,8},{1,17},{2,10},{3,19},{4,12},{5,21},{6,14},{7,23},{8,0},{9,25... | collective-permute-start | bytes 884744 | tf_op jit(solution)/shard_map/ppermute | solution.py:63
  44.6 11.0 %collective-permute-start.5 = (bf16[2,288,256]{2,1,0:T(8,128)(2,1)S(1)}, bf16[2,288,256]{2,1,0:T(8,128)(2,1)S(1)}, u32[]{:S(2)}, u32[]{:S(2)}) collective-permute-start(bf16[2,288,256]{2,1,0:T(8,128)(2,1)S(1)} %collective-permute-done.3.refs_2_), channel_id=1, source_target_pairs={{0,16},{1,9},{2,18},{3,11},{4,20},{5,13},{6,22},{7,15},{8,24},{9,1... | collective-permute-start | bytes 884744 | tf_op jit(solution)/shard_map/ppermute | solution.py:63
  47.9 10.3 %collective-permute-start.13 = (bf16[2,288,256]{2,1,0:T(8,128)(2,1)S(1)}, bf16[2,288,256]{2,1,0:T(8,128)(2,1)S(1)}, u32[]{:S(2)}, u32[]{:S(2)}) collective-permute-start(bf16[2,288,256]{2,1,0:T(8,128)(2,1)S(1)} %collective-permute-done.12.refs_11_), channel_id=1, source_target_pairs={{0,8},{1,17},{2,10},{3,19},{4,12},{5,21},{6,14},{7,23},{8,0},{9,25... | collective-permute-start | bytes 884744 | tf_op jit(solution)/shard_map/ppermute | solution.py:63
  49.4 12.6 %collective-permute-start.9 = (bf16[2,288,256]{2,1,0:T(8,128)(2,1)S(1)}, bf16[2,288,256]{2,1,0:T(8,128)(2,1)S(1)}, u32[]{:S(2)}, u32[]{:S(2)}) collective-permute-start(bf16[2,288,256]{2,1,0:T(8,128)(2,1)S(1)} %collective-permute-done.7.refs_6_), channel_id=1, source_target_pairs={{0,16},{1,9},{2,18},{3,11},{4,20},{5,13},{6,22},{7,15},{8,24},{9,1... | collective-permute-start | bytes 884744 | tf_op jit(solution)/shard_map/ppermute | solution.py:63
  49.9 12.2 %collective-permute-start.17 = (bf16[2,288,256]{2,1,0:T(8,128)(2,1)S(1)}, bf16[2,288,256]{2,1,0:T(8,128)(2,1)S(1)}, u32[]{:S(2)}, u32[]{:S(2)}) collective-permute-start(bf16[2,288,256]{2,1,0:T(8,128)(2,1)S(1)} %collective-permute-done.12.refs_11_), channel_id=1, source_target_pairs={{0,2},{1,3},{2,0},{3,1},{4,6},{5,7},{6,4},{7,5},{8,10},{9,11},{10,... | collective-permute-start | bytes 884744 | tf_op jit(solution)/shard_map/ppermute | solution.py:60
  51.8 10.4 %collective-permute-start.10 = (bf16[2,288,256]{2,1,0:T(8,128)(2,1)S(1)}, bf16[2,288,256]{2,1,0:T(8,128)(2,1)S(1)}, u32[]{:S(2)}, u32[]{:S(2)}) collective-permute-start(bf16[2,288,256]{2,1,0:T(8,128)(2,1)S(1)} %collective-permute-done.8.refs_7_), channel_id=1, source_target_pairs={{0,16},{1,9},{2,18},{3,11},{4,20},{5,13},{6,22},{7,15},{8,24},{9,1... | collective-permute-start | bytes 884744 | tf_op jit(solution)/shard_map/ppermute | solution.py:63
  55.5 9.3 %collective-permute-start.14 = (bf16[2,288,256]{2,1,0:T(8,128)(2,1)S(1)}, bf16[2,288,256]{2,1,0:T(8,128)(2,1)S(1)}, u32[]{:S(2)}, u32[]{:S(2)}) collective-permute-start(bf16[2,288,256]{2,1,0:T(8,128)(2,1)S(1)} %collective-permute-done.12.refs_11_), channel_id=1, source_target_pairs={{0,16},{1,9},{2,18},{3,11},{4,20},{5,13},{6,22},{7,15},{8,24},{9,1... | collective-permute-start | bytes 884744 | tf_op jit(solution)/shard_map/ppermute | solution.py:63
  58.2 12.2 %collective-permute-start.15 = (bf16[2,288,256]{2,1,0:T(8,128)(2,1)S(1)}, bf16[2,288,256]{2,1,0:T(8,128)(2,1)S(1)}, u32[]{:S(2)}, u32[]{:S(2)}) collective-permute-start(bf16[2,288,256]{2,1,0:T(8,128)(2,1)S(1)} %collective-permute-done.13.refs_12_), channel_id=1, source_target_pairs={{0,16},{1,9},{2,18},{3,11},{4,20},{5,13},{6,22},{7,15},{8,24},{9,1... | collective-permute-start | bytes 884744 | tf_op jit(solution)/shard_map/ppermute | solution.py:63
  62.0 21.2 %collective-permute-start.6 = (bf16[8,288,256]{2,1,0:T(8,128)(2,1)S(1)}, bf16[8,288,256]{2,1,0:T(8,128)(2,1)S(1)}, u32[]{:S(2)}, u32[]{:S(2)}) collective-permute-start(bf16[8,288,256]{2,1,0:T(8,128)(2,1)S(1)} %pad_maximum_fusion), channel_id=1, source_target_pairs={{0,1},{1,0},{2,3},{3,2},{4,5},{5,4},{6,7},{7,6},{8,9},{9,8},{10,11... | collective-permute-start | bytes 3538952 | tf_op jit(solution)/shard_map/ppermute | solution.py:66
  62.1 12.3 %collective-permute-start.19 = (bf16[2,288,256]{2,1,0:T(8,128)(2,1)S(1)}, bf16[2,288,256]{2,1,0:T(8,128)(2,1)S(1)}, u32[]{:S(2)}, u32[]{:S(2)}) collective-permute-start(bf16[2,288,256]{2,1,0:T(8,128)(2,1)S(1)} %collective-permute-done.17.refs_17_), channel_id=1, source_target_pairs={{0,16},{1,9},{2,18},{3,11},{4,20},{5,13},{6,22},{7,15},{8,24},{9,1... | collective-permute-start | bytes 884744 | tf_op jit(solution)/shard_map/ppermute | solution.py:63
  62.2 12.2 %collective-permute-start.18 = (bf16[2,288,256]{2,1,0:T(8,128)(2,1)S(1)}, bf16[2,288,256]{2,1,0:T(8,128)(2,1)S(1)}, u32[]{:S(2)}, u32[]{:S(2)}) collective-permute-start(bf16[2,288,256]{2,1,0:T(8,128)(2,1)S(1)} %collective-permute-done.17.refs_17_), channel_id=1, source_target_pairs={{0,8},{1,17},{2,10},{3,19},{4,12},{5,21},{6,14},{7,23},{8,0},{9,25... | collective-permute-start | bytes 884744 | tf_op jit(solution)/shard_map/ppermute | solution.py:63
  64.9 18.3 %collective-permute-start.11 = (bf16[8,288,256]{2,1,0:T(8,128)(2,1)S(1)}, bf16[8,288,256]{2,1,0:T(8,128)(2,1)S(1)}, u32[]{:S(2)}, u32[]{:S(2)}) collective-permute-start(bf16[8,288,256]{2,1,0:T(8,128)(2,1)S(1)} %pad_maximum_fusion.1), channel_id=1, source_target_pairs={{0,1},{1,0},{2,3},{3,2},{4,5},{5,4},{6,7},{7,6},{8,9},{9,8},{10,11... | collective-permute-start | bytes 3538952 | tf_op jit(solution)/shard_map/ppermute | solution.py:66
  70.5 12.7 %copy-start = (f32[256]{0:T(256)S(1)}, f32[256]{0:T(256)}, u32[]{:S(2)}) copy-start(f32[256]{0:T(256)} %param.15) | copy-start | bytes 3076
  70.5 12.7 %copy-start.1 = (f32[256]{0:T(256)S(1)}, f32[256]{0:T(256)}, u32[]{:S(2)}) copy-start(f32[256]{0:T(256)} %param.16) | copy-start | bytes 3076
  70.5 12.7 %copy-start.2 = (f32[256]{0:T(256)S(1)}, f32[256]{0:T(256)}, u32[]{:S(2)}) copy-start(f32[256]{0:T(256)} %param.17) | copy-start | bytes 3076
  70.5 12.7 %collective-permute-start.16 = (bf16[8,288,256]{2,1,0:T(8,128)(2,1)S(1)}, bf16[8,288,256]{2,1,0:T(8,128)(2,1)S(1)}, u32[]{:S(2)}, u32[]{:S(2)}) collective-permute-start(bf16[8,288,256]{2,1,0:T(8,128)(2,1)S(1)} %pad_maximum_fusion.2), channel_id=1, source_target_pairs={{0,1},{1,0},{2,3},{3,2},{4,5},{5,4},{6,7},{7,6},{8,9},{9,8},{10,11... | collective-permute-start | bytes 3538952 | tf_op jit(solution)/shard_map/ppermute | solution.py:66
  74.5 8.7 %collective-permute-start.20 = (bf16[6,288,256]{2,1,0:T(8,128)(2,1)S(1)}, bf16[6,288,256]{2,1,0:T(8,128)(2,1)S(1)}, u32[]{:S(2)}, u32[]{:S(2)}) collective-permute-start(bf16[6,288,256]{2,1,0:T(8,128)(2,1)S(1)} %pad_maximum_fusion.3), channel_id=1, source_target_pairs={{0,1},{1,0},{2,3},{3,2},{4,5},{5,4},{6,7},{7,6},{8,9},{9,8},{10,11... | collective-permute-start | bytes 2654216 | tf_op jit(solution)/shard_map/ppermute | solution.py:66
  74.9 6.7 %collective-permute-start.21 = (bf16[2,288,256]{2,1,0:T(8,128)(2,1)S(1)}, bf16[2,288,256]{2,1,0:T(8,128)(2,1)S(1)}, u32[]{:S(2)}, u32[]{:S(2)}) collective-permute-start(bf16[2,288,256]{2,1,0:T(8,128)(2,1)S(1)} %collective-permute-done.18.refs_18_), channel_id=1, source_target_pairs={{0,16},{1,9},{2,18},{3,11},{4,20},{5,13},{6,22},{7,15},{8,24},{9,1... | collective-permute-start | bytes 884744 | tf_op jit(solution)/shard_map/ppermute | solution.py:63
  81.6 1.6 %collective-permute-start.22 = (bf16[2,288,256]{2,1,0:T(8,128)(2,1)S(1)}, bf16[2,288,256]{2,1,0:T(8,128)(2,1)S(1)}, u32[]{:S(2)}, u32[]{:S(2)}) collective-permute-start(bf16[2,288,256]{2,1,0:T(8,128)(2,1)S(1)} %collective-permute-done.21.refs_20_), channel_id=1, source_target_pairs={{0,1},{1,0},{2,3},{3,2},{4,5},{5,4},{6,7},{7,6},{8,9},{9,8},{10,11... | collective-permute-start | bytes 884744 | tf_op jit(solution)/shard_map/ppermute | solution.py:66

commit v2 on v1

--- a/solution.py
+++ b/solution.py
@@ -2,6 +2,7 @@
 
 import jax
 import jax.numpy as jnp
+import numpy as np
 from jax import lax
 from jax.experimental import pallas as pl
 from jax.experimental.pallas import tpu as pltpu
@@ -36,20 +37,73 @@
     return pairs(learners, actors, lambda l, a: (l ^ (low if a % 2 == 0 else high), a))
 
 
+def pick_kernel(subsets, bits, gradients, *refs):
+    outs, arrived = refs[:-1], refs[-1]
+    me, core = lax.axis_index("learn"), lax.axis_index("act") % 2
+    copies = []
+    for number, (subset, out) in enumerate(zip(subsets, outs)):
+        layer = me ^ jnp.where(core == 0, route_mask(0, subset, bits), route_mask(1, subset, bits))
+        copies.append(pltpu.make_async_copy(gradients.at[layer], out, arrived.at[number]))
+        copies[-1].start()
+    for copy in copies:
+        copy.wait()
+
+
+def pick(gradients, subsets, bits):
+    shape = jax.ShapeDtypeStruct(gradients.shape[1:], gradients.dtype)
+    return pl.pallas_call(
+        functools.partial(pick_kernel, subsets, bits),
+        out_shape=[shape] * len(subsets),
+        in_specs=[pl.BlockSpec(memory_space=pl.ANY)],
+        out_specs=[pl.BlockSpec(memory_space=pltpu.VMEM)] * len(subsets),
+        scratch_shapes=[pltpu.SemaphoreType.DMA((len(subsets),))],
+        compiler_params=pltpu.CompilerParams(vmem_limit_bytes=32 * 2**20),
+        name="pick",
+    )(gradients)
+
+
 def reduce_gradients(gradients, learners, actors):
     bits = learners.bit_length() - 1
-    me, core = lax.axis_index("learn"), lax.axis_index("act") % 2
-    held = {}
-    for subset in range(learners):
-        layer = me ^ jnp.where(core == 0, route_mask(0, subset, bits), route_mask(1, subset, bits))
-        held[subset] = lax.dynamic_index_in_dim(gradients, layer, 0, keepdims=False)
+    order = sorted(range(learners), key=lambda subset: (not subset & 1, -subset))
+    held, terms = {}, []
+    for subsets in (order[:1], order[1:]):
+        held.update(zip(subsets, pick(gradients, subsets, bits)))
     for step in range(bits):
         route = plane_route(learners, actors, step)
         for subset in sorted(held, reverse=True):
             if subset >> step & 1:
                 kept = subset ^ 1 << step
-                held[kept] = held[kept] + lax.ppermute(held.pop(subset), AXES, route)
-    return held[0]
+                came = lax.ppermute(held.pop(subset), AXES, route)
+                if kept:
+                    held[kept] = held[kept] + came
+                else:
+                    terms.append(came)
+    return held[0], *terms
+
+
+def update_kernel(learners, *refs):
+    *terms, master, updated, rounded = refs
+    total = terms[0][...]
+    for term in terms[1:]:
+        total = total + term[...]
+    new = master[...] - total / learners
+    updated[...] = new
+    rounded[...] = new.astype(jnp.bfloat16)
+
+
+def update(terms, master, learners):
+    inside = pl.BlockSpec(memory_space=pltpu.VMEM)
+    return pl.pallas_call(
+        functools.partial(update_kernel, learners),
+        out_shape=(
+            jax.ShapeDtypeStruct(master.shape, jnp.float32),
+            jax.ShapeDtypeStruct(master.shape, jnp.bfloat16),
+        ),
+        in_specs=[inside] * (len(terms) + 1),
+        out_specs=(inside, inside),
+        compiler_params=pltpu.CompilerParams(vmem_limit_bytes=32 * 2**20),
+        name="update",
+    )(*terms, master)
 
 
 def gather_blocks(own, learners, actors):
@@ -81,7 +135,11 @@
         held = {0: starts[away]}
         for step in range(bits):
             for subset in sorted(held):
-                held[subset | 1 << step] = along_plane(held[subset], step)
+                if (away, subset | 1 << step) in ((1,3),):
+                    held[subset | 1 << step] = along_z(before[subset | 1 << step], 1)
+                else:
+                    held[subset | 1 << step] = along_plane(held[subset], step)
+        before = held
         groups = [sorted(held)] if away < chips - 1 else [sorted(held)[:-1], [learners - 1]]
         for group in groups:
             joined = jnp.concatenate([held[subset] for subset in group], axis=0) if len(group) > 1 else held[group[0]]
@@ -98,8 +156,8 @@
 
 def tower(places, layers, rows, number, width, cuts, *refs):
     blocks = refs[: len(places)]
-    stem, legal, policy, passing, valuing, logp, extra = refs[len(places) : len(places) + 7]
-    weights, field, stream, mask, arrived = refs[len(places) + 7 :]
+    stem, legal, policy, passing, valuing, places_of_points, logp, worth = refs[len(places) : len(places) + 8]
+    weights, field, stream, mask, arrived = refs[len(places) + 8 :]
     points = BOARD * width
     for labels, block in zip(places, blocks):
         if labels is None:
@@ -171,12 +229,32 @@
     allowed = inside & (legal[...] > 0)
     shares = jnp.sum(jnp.where(allowed, jnp.exp(logits), 0.0), axis=1, keepdims=True)
     scale = jnp.log(shares + jnp.exp(pass_logit))
-    logp[...] = jnp.where(allowed, logits - scale, 0.0)
-    lane = lax.broadcasted_iota(jnp.int32, extra.shape, 1)
-    extra[...] = jnp.where(lane == 0, pass_logit - scale, value)
-
-
-def run_tower(found, layers, rows, depth, stem, legal, policy, passing, valuing, number, width):
+    padded = jnp.where(allowed, logits - scale, 0.0)
+    parts, rest = [], padded
+    for _ in range(3):
+        parts.append(rest.astype(jnp.bfloat16))
+        rest = rest - parts[-1].astype(jnp.float32)
+    parts = jnp.concatenate(parts, axis=0)
+    moved = jnp.dot(parts, places_of_points[...], preferred_element_type=jnp.float32)
+    packed = moved[:8] + moved[8:16] + moved[16:]
+    lane = lax.broadcasted_iota(jnp.int32, packed.shape, 1)
+    packed = jnp.where(lane == CELLS, pass_logit - scale, packed)
+    steps_here, local_count = logp.shape[:2]
+    for board in range(number):
+        step, local = divmod(board, local_count)
+        logp[step, local : local + 1, :] = packed[board : board + 1, : CELLS + 1]
+        worth[local : local + 1, step : step + 1] = value[board : board + 1, :]
+
+
+def run_tower(found, layers, rows, depth, stem, legal, policy, passing, valuing, steps_here, local_count, width):
+    number = steps_here * local_count
+    point = np.arange(BOARD * width)
+    column = point % width
+    cell = point // width * BOARD + column % PITCH
+    known = (column % PITCH < BOARD) & (column < PITCH * number)
+    lanes = -(-(CELLS + 1) // 128) * 128
+    target = np.where(known, cell, lanes)[:, None] == np.arange(lanes)[None]
+    places_of_points = jnp.asarray(target.astype(jnp.bfloat16))
     points = BOARD * width
     channels = stem.shape[1]
     places = [labels for _, labels in found]
@@ -187,10 +265,10 @@
     return pl.pallas_call(
         functools.partial(tower, places, layers, rows, number, width, cuts),
         out_shape=(
-            jax.ShapeDtypeStruct((8, points), jnp.float32),
-            jax.ShapeDtypeStruct((8, 128), jnp.float32),
+            jax.ShapeDtypeStruct((steps_here, local_count, CELLS + 1), jnp.float32),
+            jax.ShapeDtypeStruct((local_count, steps_here), jnp.float32),
         ),
-        in_specs=[anywhere] * len(found) + [inside] * 5,
+        in_specs=[anywhere] * len(found) + [inside] * 6,
         out_specs=(inside, inside),
         scratch_shapes=[
             pltpu.VMEM((layers, 2, depth, channels), jnp.bfloat16),
@@ -201,7 +279,7 @@
         ],
         compiler_params=pltpu.CompilerParams(vmem_limit_bytes=36 * 2**20),
         name="tower",
-    )(*[block for block, _ in found], stem, legal, policy, passing, valuing)
+    )(*[block for block, _ in found], stem, legal, policy, passing, valuing, places_of_points)
 
 
 def padded_boards(rows, width):
@@ -250,10 +328,10 @@
     stem = stem_stream(boards, to_move.reshape(number), stem_weight, width)
     legal = padded_boards(legal_moves.reshape(number, CELLS), width).reshape(1, BOARD * width)
 
-    total = reduce_gradients(gradients[0], learners, actors)
-    total, stem, legal = lax.optimization_barrier((total, stem, legal))
-    updated = master[0] - total / learners
-    found = gather_blocks(updated.astype(jnp.bfloat16), learners, actors)
+    terms = reduce_gradients(gradients[0], learners, actors)
+    *terms, stem, legal = lax.optimization_barrier((*terms, stem, legal))
+    updated, rounded = update(terms, master[0], learners)
+    found = gather_blocks(rounded, learners, actors)
     if rows % 16:
         whole = jnp.zeros((learners, 2, depth, channels), jnp.bfloat16)
         for block, labels in found:
@@ -262,7 +340,7 @@
                 piece = block[2 * entry : 2 * entry + 2]
                 whole = lax.dynamic_update_slice(whole, piece[None], (layer, 0, actor * rows, 0))
         found = [(whole, None)]
-    logp, extra = run_tower(
+    logp, values = run_tower(
         found,
         learners,
         rows,
@@ -272,20 +350,11 @@
         policy_weight[None],
         pass_weight[None],
         value_weight[None],
-        number,
+        steps_here,
+        local_count,
         width,
     )
-    boards_out = logp[:number].reshape(number, BOARD, width)
-    moves = [
-        boards_out[board, :, board * PITCH : board * PITCH + BOARD].reshape(1, CELLS)
-        for board in range(number)
-    ]
-    moves = jnp.concatenate([jnp.concatenate(moves, axis=0), extra[:number, :1]], axis=1)
-    return (
-        updated[None],
-        moves.reshape(steps_here, local_count, CELLS + 1),
-        extra[:number, 1].reshape(steps_here, local_count),
-    )
+    return updated[None], logp, values.T
 
 
 def solution(mesh):

time: 97.3 us -> 91.4 us (0.939)
  starting transfers between devices: 33.4 us -> 24.7 us
  waiting for transfers between devices: 35.7 us -> 41 us
  other arithmetic: 5 us -> 1.63 us
  Pallas kernels: 12.2 us -> 15.2 us
  local copies, waits for them, and re-layouts: 6.13 us -> 3.87 us
    ppermute x12 -> x11, starting transfers between devices: 21.2 us -> 12.6 us  [along_plane(): return lax.ppermute(block, AXES, plane_route(learners, actors, step))]
    ppermute x3 -> x4, waiting for transfers between devices: 7.64 us -> 11.7 us  [along_z(): lax.ppermute(block, AXES, pairs(learners, actors, lambda l, a: (l, a ^ 2...]
    add x2 -> x1, other arithmetic: 3.32 us -> 0.92 us  [reduce_gradients(): held[kept] = held[kept] + came]
    squeeze x1 -> x0, local copies, waits for them, and re-layouts: 2.32 us -> none  [reduce_gradients(): held[subset] = lax.dynamic_index_in_dim(gradients, layer, 0, keepdims=False)]
    pallas_call x0 -> x3, Pallas kernels: none -> 2.26 us  [the longest x2 1.33 us: pick(): pl.pallas_call(functools.partial(pick_kernel, subsets, bits), out_shape=[...]
    ppermute x12 -> x11, waiting for transfers between devices: 16.6 us -> 18.5 us  [along_plane(): return lax.ppermute(block, AXES, plane_route(learners, actors, step))]
    ppermute x5, starting transfers between devices: 2.2 us -> 0.8 us  [swapped(): lax.ppermute(block, AXES, pairs(learners, actors, lambda l, a: (l, a ^ 1)))]
    ppermute x3 -> x4, starting transfers between devices: 4.89 us -> 6.19 us  [along_z(): lax.ppermute(block, AXES, pairs(learners, actors, lambda l, a: (l, a ^ 2...]
  transfers between devices with their start and end apart: 23 -> 23, of which waited for: 11 -> 11; matrix products, arithmetic and copies ran while one was open for 8% -> 8% of each run, Pallas kernels for 0% -> 1%
where the time goes in v2:
time: 91.4 us; the launch traced here: 91.2 us
  waiting for transfers between devices  41 us (45%)
  starting transfers between devices  24.7 us (27%)
  Pallas kernels  15.2 us (17%)
  local copies, waits for them, and re-layouts  3.87 us (4%)
  matrix products  3.72 us (4%)
  other arithmetic  1.63 us (2%)
  between operations  1.11 us (1%)
    ppermute x11, waiting for transfers between devices, along_plane(): return lax.ppermute(block, AXES, plane_route(learners, actors, step))  18.5 us
    pallas_call x1, Pallas kernels, run_tower(): pl.pallas_call(functools.partial(tower, places, layers, rows, number, wid...  13 us
    ppermute x11, starting transfers between devices, along_plane(): return lax.ppermute(block, AXES, plane_route(learners, actors, step))  12.6 us
    ppermute x4, waiting for transfers between devices, along_z(): lax.ppermute(block, AXES, pairs(learners, actors, lambda l, a: (l, a ^ 2...  11.7 us
    ppermute x3, waiting for transfers between devices, reduce_gradients(): came = lax.ppermute(held.pop(subset), AXES, route)  9.2 us
    ppermute x4, starting transfers between devices, along_z(): lax.ppermute(block, AXES, pairs(learners, actors, lambda l, a: (l, a ^ 2...  6.19 us
    ppermute x3, starting transfers between devices, reduce_gradients(): came = lax.ppermute(held.pop(subset), AXES, route)  5.15 us
    conv_general_dilated x1, matrix products, stem_stream(): lax.conv_general_dilated(field, kernel, (1, 1), ((1, 1), (1, 1)), dimensi...  3.72 us
  transfers between devices with their start and end apart: 23, of which 11 were waited for; matrix products, arithmetic and copies ran while one was open for 8% of the time, Pallas kernels for 1%

profile of v2, /device:TPU:0, one launch (start us, length us, event | category | flops | bytes accessed | tf_op | source)
XLA Modules:
  0.0 91.2 jit_solution(11242763497380835320)
XLA Ops:
  0.6 1.7 %copy-done = f32[1,4,2,288,256]{4,3,2,1,0:T(8,128)S(1)} copy-done((f32[1,4,2,288,256]{4,3,2,1,0:T(8,128)S(1)}, f32[1,4,2,288,256]{4,3,2,1,0:T(8,128)}, u32[]{:S(2)}) %copy-start) | copy-done | bytes 2359320
  2.5 3.0 %collective-permute-start.1 = (f32[2,288,256]{2,1,0:T(8,128)S(1)}, f32[2,288,256]{2,1,0:T(8,128)S(1)}, u32[]{:S(2)}, u32[]{:S(2)}) collective-permute-start(f32[2,288,256]{2,1,0:T(8,128)S(1)} %pick.3), channel_id=1, source_target_pairs={{0,8},{1,17},{2,10},{3,19},{4,12},{5,21},{6,14},{7,23},{8,0},{9,25... | collective-permute-start | bytes 1769480 | tf_op jit(solution)/shard_map/ppermute | solution.py:76
  5.5 1.2 %pick.2 = (f32[2,288,256]{2,1,0:T(8,128)}, f32[2,288,256]{2,1,0:T(8,128)S(1)}, f32[2,288,256]{2,1,0:T(8,128)S(1)}) custom-call(f32[4,2,288,256]{3,2,1,0:T(8,128)S(1)} %bitcast.25), custom_call_target="tpu_custom_call" | custom-call | tf_op jit(solution)/shard_map/pick/pallas_call | solution.py:54
  7.2 6.1 %collective-permute-done.1 = f32[2,288,256]{2,1,0:T(8,128)S(1)} collective-permute-done((f32[2,288,256]{2,1,0:T(8,128)S(1)}, f32[2,288,256]{2,1,0:T(8,128)S(1)}, u32[]{:S(2)}, u32[]{:S(2)}) %collective-permute-start.1) | collective-permute-done | bytes 589856 | tf_op jit(solution)/shard_map/ppermute | solution.py:76
  13.3 0.9 %add.10 = f32[2,288,256]{2,1,0:T(8,128)} add(f32[2,288,256]{2,1,0:T(8,128)S(1)} %get-tuple-element.17, f32[2,288,256]{2,1,0:T(8,128)S(1)} %collective-permute-done.1) | non-fusion elementwise | flops 147456 | bytes 1769472 | tf_op jit(solution)/shard_map/add | solution.py:78
  14.2 2.0 %collective-permute-start.2 = (f32[2,288,256]{2,1,0:T(8,128)}, f32[2,288,256]{2,1,0:T(8,128)S(1)}, u32[]{:S(2)}, u32[]{:S(2)}) collective-permute-start(f32[2,288,256]{2,1,0:T(8,128)} %add.10), channel_id=1, source_target_pairs={{0,16},{1,9},{2,18},{3,11},{4,20},{5,13},{6,22},{7,15},{8,24},{9,1... | collective-permute-start | bytes 1769480 | tf_op jit(solution)/shard_map/ppermute | solution.py:76
  16.5 0.8 copy.21
  17.4 3.7 %fusion.3 = f32[1,19,40,256]{3,0,2,1:T(1,128)S(1)} fusion(bf16[1,19,40,4]{3,0,2,1:T(2,128)(2,1)S(1)} %copy.21, bf16[3,3,4,256]{3,2,1,0:T(4,128)(2,1)S(1)} %reshape.50), kind=kOutput, calls=%fused_computation.17 | convolution fusion | flops 13291520 | bytes 802752 | tf_op jit(solution)/shard_map/conv_general_dilated | solution.py:298
  22.0 0.8 collective-permute-done.refs_1_
  22.9 2.3 %collective-permute-done.2.refs_2_ = f32[2,288,256]{2,1,0:T(8,128)S(1)} collective-permute-done((f32[2,288,256]{2,1,0:T(8,128)}, f32[2,288,256]{2,1,0:T(8,128)S(1)}, u32[]{:S(2)}, u32[]{:S(2)}) %collective-permute-start.2) | collective-permute-done | bytes 589856 | tf_op jit(solution)/shard_map/ppermute | solution.py:76
  25.1 0.9 %update.1 = (f32[2,288,256]{2,1,0:T(8,128)}, bf16[2,288,256]{2,1,0:T(8,128)(2,1)S(1)}) custom-call(f32[2,288,256]{2,1,0:T(8,128)S(1)} %get-tuple-element.18.refs_0_, f32[2,288,256]{2,1,0:T(8,128)S(1)} %collective-permute-done.refs_1_, f32[2,288,256]{2,1,0:T(8,128)S(1)} %collective-permute-done.2.refs_2_, f32[2,288,256]{2,1,0:T(8,128)S(1)} %bitcast.27), custom_call_target="tpu_custom_call" | custom-call | tf_op jit(solution)/shard_map/update/pallas_call | solution.py:96
  26.1 1.7 %collective-permute-start.3 = (bf16[2,288,256]{2,1,0:T(8,128)(2,1)S(1)}, bf16[2,288,256]{2,1,0:T(8,128)(2,1)S(1)}, u32[]{:S(2)}, u32[]{:S(2)}) collective-permute-start(bf16[2,288,256]{2,1,0:T(8,128)(2,1)S(1)} %get-tuple-element.22.refs_1_), channel_id=1, source_target_pairs={{0,8},{1,17},{2,10},{3,19},{4,12},{5,21},{6,14},{7,23},{8,0},{9,25... | collective-permute-start | bytes 884744 | tf_op jit(solution)/shard_map/ppermute | solution.py:117
  27.8 1.6 %collective-permute-start.7 = (bf16[2,288,256]{2,1,0:T(8,128)(2,1)S(1)}, bf16[2,288,256]{2,1,0:T(8,128)(2,1)S(1)}, u32[]{:S(2)}, u32[]{:S(2)}) collective-permute-start(bf16[2,288,256]{2,1,0:T(8,128)(2,1)S(1)} %get-tuple-element.22.refs_1_), channel_id=1, source_target_pairs={{0,2},{1,3},{2,0},{3,1},{4,6},{5,7},{6,4},{7,5},{8,10},{9,11},{10,... | collective-permute-start | bytes 884744 | tf_op jit(solution)/shard_map/ppermute | solution.py:114
  29.4 2.6 %collective-permute-start.12 = (bf16[2,288,256]{2,1,0:T(8,128)(2,1)S(1)}, bf16[2,288,256]{2,1,0:T(8,128)(2,1)S(1)}, u32[]{:S(2)}, u32[]{:S(2)}) collective-permute-start(bf16[2,288,256]{2,1,0:T(8,128)(2,1)S(1)} %get-tuple-element.22.refs_1_), channel_id=1, source_target_pairs={{0,4},{1,5},{2,6},{3,7},{4,0},{5,1},{6,2},{7,3},{8,12},{9,13},{10,... | collective-permute-start | bytes 884744 | tf_op jit(solution)/shard_map/ppermute | solution.py:114
  31.9 1.5 %collective-permute-start.4 = (bf16[2,288,256]{2,1,0:T(8,128)(2,1)S(1)}, bf16[2,288,256]{2,1,0:T(8,128)(2,1)S(1)}, u32[]{:S(2)}, u32[]{:S(2)}) collective-permute-start(bf16[2,288,256]{2,1,0:T(8,128)(2,1)S(1)} %get-tuple-element.22.refs_1_), channel_id=1, source_target_pairs={{0,16},{1,9},{2,18},{3,11},{4,20},{5,13},{6,22},{7,15},{8,24},{9,1... | collective-permute-start | bytes 884744 | tf_op jit(solution)/shard_map/ppermute | solution.py:117
  33.5 1.1 %collective-permute-start.5 = (bf16[2,288,256]{2,1,0:T(8,128)(2,1)S(1)}, bf16[2,288,256]{2,1,0:T(8,128)(2,1)S(1)}, u32[]{:S(2)}, u32[]{:S(2)}) collective-permute-start(bf16[2,288,256]{2,1,0:T(8,128)(2,1)S(1)} %collective-permute-done.3.refs_2_), channel_id=1, source_target_pairs={{0,16},{1,9},{2,18},{3,11},{4,20},{5,13},{6,22},{7,15},{8,24},{9,1... | collective-permute-start | bytes 884744 | tf_op jit(solution)/shard_map/ppermute | solution.py:117
  34.5 9.1 %collective-permute-done.7.refs_6_ = bf16[2,288,256]{2,1,0:T(8,128)(2,1)S(1)} collective-permute-done((bf16[2,288,256]{2,1,0:T(8,128)(2,1)S(1)}, bf16[2,288,256]{2,1,0:T(8,128)(2,1)S(1)}, u32[]{:S(2)}, u32[]{:S(2)}) %collective-permute-start.7) | collective-permute-done | bytes 294944 | tf_op jit(solution)/shard_map/ppermute | solution.py:114
  43.9 2.0 %collective-permute-done.12.refs_11_ = bf16[2,288,256]{2,1,0:T(8,128)(2,1)S(1)} collective-permute-done((bf16[2,288,256]{2,1,0:T(8,128)(2,1)S(1)}, bf16[2,288,256]{2,1,0:T(8,128)(2,1)S(1)}, u32[]{:S(2)}, u32[]{:S(2)}) %collective-permute-start.12) | collective-permute-done | bytes 294944 | tf_op jit(solution)/shard_map/ppermute | solution.py:114
  46.0 0.7 collective-permute-start.13
  46.7 1.3 %collective-permute-start.8 = (bf16[2,288,256]{2,1,0:T(8,128)(2,1)S(1)}, bf16[2,288,256]{2,1,0:T(8,128)(2,1)S(1)}, u32[]{:S(2)}, u32[]{:S(2)}) collective-permute-start(bf16[2,288,256]{2,1,0:T(8,128)(2,1)S(1)} %collective-permute-done.7.refs_6_), channel_id=1, source_target_pairs={{0,8},{1,17},{2,10},{3,19},{4,12},{5,21},{6,14},{7,23},{8,0},{9,25... | collective-permute-start | bytes 884744 | tf_op jit(solution)/shard_map/ppermute | solution.py:117
  48.4 1.6 %collective-permute-start.10 = (bf16[2,288,256]{2,1,0:T(8,128)(2,1)S(1)}, bf16[2,288,256]{2,1,0:T(8,128)(2,1)S(1)}, u32[]{:S(2)}, u32[]{:S(2)}) collective-permute-start(bf16[2,288,256]{2,1,0:T(8,128)(2,1)S(1)} %collective-permute-done.5.refs_4_), channel_id=1, source_target_pairs={{0,2},{1,3},{2,0},{3,1},{4,6},{5,7},{6,4},{7,5},{8,10},{9,11},{10,... | collective-permute-start | bytes 884744 | tf_op jit(solution)/shard_map/ppermute | solution.py:114
  50.0 3.4 %collective-permute-done.9.refs_8_ = bf16[2,288,256]{2,1,0:T(8,128)(2,1)S(1)} collective-permute-done((bf16[2,288,256]{2,1,0:T(8,128)(2,1)S(1)}, bf16[2,288,256]{2,1,0:T(8,128)(2,1)S(1)}, u32[]{:S(2)}, u32[]{:S(2)}) %collective-permute-start.9) | collective-permute-done | bytes 294944 | tf_op jit(solution)/shard_map/ppermute | solution.py:117
  53.6 1.9 %collective-permute-start.15 = (bf16[2,288,256]{2,1,0:T(8,128)(2,1)S(1)}, bf16[2,288,256]{2,1,0:T(8,128)(2,1)S(1)}, u32[]{:S(2)}, u32[]{:S(2)}) collective-permute-start(bf16[2,288,256]{2,1,0:T(8,128)(2,1)S(1)} %collective-permute-done.13.refs_12_), channel_id=1, source_target_pairs={{0,16},{1,9},{2,18},{3,11},{4,20},{5,13},{6,22},{7,15},{8,24},{9,1... | collective-permute-start | bytes 884744 | tf_op jit(solution)/shard_map/ppermute | solution.py:117
  55.6 4.1 %collective-permute-done.8.refs_7_ = bf16[2,288,256]{2,1,0:T(8,128)(2,1)S(1)} collective-permute-done((bf16[2,288,256]{2,1,0:T(8,128)(2,1)S(1)}, bf16[2,288,256]{2,1,0:T(8,128)(2,1)S(1)}, u32[]{:S(2)}, u32[]{:S(2)}) %collective-permute-start.8) | collective-permute-done | bytes 294944 | tf_op jit(solution)/shard_map/ppermute | solution.py:117
  59.7 0.8 collective-permute-start.19
  60.5 0.6 collective-permute-done.10.refs_9_
  61.2 2.4 %collective-permute-start.18 = (bf16[2,288,256]{2,1,0:T(8,128)(2,1)S(1)}, bf16[2,288,256]{2,1,0:T(8,128)(2,1)S(1)}, u32[]{:S(2)}, u32[]{:S(2)}) collective-permute-start(bf16[2,288,256]{2,1,0:T(8,128)(2,1)S(1)} %collective-permute-done.17.refs_17_), channel_id=1, source_target_pairs={{0,8},{1,17},{2,10},{3,19},{4,12},{5,21},{6,14},{7,23},{8,0},{9,25... | collective-permute-start | bytes 884744 | tf_op jit(solution)/shard_map/ppermute | solution.py:117
  64.6 4.9 %collective-permute-done.19.refs_19_ = bf16[2,288,256]{2,1,0:T(8,128)(2,1)S(1)} collective-permute-done((bf16[2,288,256]{2,1,0:T(8,128)(2,1)S(1)}, bf16[2,288,256]{2,1,0:T(8,128)(2,1)S(1)}, u32[]{:S(2)}, u32[]{:S(2)}) %collective-permute-start.19) | collective-permute-done | bytes 294944 | tf_op jit(solution)/shard_map/ppermute | solution.py:117
  69.7 0.7 collective-permute-start.21
  70.4 6.0 %collective-permute-done.21.refs_20_ = bf16[2,288,256]{2,1,0:T(8,128)(2,1)S(1)} collective-permute-done((bf16[2,288,256]{2,1,0:T(8,128)(2,1)S(1)}, bf16[2,288,256]{2,1,0:T(8,128)(2,1)S(1)}, u32[]{:S(2)}, u32[]{:S(2)}) %collective-permute-start.21) | collective-permute-done | bytes 294944 | tf_op jit(solution)/shard_map/ppermute | solution.py:117
  76.4 1.6 %collective-permute-done.22.refs_16_ = bf16[2,288,256]{2,1,0:T(8,128)(2,1)S(1)} collective-permute-done((bf16[2,288,256]{2,1,0:T(8,128)(2,1)S(1)}, bf16[2,288,256]{2,1,0:T(8,128)(2,1)S(1)}, u32[]{:S(2)}, u32[]{:S(2)}) %collective-permute-start.22) | collective-permute-done | bytes 294944 | tf_op jit(solution)/shard_map/ppermute | solution.py:120
  78.1 13.0 %tower.1 = (f32[2,1,362]{2,1,0:T(1,128)}, f32[1,2]{1,0:T(1,128)}) custom-call(bf16[8,288,256]{2,1,0:T(8,128)(2,1)S(1)} %collective-permute-done.6.refs_0_, bf16[2,288,256]{2,1,0:T(8,128)(2,1)S(1)} %get-tuple-element.22.refs_1_, bf16[2,288,256]{2,1,0:T(8,128)(2,1)S(1)} %collective-permute-done.3.refs_2_, ...), custom_call_target="tpu_custom_call" | custom-call | tf_op jit(solution)/shard_map/tower/pallas_call | solution.py:265
  (70 shorter events, 4.2 us)
Async XLA Ops:
  0.6 1.7 %copy-start = (f32[1,4,2,288,256]{4,3,2,1,0:T(8,128)S(1)}, f32[1,4,2,288,256]{4,3,2,1,0:T(8,128)}, u32[]{:S(2)}) copy-start(f32[1,4,2,288,256]{4,3,2,1,0:T(8,128)} %param.14) | copy-start | bytes 7077892
  2.4 4.4 %copy-start.7 = (s32[2,1,361]{2,1,0:T(1,128)S(1)}, s32[2,1,361]{2,1,0:T(1,128)}, u32[]{:S(2)}) copy-start(s32[2,1,361]{2,1,0:T(1,128)} %param.10) | copy-start | bytes 8668
  2.4 4.6 %copy-start.9 = (s32[2,1]{0,1:T(1,128)S(1)}, s32[2,1]{0,1:T(1,128)}, u32[]{:S(2)}) copy-start(s32[2,1]{0,1:T(1,128)} %param.11) | copy-start | bytes 28
  2.5 10.9 %collective-permute-start.1 = (f32[2,288,256]{2,1,0:T(8,128)S(1)}, f32[2,288,256]{2,1,0:T(8,128)S(1)}, u32[]{:S(2)}, u32[]{:S(2)}) collective-permute-start(f32[2,288,256]{2,1,0:T(8,128)S(1)} %pick.3), channel_id=1, source_target_pairs={{0,8},{1,17},{2,10},{3,19},{4,12},{5,21},{6,14},{7,23},{8,0},{9,25... | collective-permute-start | bytes 1769480 | tf_op jit(solution)/shard_map/ppermute | solution.py:76
  6.7 16.2 %collective-permute-start = (f32[2,288,256]{2,1,0:T(8,128)}, f32[2,288,256]{2,1,0:T(8,128)S(1)}, u32[]{:S(2)}, u32[]{:S(2)}) collective-permute-start(f32[2,288,256]{2,1,0:T(8,128)} %get-tuple-element.16), channel_id=1, source_target_pairs={{0,8},{1,17},{2,10},{3,19},{4,12},{5,21},{6,14},{7,23},{8,0},{9,25... | collective-permute-start | bytes 1769480 | tf_op jit(solution)/shard_map/ppermute | solution.py:76
  13.3 4.0 %copy-start.6 = (bf16[36,256]{1,0:T(8,128)(2,1)S(1)}, bf16[36,256]{1,0:T(8,128)(2,1)}, u32[]{:S(2)}) copy-start(bf16[36,256]{1,0:T(8,128)(2,1)} %param.15) | copy-start | bytes 55300
  14.2 10.9 %collective-permute-start.2 = (f32[2,288,256]{2,1,0:T(8,128)}, f32[2,288,256]{2,1,0:T(8,128)S(1)}, u32[]{:S(2)}, u32[]{:S(2)}) collective-permute-start(f32[2,288,256]{2,1,0:T(8,128)} %add.10), channel_id=1, source_target_pairs={{0,16},{1,9},{2,18},{3,11},{4,20},{5,13},{6,22},{7,15},{8,24},{9,1... | collective-permute-start | bytes 1769480 | tf_op jit(solution)/shard_map/ppermute | solution.py:76
  21.1 4.0 %copy-start.1 = (f32[1,2,288,256]{3,2,1,0:T(8,128)S(1)}, f32[1,2,288,256]{3,2,1,0:T(8,128)}, u32[]{:S(2)}) copy-start(f32[1,2,288,256]{3,2,1,0:T(8,128)} %param.13) | copy-start | bytes 1769476
  26.1 7.4 %collective-permute-start.3 = (bf16[2,288,256]{2,1,0:T(8,128)(2,1)S(1)}, bf16[2,288,256]{2,1,0:T(8,128)(2,1)S(1)}, u32[]{:S(2)}, u32[]{:S(2)}) collective-permute-start(bf16[2,288,256]{2,1,0:T(8,128)(2,1)S(1)} %get-tuple-element.22.refs_1_), channel_id=1, source_target_pairs={{0,8},{1,17},{2,10},{3,19},{4,12},{5,21},{6,14},{7,23},{8,0},{9,25... | collective-permute-start | bytes 884744 | tf_op jit(solution)/shard_map/ppermute | solution.py:117
  27.8 15.8 %collective-permute-start.7 = (bf16[2,288,256]{2,1,0:T(8,128)(2,1)S(1)}, bf16[2,288,256]{2,1,0:T(8,128)(2,1)S(1)}, u32[]{:S(2)}, u32[]{:S(2)}) collective-permute-start(bf16[2,288,256]{2,1,0:T(8,128)(2,1)S(1)} %get-tuple-element.22.refs_1_), channel_id=1, source_target_pairs={{0,2},{1,3},{2,0},{3,1},{4,6},{5,7},{6,4},{7,5},{8,10},{9,11},{10,... | collective-permute-start | bytes 884744 | tf_op jit(solution)/shard_map/ppermute | solution.py:114
  29.4 16.6 %collective-permute-start.12 = (bf16[2,288,256]{2,1,0:T(8,128)(2,1)S(1)}, bf16[2,288,256]{2,1,0:T(8,128)(2,1)S(1)}, u32[]{:S(2)}, u32[]{:S(2)}) collective-permute-start(bf16[2,288,256]{2,1,0:T(8,128)(2,1)S(1)} %get-tuple-element.22.refs_1_), channel_id=1, source_target_pairs={{0,4},{1,5},{2,6},{3,7},{4,0},{5,1},{6,2},{7,3},{8,12},{9,13},{10,... | collective-permute-start | bytes 884744 | tf_op jit(solution)/shard_map/ppermute | solution.py:114
  31.9 16.1 %collective-permute-start.4 = (bf16[2,288,256]{2,1,0:T(8,128)(2,1)S(1)}, bf16[2,288,256]{2,1,0:T(8,128)(2,1)S(1)}, u32[]{:S(2)}, u32[]{:S(2)}) collective-permute-start(bf16[2,288,256]{2,1,0:T(8,128)(2,1)S(1)} %get-tuple-element.22.refs_1_), channel_id=1, source_target_pairs={{0,16},{1,9},{2,18},{3,11},{4,20},{5,13},{6,22},{7,15},{8,24},{9,1... | collective-permute-start | bytes 884744 | tf_op jit(solution)/shard_map/ppermute | solution.py:117
  33.5 15.0 %collective-permute-start.5 = (bf16[2,288,256]{2,1,0:T(8,128)(2,1)S(1)}, bf16[2,288,256]{2,1,0:T(8,128)(2,1)S(1)}, u32[]{:S(2)}, u32[]{:S(2)}) collective-permute-start(bf16[2,288,256]{2,1,0:T(8,128)(2,1)S(1)} %collective-permute-done.3.refs_2_), channel_id=1, source_target_pairs={{0,16},{1,9},{2,18},{3,11},{4,20},{5,13},{6,22},{7,15},{8,24},{9,1... | collective-permute-start | bytes 884744 | tf_op jit(solution)/shard_map/ppermute | solution.py:117
  43.6 9.9 %collective-permute-start.9 = (bf16[2,288,256]{2,1,0:T(8,128)(2,1)S(1)}, bf16[2,288,256]{2,1,0:T(8,128)(2,1)S(1)}, u32[]{:S(2)}, u32[]{:S(2)}) collective-permute-start(bf16[2,288,256]{2,1,0:T(8,128)(2,1)S(1)} %collective-permute-done.7.refs_6_), channel_id=1, source_target_pairs={{0,16},{1,9},{2,18},{3,11},{4,20},{5,13},{6,22},{7,15},{8,24},{9,1... | collective-permute-start | bytes 884744 | tf_op jit(solution)/shard_map/ppermute | solution.py:117
  46.0 7.6 %collective-permute-start.13 = (bf16[2,288,256]{2,1,0:T(8,128)(2,1)S(1)}, bf16[2,288,256]{2,1,0:T(8,128)(2,1)S(1)}, u32[]{:S(2)}, u32[]{:S(2)}) collective-permute-start(bf16[2,288,256]{2,1,0:T(8,128)(2,1)S(1)} %collective-permute-done.12.refs_11_), channel_id=1, source_target_pairs={{0,8},{1,17},{2,10},{3,19},{4,12},{5,21},{6,14},{7,23},{8,0},{9,25... | collective-permute-start | bytes 884744 | tf_op jit(solution)/shard_map/ppermute | solution.py:117
  46.7 13.0 %collective-permute-start.8 = (bf16[2,288,256]{2,1,0:T(8,128)(2,1)S(1)}, bf16[2,288,256]{2,1,0:T(8,128)(2,1)S(1)}, u32[]{:S(2)}, u32[]{:S(2)}) collective-permute-start(bf16[2,288,256]{2,1,0:T(8,128)(2,1)S(1)} %collective-permute-done.7.refs_6_), channel_id=1, source_target_pairs={{0,8},{1,17},{2,10},{3,19},{4,12},{5,21},{6,14},{7,23},{8,0},{9,25... | collective-permute-start | bytes 884744 | tf_op jit(solution)/shard_map/ppermute | solution.py:117
  48.0 11.7 %collective-permute-start.17 = (bf16[2,288,256]{2,1,0:T(8,128)(2,1)S(1)}, bf16[2,288,256]{2,1,0:T(8,128)(2,1)S(1)}, u32[]{:S(2)}, u32[]{:S(2)}) collective-permute-start(bf16[2,288,256]{2,1,0:T(8,128)(2,1)S(1)} %collective-permute-done.12.refs_11_), channel_id=1, source_target_pairs={{0,2},{1,3},{2,0},{3,1},{4,6},{5,7},{6,4},{7,5},{8,10},{9,11},{10,... | collective-permute-start | bytes 884744 | tf_op jit(solution)/shard_map/ppermute | solution.py:114
  48.4 12.7 %collective-permute-start.10 = (bf16[2,288,256]{2,1,0:T(8,128)(2,1)S(1)}, bf16[2,288,256]{2,1,0:T(8,128)(2,1)S(1)}, u32[]{:S(2)}, u32[]{:S(2)}) collective-permute-start(bf16[2,288,256]{2,1,0:T(8,128)(2,1)S(1)} %collective-permute-done.5.refs_4_), channel_id=1, source_target_pairs={{0,2},{1,3},{2,0},{3,1},{4,6},{5,7},{6,4},{7,5},{8,10},{9,11},{10,... | collective-permute-start | bytes 884744 | tf_op jit(solution)/shard_map/ppermute | solution.py:114
  53.4 10.3 %collective-permute-start.14 = (bf16[2,288,256]{2,1,0:T(8,128)(2,1)S(1)}, bf16[2,288,256]{2,1,0:T(8,128)(2,1)S(1)}, u32[]{:S(2)}, u32[]{:S(2)}) collective-permute-start(bf16[2,288,256]{2,1,0:T(8,128)(2,1)S(1)} %collective-permute-done.12.refs_11_), channel_id=1, source_target_pairs={{0,16},{1,9},{2,18},{3,11},{4,20},{5,13},{6,22},{7,15},{8,24},{9,1... | collective-permute-start | bytes 884744 | tf_op jit(solution)/shard_map/ppermute | solution.py:117
  53.6 10.2 %collective-permute-start.15 = (bf16[2,288,256]{2,1,0:T(8,128)(2,1)S(1)}, bf16[2,288,256]{2,1,0:T(8,128)(2,1)S(1)}, u32[]{:S(2)}, u32[]{:S(2)}) collective-permute-start(bf16[2,288,256]{2,1,0:T(8,128)(2,1)S(1)} %collective-permute-done.13.refs_12_), channel_id=1, source_target_pairs={{0,16},{1,9},{2,18},{3,11},{4,20},{5,13},{6,22},{7,15},{8,24},{9,1... | collective-permute-start | bytes 884744 | tf_op jit(solution)/shard_map/ppermute | solution.py:117
  59.7 18.3 %collective-permute-start.6 = (bf16[8,288,256]{2,1,0:T(8,128)(2,1)S(1)}, bf16[8,288,256]{2,1,0:T(8,128)(2,1)S(1)}, u32[]{:S(2)}, u32[]{:S(2)}) collective-permute-start(bf16[8,288,256]{2,1,0:T(8,128)(2,1)S(1)} %pad_maximum_fusion), channel_id=1, source_target_pairs={{0,1},{1,0},{2,3},{3,2},{4,5},{5,4},{6,7},{7,6},{8,9},{9,8},{10,11... | collective-permute-start | bytes 3538952 | tf_op jit(solution)/shard_map/ppermute | solution.py:120
  59.7 9.7 %collective-permute-start.19 = (bf16[2,288,256]{2,1,0:T(8,128)(2,1)S(1)}, bf16[2,288,256]{2,1,0:T(8,128)(2,1)S(1)}, u32[]{:S(2)}, u32[]{:S(2)}) collective-permute-start(bf16[2,288,256]{2,1,0:T(8,128)(2,1)S(1)} %collective-permute-done.17.refs_17_), channel_id=1, source_target_pairs={{0,16},{1,9},{2,18},{3,11},{4,20},{5,13},{6,22},{7,15},{8,24},{9,1... | collective-permute-start | bytes 884744 | tf_op jit(solution)/shard_map/ppermute | solution.py:117
  61.2 8.3 %collective-permute-start.18 = (bf16[2,288,256]{2,1,0:T(8,128)(2,1)S(1)}, bf16[2,288,256]{2,1,0:T(8,128)(2,1)S(1)}, u32[]{:S(2)}, u32[]{:S(2)}) collective-permute-start(bf16[2,288,256]{2,1,0:T(8,128)(2,1)S(1)} %collective-permute-done.17.refs_17_), channel_id=1, source_target_pairs={{0,8},{1,17},{2,10},{3,19},{4,12},{5,21},{6,14},{7,23},{8,0},{9,25... | collective-permute-start | bytes 884744 | tf_op jit(solution)/shard_map/ppermute | solution.py:117
  63.7 14.3 %collective-permute-start.11 = (bf16[8,288,256]{2,1,0:T(8,128)(2,1)S(1)}, bf16[8,288,256]{2,1,0:T(8,128)(2,1)S(1)}, u32[]{:S(2)}, u32[]{:S(2)}) collective-permute-start(bf16[8,288,256]{2,1,0:T(8,128)(2,1)S(1)} %pad_maximum_fusion.1), channel_id=1, source_target_pairs={{0,1},{1,0},{2,3},{3,2},{4,5},{5,4},{6,7},{7,6},{8,9},{9,8},{10,11... | collective-permute-start | bytes 3538952 | tf_op jit(solution)/shard_map/ppermute | solution.py:120
  64.0 14.1 %copy-start.2 = (bf16[760,384]{1,0:T(8,128)(2,1)S(1)}, bf16[760,384]{1,0:T(8,128)(2,1)}, u32[]{:S(2)}) copy-start(bf16[760,384]{1,0:T(8,128)(2,1)} %constant.15.clone.refs_26_) | copy-start | bytes 1751044
  64.0 14.1 %copy-start.3 = (f32[256]{0:T(256)S(1)}, f32[256]{0:T(256)}, u32[]{:S(2)}) copy-start(f32[256]{0:T(256)} %param.16) | copy-start | bytes 3076
  64.0 14.1 %copy-start.4 = (f32[256]{0:T(256)S(1)}, f32[256]{0:T(256)}, u32[]{:S(2)}) copy-start(f32[256]{0:T(256)} %param.17) | copy-start | bytes 3076
  64.0 14.1 %copy-start.5 = (f32[256]{0:T(256)S(1)}, f32[256]{0:T(256)}, u32[]{:S(2)}) copy-start(f32[256]{0:T(256)} %param.18) | copy-start | bytes 3076
  64.0 14.0 %collective-permute-start.16 = (bf16[8,288,256]{2,1,0:T(8,128)(2,1)S(1)}, bf16[8,288,256]{2,1,0:T(8,128)(2,1)S(1)}, u32[]{:S(2)}, u32[]{:S(2)}) collective-permute-start(bf16[8,288,256]{2,1,0:T(8,128)(2,1)S(1)} %pad_maximum_fusion.2), channel_id=1, source_target_pairs={{0,1},{1,0},{2,3},{3,2},{4,5},{5,4},{6,7},{7,6},{8,9},{9,8},{10,11... | collective-permute-start | bytes 3538952 | tf_op jit(solution)/shard_map/ppermute | solution.py:120
  69.5 8.5 %collective-permute-start.20 = (bf16[6,288,256]{2,1,0:T(8,128)(2,1)S(1)}, bf16[6,288,256]{2,1,0:T(8,128)(2,1)S(1)}, u32[]{:S(2)}, u32[]{:S(2)}) collective-permute-start(bf16[6,288,256]{2,1,0:T(8,128)(2,1)S(1)} %pad_maximum_fusion.3), channel_id=1, source_target_pairs={{0,1},{1,0},{2,3},{3,2},{4,5},{5,4},{6,7},{7,6},{8,9},{9,8},{10,11... | collective-permute-start | bytes 2654216 | tf_op jit(solution)/shard_map/ppermute | solution.py:120
  69.7 6.7 %collective-permute-start.21 = (bf16[2,288,256]{2,1,0:T(8,128)(2,1)S(1)}, bf16[2,288,256]{2,1,0:T(8,128)(2,1)S(1)}, u32[]{:S(2)}, u32[]{:S(2)}) collective-permute-start(bf16[2,288,256]{2,1,0:T(8,128)(2,1)S(1)} %collective-permute-done.18.refs_18_), channel_id=1, source_target_pairs={{0,16},{1,9},{2,18},{3,11},{4,20},{5,13},{6,22},{7,15},{8,24},{9,1... | collective-permute-start | bytes 884744 | tf_op jit(solution)/shard_map/ppermute | solution.py:117
  76.4 1.6 %collective-permute-start.22 = (bf16[2,288,256]{2,1,0:T(8,128)(2,1)S(1)}, bf16[2,288,256]{2,1,0:T(8,128)(2,1)S(1)}, u32[]{:S(2)}, u32[]{:S(2)}) collective-permute-start(bf16[2,288,256]{2,1,0:T(8,128)(2,1)S(1)} %collective-permute-done.21.refs_20_), channel_id=1, source_target_pairs={{0,1},{1,0},{2,3},{3,2},{4,5},{5,4},{6,7},{7,6},{8,9},{9,8},{10,11... | collective-permute-start | bytes 884744 | tf_op jit(solution)/shard_map/ppermute | solution.py:120
  (1 other events, 0.7 us)

commit v3 on v2

--- a/solution.py
+++ b/solution.py
@@ -66,8 +66,10 @@
     bits = learners.bit_length() - 1
     order = sorted(range(learners), key=lambda subset: (not subset & 1, -subset))
     held, terms = {}, []
-    for subsets in (order[:1], order[1:]):
-        held.update(zip(subsets, pick(gradients, subsets, bits)))
+    me, core = lax.axis_index("learn"), lax.axis_index("act") % 2
+    layer = me ^ jnp.where(core == 0, route_mask(0, order[0], bits), route_mask(1, order[0], bits))
+    held[order[0]] = lax.dynamic_index_in_dim(gradients, layer, 0, keepdims=False)
+    held.update(zip(order[1:], pick(gradients, order[1:], bits)))
     for step in range(bits):
         route = plane_route(learners, actors, step)
         for subset in sorted(held, reverse=True):
@@ -258,7 +260,7 @@
     points = BOARD * width
     channels = stem.shape[1]
     places = [labels for _, labels in found]
-    steps = [0, 7, 13, BOARD]
+    steps = [0, 5, 10, 15, BOARD]
     cuts = [(low * width, high * width) for low, high in zip(steps, steps[1:])]
     anywhere = pl.BlockSpec(memory_space=pl.ANY)
     inside = pl.BlockSpec(memory_space=pltpu.VMEM)

time: 91.4 us -> 90.4 us (0.989)
  waiting for transfers between devices: 41 us -> 39.3 us
  local copies, waits for them, and re-layouts: 3.87 us -> 4.97 us
    ppermute x3, waiting for transfers between devices: 9.2 us -> 7.57 us  [reduce_gradients(): came = lax.ppermute(held.pop(subset), AXES, route)]
    squeeze x0 -> x1, local copies, waits for them, and re-layouts: none -> 1.11 us  [reduce_gradients(): lax.dynamic_index_in_dim(gradients, layer, 0, keepdims=False)]
where the time goes in v3:
time: 90.4 us; the launch traced here: 90.2 us
  waiting for transfers between devices  39.3 us (43%)
  starting transfers between devices  24.7 us (27%)
  Pallas kernels  14.8 us (16%)
  local copies, waits for them, and re-layouts  4.97 us (5%)
  matrix products  3.73 us (4%)
  other arithmetic  1.59 us (2%)
  between operations  1.11 us (1%)
    ppermute x11, waiting for transfers between devices, along_plane(): return lax.ppermute(block, AXES, plane_route(learners, actors, step))  18.5 us
    pallas_call x1, Pallas kernels, run_tower(): pl.pallas_call(functools.partial(tower, places, layers, rows, number, wid...  12.7 us
    ppermute x11, starting transfers between devices, along_plane(): return lax.ppermute(block, AXES, plane_route(learners, actors, step))  12.6 us
    ppermute x4, waiting for transfers between devices, along_z(): lax.ppermute(block, AXES, pairs(learners, actors, lambda l, a: (l, a ^ 2...  11.7 us
    ppermute x3, waiting for transfers between devices, reduce_gradients(): came = lax.ppermute(held.pop(subset), AXES, route)  7.57 us
    ppermute x4, starting transfers between devices, along_z(): lax.ppermute(block, AXES, pairs(learners, actors, lambda l, a: (l, a ^ 2...  6.19 us
    ppermute x3, starting transfers between devices, reduce_gradients(): came = lax.ppermute(held.pop(subset), AXES, route)  5.13 us
    conv_general_dilated x1, matrix products, stem_stream(): lax.conv_general_dilated(field, kernel, (1, 1), ((1, 1), (1, 1)), dimensi...  3.73 us
  transfers between devices with their start and end apart: 23, of which 11 were waited for; matrix products, arithmetic and copies ran while one was open for 8% of the time, Pallas kernels for 1%

profile of v3, /device:TPU:0, one launch (start us, length us, event | category | flops | bytes accessed | tf_op | source)
XLA Modules:
  0.0 90.2 jit_solution(3097870379441873638)
XLA Ops:
  0.6 1.1 %dynamic-slice_bitcast_fusion = f32[2,288,256]{2,1,0:T(8,128)S(1)} fusion(f32[1,4,2,288,256]{4,3,2,1,0:T(8,128)} %param.14, s32[]{:T(128)S(6)} %select_n.11), kind=kLoop, calls=%fused_computation.4 | loop fusion | bytes 1179652 | tf_op jit(solution)/shard_map/jit(dynamic_index_in_dim)/squeeze | solution.py:71
  1.7 3.0 %collective-permute-start.1 = (f32[2,288,256]{2,1,0:T(8,128)S(1)}, f32[2,288,256]{2,1,0:T(8,128)S(1)}, u32[]{:S(2)}, u32[]{:S(2)}) collective-permute-start(f32[2,288,256]{2,1,0:T(8,128)S(1)} %dynamic-slice_bitcast_fusion), channel_id=1, source_target_pairs={{0,8},{1,17},{2,10},{3,19},{4,12},{5,21},{6,14},{7,23},{8,0},{9,25... | collective-permute-start | bytes 1769480 | tf_op jit(solution)/shard_map/ppermute | solution.py:78
  4.8 1.7 %copy-done = f32[1,4,2,288,256]{4,3,2,1,0:T(8,128)S(1)} copy-done((f32[1,4,2,288,256]{4,3,2,1,0:T(8,128)S(1)}, f32[1,4,2,288,256]{4,3,2,1,0:T(8,128)}, u32[]{:S(2)}) %copy-start) | copy-done | bytes 2359320
  6.4 1.2 %pick.1 = (f32[2,288,256]{2,1,0:T(8,128)}, f32[2,288,256]{2,1,0:T(8,128)S(1)}, f32[2,288,256]{2,1,0:T(8,128)S(1)}) custom-call(f32[4,2,288,256]{3,2,1,0:T(8,128)S(1)} %bitcast.26), custom_call_target="tpu_custom_call" | custom-call | tf_op jit(solution)/shard_map/pick/pallas_call | solution.py:54
  8.2 4.4 %collective-permute-done.1 = f32[2,288,256]{2,1,0:T(8,128)S(1)} collective-permute-done((f32[2,288,256]{2,1,0:T(8,128)S(1)}, f32[2,288,256]{2,1,0:T(8,128)S(1)}, u32[]{:S(2)}, u32[]{:S(2)}) %collective-permute-start.1) | collective-permute-done | bytes 589856 | tf_op jit(solution)/shard_map/ppermute | solution.py:78
  12.6 0.9 add.17
  13.5 2.0 %collective-permute-start.2 = (f32[2,288,256]{2,1,0:T(8,128)}, f32[2,288,256]{2,1,0:T(8,128)S(1)}, u32[]{:S(2)}, u32[]{:S(2)}) collective-permute-start(f32[2,288,256]{2,1,0:T(8,128)} %add.17), channel_id=1, source_target_pairs={{0,16},{1,9},{2,18},{3,11},{4,20},{5,13},{6,22},{7,15},{8,24},{9,1... | collective-permute-start | bytes 1769480 | tf_op jit(solution)/shard_map/ppermute | solution.py:78
  15.8 0.8 copy.21
  16.6 3.7 %fusion.3 = f32[1,19,40,256]{3,0,2,1:T(1,128)S(1)} fusion(bf16[1,19,40,4]{3,0,2,1:T(2,128)(2,1)S(1)} %copy.21, bf16[3,3,4,256]{3,2,1,0:T(4,128)(2,1)S(1)} %reshape.52), kind=kOutput, calls=%fused_computation.18 | convolution fusion | flops 13291520 | bytes 802752 | tf_op jit(solution)/shard_map/conv_general_dilated | solution.py:300
  21.3 0.9 collective-permute-done.refs_1_
  22.2 2.2 %collective-permute-done.2.refs_2_ = f32[2,288,256]{2,1,0:T(8,128)S(1)} collective-permute-done((f32[2,288,256]{2,1,0:T(8,128)}, f32[2,288,256]{2,1,0:T(8,128)S(1)}, u32[]{:S(2)}, u32[]{:S(2)}) %collective-permute-start.2) | collective-permute-done | bytes 589856 | tf_op jit(solution)/shard_map/ppermute | solution.py:78
  24.4 0.9 %update.1 = (f32[2,288,256]{2,1,0:T(8,128)}, bf16[2,288,256]{2,1,0:T(8,128)(2,1)S(1)}) custom-call(f32[2,288,256]{2,1,0:T(8,128)S(1)} %get-tuple-element.18.refs_0_, f32[2,288,256]{2,1,0:T(8,128)S(1)} %collective-permute-done.refs_1_, f32[2,288,256]{2,1,0:T(8,128)S(1)} %collective-permute-done.2.refs_2_, f32[2,288,256]{2,1,0:T(8,128)S(1)} %bitcast.28), custom_call_target="tpu_custom_call" | custom-call | tf_op jit(solution)/shard_map/update/pallas_call | solution.py:98
  25.4 1.7 %collective-permute-start.3 = (bf16[2,288,256]{2,1,0:T(8,128)(2,1)S(1)}, bf16[2,288,256]{2,1,0:T(8,128)(2,1)S(1)}, u32[]{:S(2)}, u32[]{:S(2)}) collective-permute-start(bf16[2,288,256]{2,1,0:T(8,128)(2,1)S(1)} %get-tuple-element.22.refs_1_), channel_id=1, source_target_pairs={{0,8},{1,17},{2,10},{3,19},{4,12},{5,21},{6,14},{7,23},{8,0},{9,25... | collective-permute-start | bytes 884744 | tf_op jit(solution)/shard_map/ppermute | solution.py:119
  27.1 1.6 %collective-permute-start.7 = (bf16[2,288,256]{2,1,0:T(8,128)(2,1)S(1)}, bf16[2,288,256]{2,1,0:T(8,128)(2,1)S(1)}, u32[]{:S(2)}, u32[]{:S(2)}) collective-permute-start(bf16[2,288,256]{2,1,0:T(8,128)(2,1)S(1)} %get-tuple-element.22.refs_1_), channel_id=1, source_target_pairs={{0,2},{1,3},{2,0},{3,1},{4,6},{5,7},{6,4},{7,5},{8,10},{9,11},{10,... | collective-permute-start | bytes 884744 | tf_op jit(solution)/shard_map/ppermute | solution.py:116
  28.6 2.6 %collective-permute-start.12 = (bf16[2,288,256]{2,1,0:T(8,128)(2,1)S(1)}, bf16[2,288,256]{2,1,0:T(8,128)(2,1)S(1)}, u32[]{:S(2)}, u32[]{:S(2)}) collective-permute-start(bf16[2,288,256]{2,1,0:T(8,128)(2,1)S(1)} %get-tuple-element.22.refs_1_), channel_id=1, source_target_pairs={{0,4},{1,5},{2,6},{3,7},{4,0},{5,1},{6,2},{7,3},{8,12},{9,13},{10,... | collective-permute-start | bytes 884744 | tf_op jit(solution)/shard_map/ppermute | solution.py:116
  31.2 1.5 %collective-permute-start.4 = (bf16[2,288,256]{2,1,0:T(8,128)(2,1)S(1)}, bf16[2,288,256]{2,1,0:T(8,128)(2,1)S(1)}, u32[]{:S(2)}, u32[]{:S(2)}) collective-permute-start(bf16[2,288,256]{2,1,0:T(8,128)(2,1)S(1)} %get-tuple-element.22.refs_1_), channel_id=1, source_target_pairs={{0,16},{1,9},{2,18},{3,11},{4,20},{5,13},{6,22},{7,15},{8,24},{9,1... | collective-permute-start | bytes 884744 | tf_op jit(solution)/shard_map/ppermute | solution.py:119
  32.8 1.1 %collective-permute-start.5 = (bf16[2,288,256]{2,1,0:T(8,128)(2,1)S(1)}, bf16[2,288,256]{2,1,0:T(8,128)(2,1)S(1)}, u32[]{:S(2)}, u32[]{:S(2)}) collective-permute-start(bf16[2,288,256]{2,1,0:T(8,128)(2,1)S(1)} %collective-permute-done.3.refs_2_), channel_id=1, source_target_pairs={{0,16},{1,9},{2,18},{3,11},{4,20},{5,13},{6,22},{7,15},{8,24},{9,1... | collective-permute-start | bytes 884744 | tf_op jit(solution)/shard_map/ppermute | solution.py:119
  33.8 9.1 %collective-permute-done.7.refs_6_ = bf16[2,288,256]{2,1,0:T(8,128)(2,1)S(1)} collective-permute-done((bf16[2,288,256]{2,1,0:T(8,128)(2,1)S(1)}, bf16[2,288,256]{2,1,0:T(8,128)(2,1)S(1)}, u32[]{:S(2)}, u32[]{:S(2)}) %collective-permute-start.7) | collective-permute-done | bytes 294944 | tf_op jit(solution)/shard_map/ppermute | solution.py:116
  43.2 2.0 %collective-permute-done.12.refs_11_ = bf16[2,288,256]{2,1,0:T(8,128)(2,1)S(1)} collective-permute-done((bf16[2,288,256]{2,1,0:T(8,128)(2,1)S(1)}, bf16[2,288,256]{2,1,0:T(8,128)(2,1)S(1)}, u32[]{:S(2)}, u32[]{:S(2)}) %collective-permute-start.12) | collective-permute-done | bytes 294944 | tf_op jit(solution)/shard_map/ppermute | solution.py:116
  45.3 0.7 collective-permute-start.13
  46.0 1.3 %collective-permute-start.8 = (bf16[2,288,256]{2,1,0:T(8,128)(2,1)S(1)}, bf16[2,288,256]{2,1,0:T(8,128)(2,1)S(1)}, u32[]{:S(2)}, u32[]{:S(2)}) collective-permute-start(bf16[2,288,256]{2,1,0:T(8,128)(2,1)S(1)} %collective-permute-done.7.refs_6_), channel_id=1, source_target_pairs={{0,8},{1,17},{2,10},{3,19},{4,12},{5,21},{6,14},{7,23},{8,0},{9,25... | collective-permute-start | bytes 884744 | tf_op jit(solution)/shard_map/ppermute | solution.py:119
  47.7 1.6 %collective-permute-start.10 = (bf16[2,288,256]{2,1,0:T(8,128)(2,1)S(1)}, bf16[2,288,256]{2,1,0:T(8,128)(2,1)S(1)}, u32[]{:S(2)}, u32[]{:S(2)}) collective-permute-start(bf16[2,288,256]{2,1,0:T(8,128)(2,1)S(1)} %collective-permute-done.5.refs_4_), channel_id=1, source_target_pairs={{0,2},{1,3},{2,0},{3,1},{4,6},{5,7},{6,4},{7,5},{8,10},{9,11},{10,... | collective-permute-start | bytes 884744 | tf_op jit(solution)/shard_map/ppermute | solution.py:116
  49.3 3.4 %collective-permute-done.9.refs_8_ = bf16[2,288,256]{2,1,0:T(8,128)(2,1)S(1)} collective-permute-done((bf16[2,288,256]{2,1,0:T(8,128)(2,1)S(1)}, bf16[2,288,256]{2,1,0:T(8,128)(2,1)S(1)}, u32[]{:S(2)}, u32[]{:S(2)}) %collective-permute-start.9) | collective-permute-done | bytes 294944 | tf_op jit(solution)/shard_map/ppermute | solution.py:119
  52.9 1.9 %collective-permute-start.15 = (bf16[2,288,256]{2,1,0:T(8,128)(2,1)S(1)}, bf16[2,288,256]{2,1,0:T(8,128)(2,1)S(1)}, u32[]{:S(2)}, u32[]{:S(2)}) collective-permute-start(bf16[2,288,256]{2,1,0:T(8,128)(2,1)S(1)} %collective-permute-done.13.refs_12_), channel_id=1, source_target_pairs={{0,16},{1,9},{2,18},{3,11},{4,20},{5,13},{6,22},{7,15},{8,24},{9,1... | collective-permute-start | bytes 884744 | tf_op jit(solution)/shard_map/ppermute | solution.py:119
  54.9 4.1 %collective-permute-done.8.refs_7_ = bf16[2,288,256]{2,1,0:T(8,128)(2,1)S(1)} collective-permute-done((bf16[2,288,256]{2,1,0:T(8,128)(2,1)S(1)}, bf16[2,288,256]{2,1,0:T(8,128)(2,1)S(1)}, u32[]{:S(2)}, u32[]{:S(2)}) %collective-permute-start.8) | collective-permute-done | bytes 294944 | tf_op jit(solution)/shard_map/ppermute | solution.py:119
  59.0 0.8 collective-permute-start.19
  60.5 2.4 %collective-permute-start.18 = (bf16[2,288,256]{2,1,0:T(8,128)(2,1)S(1)}, bf16[2,288,256]{2,1,0:T(8,128)(2,1)S(1)}, u32[]{:S(2)}, u32[]{:S(2)}) collective-permute-start(bf16[2,288,256]{2,1,0:T(8,128)(2,1)S(1)} %collective-permute-done.17.refs_17_), channel_id=1, source_target_pairs={{0,8},{1,17},{2,10},{3,19},{4,12},{5,21},{6,14},{7,23},{8,0},{9,25... | collective-permute-start | bytes 884744 | tf_op jit(solution)/shard_map/ppermute | solution.py:119
  63.9 4.9 %collective-permute-done.19.refs_19_ = bf16[2,288,256]{2,1,0:T(8,128)(2,1)S(1)} collective-permute-done((bf16[2,288,256]{2,1,0:T(8,128)(2,1)S(1)}, bf16[2,288,256]{2,1,0:T(8,128)(2,1)S(1)}, u32[]{:S(2)}, u32[]{:S(2)}) %collective-permute-start.19) | collective-permute-done | bytes 294944 | tf_op jit(solution)/shard_map/ppermute | solution.py:119
  69.0 0.7 collective-permute-start.21
  69.7 6.0 %collective-permute-done.21.refs_20_ = bf16[2,288,256]{2,1,0:T(8,128)(2,1)S(1)} collective-permute-done((bf16[2,288,256]{2,1,0:T(8,128)(2,1)S(1)}, bf16[2,288,256]{2,1,0:T(8,128)(2,1)S(1)}, u32[]{:S(2)}, u32[]{:S(2)}) %collective-permute-start.21) | collective-permute-done | bytes 294944 | tf_op jit(solution)/shard_map/ppermute | solution.py:119
  75.7 1.6 %collective-permute-done.22.refs_16_ = bf16[2,288,256]{2,1,0:T(8,128)(2,1)S(1)} collective-permute-done((bf16[2,288,256]{2,1,0:T(8,128)(2,1)S(1)}, bf16[2,288,256]{2,1,0:T(8,128)(2,1)S(1)}, u32[]{:S(2)}, u32[]{:S(2)}) %collective-permute-start.22) | collective-permute-done | bytes 294944 | tf_op jit(solution)/shard_map/ppermute | solution.py:122
  77.4 12.7 %tower.1 = (f32[2,1,362]{2,1,0:T(1,128)}, f32[1,2]{1,0:T(1,128)}) custom-call(bf16[8,288,256]{2,1,0:T(8,128)(2,1)S(1)} %collective-permute-done.6.refs_0_, bf16[2,288,256]{2,1,0:T(8,128)(2,1)S(1)} %get-tuple-element.22.refs_1_, bf16[2,288,256]{2,1,0:T(8,128)(2,1)S(1)} %collective-permute-done.3.refs_2_, ...), custom_call_target="tpu_custom_call" | custom-call | tf_op jit(solution)/shard_map/tower/pallas_call | solution.py:267
  (70 shorter events, 4.6 us)
Async XLA Ops:
  1.7 10.9 %collective-permute-start.1 = (f32[2,288,256]{2,1,0:T(8,128)S(1)}, f32[2,288,256]{2,1,0:T(8,128)S(1)}, u32[]{:S(2)}, u32[]{:S(2)}) collective-permute-start(f32[2,288,256]{2,1,0:T(8,128)S(1)} %dynamic-slice_bitcast_fusion), channel_id=1, source_target_pairs={{0,8},{1,17},{2,10},{3,19},{4,12},{5,21},{6,14},{7,23},{8,0},{9,25... | collective-permute-start | bytes 1769480 | tf_op jit(solution)/shard_map/ppermute | solution.py:78
  4.8 1.7 %copy-start = (f32[1,4,2,288,256]{4,3,2,1,0:T(8,128)S(1)}, f32[1,4,2,288,256]{4,3,2,1,0:T(8,128)}, u32[]{:S(2)}) copy-start(f32[1,4,2,288,256]{4,3,2,1,0:T(8,128)} %param.14) | copy-start | bytes 7077892
  6.4 1.4 %copy-start.7 = (s32[2,1,361]{2,1,0:T(1,128)S(1)}, s32[2,1,361]{2,1,0:T(1,128)}, u32[]{:S(2)}) copy-start(s32[2,1,361]{2,1,0:T(1,128)} %param.10) | copy-start | bytes 8668
  6.4 1.5 %copy-start.9 = (s32[2,1]{0,1:T(1,128)S(1)}, s32[2,1]{0,1:T(1,128)}, u32[]{:S(2)}) copy-start(s32[2,1]{0,1:T(1,128)} %param.11) | copy-start | bytes 28
  7.6 14.6 %collective-permute-start = (f32[2,288,256]{2,1,0:T(8,128)}, f32[2,288,256]{2,1,0:T(8,128)S(1)}, u32[]{:S(2)}, u32[]{:S(2)}) collective-permute-start(f32[2,288,256]{2,1,0:T(8,128)} %get-tuple-element.16), channel_id=1, source_target_pairs={{0,8},{1,17},{2,10},{3,19},{4,12},{5,21},{6,14},{7,23},{8,0},{9,25... | collective-permute-start | bytes 1769480 | tf_op jit(solution)/shard_map/ppermute | solution.py:78
  12.6 4.0 %copy-start.6 = (bf16[36,256]{1,0:T(8,128)(2,1)S(1)}, bf16[36,256]{1,0:T(8,128)(2,1)}, u32[]{:S(2)}) copy-start(bf16[36,256]{1,0:T(8,128)(2,1)} %param.15) | copy-start | bytes 55300
  13.5 10.9 %collective-permute-start.2 = (f32[2,288,256]{2,1,0:T(8,128)}, f32[2,288,256]{2,1,0:T(8,128)S(1)}, u32[]{:S(2)}, u32[]{:S(2)}) collective-permute-start(f32[2,288,256]{2,1,0:T(8,128)} %add.17), channel_id=1, source_target_pairs={{0,16},{1,9},{2,18},{3,11},{4,20},{5,13},{6,22},{7,15},{8,24},{9,1... | collective-permute-start | bytes 1769480 | tf_op jit(solution)/shard_map/ppermute | solution.py:78
  20.4 4.1 %copy-start.1 = (f32[1,2,288,256]{3,2,1,0:T(8,128)S(1)}, f32[1,2,288,256]{3,2,1,0:T(8,128)}, u32[]{:S(2)}) copy-start(f32[1,2,288,256]{3,2,1,0:T(8,128)} %param.13) | copy-start | bytes 1769476
  25.4 7.4 %collective-permute-start.3 = (bf16[2,288,256]{2,1,0:T(8,128)(2,1)S(1)}, bf16[2,288,256]{2,1,0:T(8,128)(2,1)S(1)}, u32[]{:S(2)}, u32[]{:S(2)}) collective-permute-start(bf16[2,288,256]{2,1,0:T(8,128)(2,1)S(1)} %get-tuple-element.22.refs_1_), channel_id=1, source_target_pairs={{0,8},{1,17},{2,10},{3,19},{4,12},{5,21},{6,14},{7,23},{8,0},{9,25... | collective-permute-start | bytes 884744 | tf_op jit(solution)/shard_map/ppermute | solution.py:119
  27.1 15.8 %collective-permute-start.7 = (bf16[2,288,256]{2,1,0:T(8,128)(2,1)S(1)}, bf16[2,288,256]{2,1,0:T(8,128)(2,1)S(1)}, u32[]{:S(2)}, u32[]{:S(2)}) collective-permute-start(bf16[2,288,256]{2,1,0:T(8,128)(2,1)S(1)} %get-tuple-element.22.refs_1_), channel_id=1, source_target_pairs={{0,2},{1,3},{2,0},{3,1},{4,6},{5,7},{6,4},{7,5},{8,10},{9,11},{10,... | collective-permute-start | bytes 884744 | tf_op jit(solution)/shard_map/ppermute | solution.py:116
  28.6 16.6 %collective-permute-start.12 = (bf16[2,288,256]{2,1,0:T(8,128)(2,1)S(1)}, bf16[2,288,256]{2,1,0:T(8,128)(2,1)S(1)}, u32[]{:S(2)}, u32[]{:S(2)}) collective-permute-start(bf16[2,288,256]{2,1,0:T(8,128)(2,1)S(1)} %get-tuple-element.22.refs_1_), channel_id=1, source_target_pairs={{0,4},{1,5},{2,6},{3,7},{4,0},{5,1},{6,2},{7,3},{8,12},{9,13},{10,... | collective-permute-start | bytes 884744 | tf_op jit(solution)/shard_map/ppermute | solution.py:116
  31.2 16.1 %collective-permute-start.4 = (bf16[2,288,256]{2,1,0:T(8,128)(2,1)S(1)}, bf16[2,288,256]{2,1,0:T(8,128)(2,1)S(1)}, u32[]{:S(2)}, u32[]{:S(2)}) collective-permute-start(bf16[2,288,256]{2,1,0:T(8,128)(2,1)S(1)} %get-tuple-element.22.refs_1_), channel_id=1, source_target_pairs={{0,16},{1,9},{2,18},{3,11},{4,20},{5,13},{6,22},{7,15},{8,24},{9,1... | collective-permute-start | bytes 884744 | tf_op jit(solution)/shard_map/ppermute | solution.py:119
  32.8 15.0 %collective-permute-start.5 = (bf16[2,288,256]{2,1,0:T(8,128)(2,1)S(1)}, bf16[2,288,256]{2,1,0:T(8,128)(2,1)S(1)}, u32[]{:S(2)}, u32[]{:S(2)}) collective-permute-start(bf16[2,288,256]{2,1,0:T(8,128)(2,1)S(1)} %collective-permute-done.3.refs_2_), channel_id=1, source_target_pairs={{0,16},{1,9},{2,18},{3,11},{4,20},{5,13},{6,22},{7,15},{8,24},{9,1... | collective-permute-start | bytes 884744 | tf_op jit(solution)/shard_map/ppermute | solution.py:119
  42.9 9.9 %collective-permute-start.9 = (bf16[2,288,256]{2,1,0:T(8,128)(2,1)S(1)}, bf16[2,288,256]{2,1,0:T(8,128)(2,1)S(1)}, u32[]{:S(2)}, u32[]{:S(2)}) collective-permute-start(bf16[2,288,256]{2,1,0:T(8,128)(2,1)S(1)} %collective-permute-done.7.refs_6_), channel_id=1, source_target_pairs={{0,16},{1,9},{2,18},{3,11},{4,20},{5,13},{6,22},{7,15},{8,24},{9,1... | collective-permute-start | bytes 884744 | tf_op jit(solution)/shard_map/ppermute | solution.py:119
  45.3 7.6 %collective-permute-start.13 = (bf16[2,288,256]{2,1,0:T(8,128)(2,1)S(1)}, bf16[2,288,256]{2,1,0:T(8,128)(2,1)S(1)}, u32[]{:S(2)}, u32[]{:S(2)}) collective-permute-start(bf16[2,288,256]{2,1,0:T(8,128)(2,1)S(1)} %collective-permute-done.12.refs_11_), channel_id=1, source_target_pairs={{0,8},{1,17},{2,10},{3,19},{4,12},{5,21},{6,14},{7,23},{8,0},{9,25... | collective-permute-start | bytes 884744 | tf_op jit(solution)/shard_map/ppermute | solution.py:119
  46.0 13.0 %collective-permute-start.8 = (bf16[2,288,256]{2,1,0:T(8,128)(2,1)S(1)}, bf16[2,288,256]{2,1,0:T(8,128)(2,1)S(1)}, u32[]{:S(2)}, u32[]{:S(2)}) collective-permute-start(bf16[2,288,256]{2,1,0:T(8,128)(2,1)S(1)} %collective-permute-done.7.refs_6_), channel_id=1, source_target_pairs={{0,8},{1,17},{2,10},{3,19},{4,12},{5,21},{6,14},{7,23},{8,0},{9,25... | collective-permute-start | bytes 884744 | tf_op jit(solution)/shard_map/ppermute | solution.py:119
  47.3 11.7 %collective-permute-start.17 = (bf16[2,288,256]{2,1,0:T(8,128)(2,1)S(1)}, bf16[2,288,256]{2,1,0:T(8,128)(2,1)S(1)}, u32[]{:S(2)}, u32[]{:S(2)}) collective-permute-start(bf16[2,288,256]{2,1,0:T(8,128)(2,1)S(1)} %collective-permute-done.12.refs_11_), channel_id=1, source_target_pairs={{0,2},{1,3},{2,0},{3,1},{4,6},{5,7},{6,4},{7,5},{8,10},{9,11},{10,... | collective-permute-start | bytes 884744 | tf_op jit(solution)/shard_map/ppermute | solution.py:116
  47.7 12.7 %collective-permute-start.10 = (bf16[2,288,256]{2,1,0:T(8,128)(2,1)S(1)}, bf16[2,288,256]{2,1,0:T(8,128)(2,1)S(1)}, u32[]{:S(2)}, u32[]{:S(2)}) collective-permute-start(bf16[2,288,256]{2,1,0:T(8,128)(2,1)S(1)} %collective-permute-done.5.refs_4_), channel_id=1, source_target_pairs={{0,2},{1,3},{2,0},{3,1},{4,6},{5,7},{6,4},{7,5},{8,10},{9,11},{10,... | collective-permute-start | bytes 884744 | tf_op jit(solution)/shard_map/ppermute | solution.py:116
  52.7 10.3 %collective-permute-start.14 = (bf16[2,288,256]{2,1,0:T(8,128)(2,1)S(1)}, bf16[2,288,256]{2,1,0:T(8,128)(2,1)S(1)}, u32[]{:S(2)}, u32[]{:S(2)}) collective-permute-start(bf16[2,288,256]{2,1,0:T(8,128)(2,1)S(1)} %collective-permute-done.12.refs_11_), channel_id=1, source_target_pairs={{0,16},{1,9},{2,18},{3,11},{4,20},{5,13},{6,22},{7,15},{8,24},{9,1... | collective-permute-start | bytes 884744 | tf_op jit(solution)/shard_map/ppermute | solution.py:119
  52.9 10.2 %collective-permute-start.15 = (bf16[2,288,256]{2,1,0:T(8,128)(2,1)S(1)}, bf16[2,288,256]{2,1,0:T(8,128)(2,1)S(1)}, u32[]{:S(2)}, u32[]{:S(2)}) collective-permute-start(bf16[2,288,256]{2,1,0:T(8,128)(2,1)S(1)} %collective-permute-done.13.refs_12_), channel_id=1, source_target_pairs={{0,16},{1,9},{2,18},{3,11},{4,20},{5,13},{6,22},{7,15},{8,24},{9,1... | collective-permute-start | bytes 884744 | tf_op jit(solution)/shard_map/ppermute | solution.py:119
  59.0 18.3 %collective-permute-start.6 = (bf16[8,288,256]{2,1,0:T(8,128)(2,1)S(1)}, bf16[8,288,256]{2,1,0:T(8,128)(2,1)S(1)}, u32[]{:S(2)}, u32[]{:S(2)}) collective-permute-start(bf16[8,288,256]{2,1,0:T(8,128)(2,1)S(1)} %pad_maximum_fusion), channel_id=1, source_target_pairs={{0,1},{1,0},{2,3},{3,2},{4,5},{5,4},{6,7},{7,6},{8,9},{9,8},{10,11... | collective-permute-start | bytes 3538952 | tf_op jit(solution)/shard_map/ppermute | solution.py:122
  59.0 9.7 %collective-permute-start.19 = (bf16[2,288,256]{2,1,0:T(8,128)(2,1)S(1)}, bf16[2,288,256]{2,1,0:T(8,128)(2,1)S(1)}, u32[]{:S(2)}, u32[]{:S(2)}) collective-permute-start(bf16[2,288,256]{2,1,0:T(8,128)(2,1)S(1)} %collective-permute-done.17.refs_17_), channel_id=1, source_target_pairs={{0,16},{1,9},{2,18},{3,11},{4,20},{5,13},{6,22},{7,15},{8,24},{9,1... | collective-permute-start | bytes 884744 | tf_op jit(solution)/shard_map/ppermute | solution.py:119
  60.5 8.3 %collective-permute-start.18 = (bf16[2,288,256]{2,1,0:T(8,128)(2,1)S(1)}, bf16[2,288,256]{2,1,0:T(8,128)(2,1)S(1)}, u32[]{:S(2)}, u32[]{:S(2)}) collective-permute-start(bf16[2,288,256]{2,1,0:T(8,128)(2,1)S(1)} %collective-permute-done.17.refs_17_), channel_id=1, source_target_pairs={{0,8},{1,17},{2,10},{3,19},{4,12},{5,21},{6,14},{7,23},{8,0},{9,25... | collective-permute-start | bytes 884744 | tf_op jit(solution)/shard_map/ppermute | solution.py:119
  63.0 14.3 %collective-permute-start.11 = (bf16[8,288,256]{2,1,0:T(8,128)(2,1)S(1)}, bf16[8,288,256]{2,1,0:T(8,128)(2,1)S(1)}, u32[]{:S(2)}, u32[]{:S(2)}) collective-permute-start(bf16[8,288,256]{2,1,0:T(8,128)(2,1)S(1)} %pad_maximum_fusion.1), channel_id=1, source_target_pairs={{0,1},{1,0},{2,3},{3,2},{4,5},{5,4},{6,7},{7,6},{8,9},{9,8},{10,11... | collective-permute-start | bytes 3538952 | tf_op jit(solution)/shard_map/ppermute | solution.py:122
  63.3 14.1 %copy-start.2 = (bf16[760,384]{1,0:T(8,128)(2,1)S(1)}, bf16[760,384]{1,0:T(8,128)(2,1)}, u32[]{:S(2)}) copy-start(bf16[760,384]{1,0:T(8,128)(2,1)} %constant.36.clone.refs_26_) | copy-start | bytes 1751044
  63.3 14.1 %copy-start.3 = (f32[256]{0:T(256)S(1)}, f32[256]{0:T(256)}, u32[]{:S(2)}) copy-start(f32[256]{0:T(256)} %param.16) | copy-start | bytes 3076
  63.3 14.1 %copy-start.4 = (f32[256]{0:T(256)S(1)}, f32[256]{0:T(256)}, u32[]{:S(2)}) copy-start(f32[256]{0:T(256)} %param.17) | copy-start | bytes 3076
  63.3 14.1 %copy-start.5 = (f32[256]{0:T(256)S(1)}, f32[256]{0:T(256)}, u32[]{:S(2)}) copy-start(f32[256]{0:T(256)} %param.18) | copy-start | bytes 3076
  63.3 14.0 %collective-permute-start.16 = (bf16[8,288,256]{2,1,0:T(8,128)(2,1)S(1)}, bf16[8,288,256]{2,1,0:T(8,128)(2,1)S(1)}, u32[]{:S(2)}, u32[]{:S(2)}) collective-permute-start(bf16[8,288,256]{2,1,0:T(8,128)(2,1)S(1)} %pad_maximum_fusion.2), channel_id=1, source_target_pairs={{0,1},{1,0},{2,3},{3,2},{4,5},{5,4},{6,7},{7,6},{8,9},{9,8},{10,11... | collective-permute-start | bytes 3538952 | tf_op jit(solution)/shard_map/ppermute | solution.py:122
  68.8 8.5 %collective-permute-start.20 = (bf16[6,288,256]{2,1,0:T(8,128)(2,1)S(1)}, bf16[6,288,256]{2,1,0:T(8,128)(2,1)S(1)}, u32[]{:S(2)}, u32[]{:S(2)}) collective-permute-start(bf16[6,288,256]{2,1,0:T(8,128)(2,1)S(1)} %pad_maximum_fusion.3), channel_id=1, source_target_pairs={{0,1},{1,0},{2,3},{3,2},{4,5},{5,4},{6,7},{7,6},{8,9},{9,8},{10,11... | collective-permute-start | bytes 2654216 | tf_op jit(solution)/shard_map/ppermute | solution.py:122
  69.0 6.7 %collective-permute-start.21 = (bf16[2,288,256]{2,1,0:T(8,128)(2,1)S(1)}, bf16[2,288,256]{2,1,0:T(8,128)(2,1)S(1)}, u32[]{:S(2)}, u32[]{:S(2)}) collective-permute-start(bf16[2,288,256]{2,1,0:T(8,128)(2,1)S(1)} %collective-permute-done.18.refs_18_), channel_id=1, source_target_pairs={{0,16},{1,9},{2,18},{3,11},{4,20},{5,13},{6,22},{7,15},{8,24},{9,1... | collective-permute-start | bytes 884744 | tf_op jit(solution)/shard_map/ppermute | solution.py:119
  75.7 1.6 %collective-permute-start.22 = (bf16[2,288,256]{2,1,0:T(8,128)(2,1)S(1)}, bf16[2,288,256]{2,1,0:T(8,128)(2,1)S(1)}, u32[]{:S(2)}, u32[]{:S(2)}) collective-permute-start(bf16[2,288,256]{2,1,0:T(8,128)(2,1)S(1)} %collective-permute-done.21.refs_20_), channel_id=1, source_target_pairs={{0,1},{1,0},{2,3},{3,2},{4,5},{5,4},{6,7},{7,6},{8,9},{9,8},{10,11... | collective-permute-start | bytes 884744 | tf_op jit(solution)/shard_map/ppermute | solution.py:122
  (1 other events, 0.7 us)

commit v4 on v3

--- a/solution.py
+++ b/solution.py
@@ -159,7 +159,7 @@
 def tower(places, layers, rows, number, width, cuts, *refs):
     blocks = refs[: len(places)]
     stem, legal, policy, passing, valuing, places_of_points, logp, worth = refs[len(places) : len(places) + 8]
-    weights, field, stream, mask, arrived = refs[len(places) + 8 :]
+    weights, field, stream, mask, of_board, arrived = refs[len(places) + 8 :]
     points = BOARD * width
     for labels, block in zip(places, blocks):
         if labels is None:
@@ -178,6 +178,8 @@
     column = lax.rem(lax.broadcasted_iota(jnp.int32, mask.shape, 0), width)
     on_board = (lax.rem(column, PITCH) < BOARD) & (column < PITCH * number)
     mask[...] = jnp.where(on_board, 1.0, 0.0)
+    for board in range(number):
+        of_board[board] = jnp.where((column >= board * PITCH) & (column < (board + 1) * PITCH), 1.0, 0.0)
 
     def rectified(low, high, values):
         keep = mask[low:high, :]
@@ -221,9 +223,15 @@
     exact = functools.partial(
         lax.dot_general, precision=lax.Precision.HIGHEST, preferred_element_type=jnp.float32
     )
-    per_point = jnp.broadcast_to(policy[...], (8, policy.shape[1]))
-    raw = exact(per_point, trunk, (((1,), (1,)), ((), ())))
-    pooled = exact(jnp.where(inside, 1.0, 0.0), trunk, (((1,), (0,)), ((), ()))) / CELLS
+    weighted = trunk * policy[...]
+    weighted = sum(weighted[:, part : part + 128] for part in range(0, weighted.shape[1], 128))
+    raw = exact(jnp.ones((8, 128), jnp.float32), weighted, (((1,), (1,)), ((), ())))
+    sums = [
+        jnp.sum(trunk * jnp.concatenate([of_board[board]] * (trunk.shape[1] // 128), axis=1), axis=0, keepdims=True)
+        for board in range(number)
+    ]
+    sums.append(jnp.zeros((8 - number, trunk.shape[1]), jnp.float32))
+    pooled = jnp.concatenate(sums, axis=0) / CELLS
     pass_raw = jnp.sum(pooled * passing[...], axis=1, keepdims=True)
     value = jnp.tanh(jnp.sum(pooled * valuing[...], axis=1, keepdims=True))
     logits = 10.0 * jnp.tanh(raw / 10.0)
@@ -277,6 +285,7 @@
             pltpu.VMEM((2, points + 2 * width, 3 * channels), jnp.bfloat16),
             pltpu.VMEM((points, channels), jnp.float32),
             pltpu.VMEM((points, 128), jnp.float32),
+            pltpu.VMEM((number, points, 128), jnp.float32),
             pltpu.SemaphoreType.DMA((layers,)),
         ],
         compiler_params=pltpu.CompilerParams(vmem_limit_bytes=36 * 2**20),

time: 90.4 us -> 90 us (level)
  no operation moved by 1% of the time
where the time goes in v4:
time: 90 us; the launch traced here: 89.8 us
  waiting for transfers between devices  39.3 us (44%)
  starting transfers between devices  24.7 us (27%)
  Pallas kernels  14.4 us (16%)
  local copies, waits for them, and re-layouts  4.97 us (6%)
  matrix products  3.73 us (4%)
  other arithmetic  1.59 us (2%)
  between operations  1.11 us (1%)
    ppermute x11, waiting for transfers between devices, along_plane(): return lax.ppermute(block, AXES, plane_route(learners, actors, step))  18.5 us
    ppermute x11, starting transfers between devices, along_plane(): return lax.ppermute(block, AXES, plane_route(learners, actors, step))  12.6 us
    pallas_call x1, Pallas kernels, run_tower(): pl.pallas_call(functools.partial(tower, places, layers, rows, number, wid...  12.3 us
    ppermute x4, waiting for transfers between devices, along_z(): lax.ppermute(block, AXES, pairs(learners, actors, lambda l, a: (l, a ^ 2...  11.7 us
    ppermute x3, waiting for transfers between devices, reduce_gradients(): came = lax.ppermute(held.pop(subset), AXES, route)  7.57 us
    ppermute x4, starting transfers between devices, along_z(): lax.ppermute(block, AXES, pairs(learners, actors, lambda l, a: (l, a ^ 2...  6.19 us
    ppermute x3, starting transfers between devices, reduce_gradients(): came = lax.ppermute(held.pop(subset), AXES, route)  5.13 us
    conv_general_dilated x1, matrix products, stem_stream(): lax.conv_general_dilated(field, kernel, (1, 1), ((1, 1), (1, 1)), dimensi...  3.73 us
  transfers between devices with their start and end apart: 23, of which 11 were waited for; matrix products, arithmetic and copies ran while one was open for 8% of the time, Pallas kernels for 1%

profile of v4, /device:TPU:0, one launch (start us, length us, event | category | flops | bytes accessed | tf_op | source)
XLA Modules:
  0.0 89.8 jit_solution(6815665775881156705)
XLA Ops:
  0.6 1.1 %dynamic-slice_bitcast_fusion = f32[2,288,256]{2,1,0:T(8,128)S(1)} fusion(f32[1,4,2,288,256]{4,3,2,1,0:T(8,128)} %param.14, s32[]{:T(128)S(6)} %select_n.11), kind=kLoop, calls=%fused_computation.4 | loop fusion | bytes 1179652 | tf_op jit(solution)/shard_map/jit(dynamic_index_in_dim)/squeeze | solution.py:71
  1.7 3.0 %collective-permute-start.1 = (f32[2,288,256]{2,1,0:T(8,128)S(1)}, f32[2,288,256]{2,1,0:T(8,128)S(1)}, u32[]{:S(2)}, u32[]{:S(2)}) collective-permute-start(f32[2,288,256]{2,1,0:T(8,128)S(1)} %dynamic-slice_bitcast_fusion), channel_id=1, source_target_pairs={{0,8},{1,17},{2,10},{3,19},{4,12},{5,21},{6,14},{7,23},{8,0},{9,25... | collective-permute-start | bytes 1769480 | tf_op jit(solution)/shard_map/ppermute | solution.py:78
  4.8 1.7 %copy-done = f32[1,4,2,288,256]{4,3,2,1,0:T(8,128)S(1)} copy-done((f32[1,4,2,288,256]{4,3,2,1,0:T(8,128)S(1)}, f32[1,4,2,288,256]{4,3,2,1,0:T(8,128)}, u32[]{:S(2)}) %copy-start) | copy-done | bytes 2359320
  6.4 1.2 %pick.1 = (f32[2,288,256]{2,1,0:T(8,128)}, f32[2,288,256]{2,1,0:T(8,128)S(1)}, f32[2,288,256]{2,1,0:T(8,128)S(1)}) custom-call(f32[4,2,288,256]{3,2,1,0:T(8,128)S(1)} %bitcast.26), custom_call_target="tpu_custom_call" | custom-call | tf_op jit(solution)/shard_map/pick/pallas_call | solution.py:54
  8.2 4.4 %collective-permute-done.1 = f32[2,288,256]{2,1,0:T(8,128)S(1)} collective-permute-done((f32[2,288,256]{2,1,0:T(8,128)S(1)}, f32[2,288,256]{2,1,0:T(8,128)S(1)}, u32[]{:S(2)}, u32[]{:S(2)}) %collective-permute-start.1) | collective-permute-done | bytes 589856 | tf_op jit(solution)/shard_map/ppermute | solution.py:78
  12.6 0.9 add.17
  13.5 2.0 %collective-permute-start.2 = (f32[2,288,256]{2,1,0:T(8,128)}, f32[2,288,256]{2,1,0:T(8,128)S(1)}, u32[]{:S(2)}, u32[]{:S(2)}) collective-permute-start(f32[2,288,256]{2,1,0:T(8,128)} %add.17), channel_id=1, source_target_pairs={{0,16},{1,9},{2,18},{3,11},{4,20},{5,13},{6,22},{7,15},{8,24},{9,1... | collective-permute-start | bytes 1769480 | tf_op jit(solution)/shard_map/ppermute | solution.py:78
  15.8 0.8 copy.21
  16.6 3.7 %fusion.3 = f32[1,19,40,256]{3,0,2,1:T(1,128)S(1)} fusion(bf16[1,19,40,4]{3,0,2,1:T(2,128)(2,1)S(1)} %copy.21, bf16[3,3,4,256]{3,2,1,0:T(4,128)(2,1)S(1)} %reshape.52), kind=kOutput, calls=%fused_computation.18 | convolution fusion | flops 13291520 | bytes 802752 | tf_op jit(solution)/shard_map/conv_general_dilated | solution.py:309
  21.3 0.9 collective-permute-done.refs_1_
  22.2 2.2 %collective-permute-done.2.refs_2_ = f32[2,288,256]{2,1,0:T(8,128)S(1)} collective-permute-done((f32[2,288,256]{2,1,0:T(8,128)}, f32[2,288,256]{2,1,0:T(8,128)S(1)}, u32[]{:S(2)}, u32[]{:S(2)}) %collective-permute-start.2) | collective-permute-done | bytes 589856 | tf_op jit(solution)/shard_map/ppermute | solution.py:78
  24.4 0.9 %update.1 = (f32[2,288,256]{2,1,0:T(8,128)}, bf16[2,288,256]{2,1,0:T(8,128)(2,1)S(1)}) custom-call(f32[2,288,256]{2,1,0:T(8,128)S(1)} %get-tuple-element.18.refs_0_, f32[2,288,256]{2,1,0:T(8,128)S(1)} %collective-permute-done.refs_1_, f32[2,288,256]{2,1,0:T(8,128)S(1)} %collective-permute-done.2.refs_2_, f32[2,288,256]{2,1,0:T(8,128)S(1)} %bitcast.28), custom_call_target="tpu_custom_call" | custom-call | tf_op jit(solution)/shard_map/update/pallas_call | solution.py:98
  25.4 1.7 %collective-permute-start.3 = (bf16[2,288,256]{2,1,0:T(8,128)(2,1)S(1)}, bf16[2,288,256]{2,1,0:T(8,128)(2,1)S(1)}, u32[]{:S(2)}, u32[]{:S(2)}) collective-permute-start(bf16[2,288,256]{2,1,0:T(8,128)(2,1)S(1)} %get-tuple-element.22.refs_1_), channel_id=1, source_target_pairs={{0,8},{1,17},{2,10},{3,19},{4,12},{5,21},{6,14},{7,23},{8,0},{9,25... | collective-permute-start | bytes 884744 | tf_op jit(solution)/shard_map/ppermute | solution.py:119
  27.1 1.6 %collective-permute-start.7 = (bf16[2,288,256]{2,1,0:T(8,128)(2,1)S(1)}, bf16[2,288,256]{2,1,0:T(8,128)(2,1)S(1)}, u32[]{:S(2)}, u32[]{:S(2)}) collective-permute-start(bf16[2,288,256]{2,1,0:T(8,128)(2,1)S(1)} %get-tuple-element.22.refs_1_), channel_id=1, source_target_pairs={{0,2},{1,3},{2,0},{3,1},{4,6},{5,7},{6,4},{7,5},{8,10},{9,11},{10,... | collective-permute-start | bytes 884744 | tf_op jit(solution)/shard_map/ppermute | solution.py:116
  28.6 2.6 %collective-permute-start.12 = (bf16[2,288,256]{2,1,0:T(8,128)(2,1)S(1)}, bf16[2,288,256]{2,1,0:T(8,128)(2,1)S(1)}, u32[]{:S(2)}, u32[]{:S(2)}) collective-permute-start(bf16[2,288,256]{2,1,0:T(8,128)(2,1)S(1)} %get-tuple-element.22.refs_1_), channel_id=1, source_target_pairs={{0,4},{1,5},{2,6},{3,7},{4,0},{5,1},{6,2},{7,3},{8,12},{9,13},{10,... | collective-permute-start | bytes 884744 | tf_op jit(solution)/shard_map/ppermute | solution.py:116
  31.2 1.5 %collective-permute-start.4 = (bf16[2,288,256]{2,1,0:T(8,128)(2,1)S(1)}, bf16[2,288,256]{2,1,0:T(8,128)(2,1)S(1)}, u32[]{:S(2)}, u32[]{:S(2)}) collective-permute-start(bf16[2,288,256]{2,1,0:T(8,128)(2,1)S(1)} %get-tuple-element.22.refs_1_), channel_id=1, source_target_pairs={{0,16},{1,9},{2,18},{3,11},{4,20},{5,13},{6,22},{7,15},{8,24},{9,1... | collective-permute-start | bytes 884744 | tf_op jit(solution)/shard_map/ppermute | solution.py:119
  32.8 1.1 %collective-permute-start.5 = (bf16[2,288,256]{2,1,0:T(8,128)(2,1)S(1)}, bf16[2,288,256]{2,1,0:T(8,128)(2,1)S(1)}, u32[]{:S(2)}, u32[]{:S(2)}) collective-permute-start(bf16[2,288,256]{2,1,0:T(8,128)(2,1)S(1)} %collective-permute-done.3.refs_2_), channel_id=1, source_target_pairs={{0,16},{1,9},{2,18},{3,11},{4,20},{5,13},{6,22},{7,15},{8,24},{9,1... | collective-permute-start | bytes 884744 | tf_op jit(solution)/shard_map/ppermute | solution.py:119
  33.8 9.1 %collective-permute-done.7.refs_6_ = bf16[2,288,256]{2,1,0:T(8,128)(2,1)S(1)} collective-permute-done((bf16[2,288,256]{2,1,0:T(8,128)(2,1)S(1)}, bf16[2,288,256]{2,1,0:T(8,128)(2,1)S(1)}, u32[]{:S(2)}, u32[]{:S(2)}) %collective-permute-start.7) | collective-permute-done | bytes 294944 | tf_op jit(solution)/shard_map/ppermute | solution.py:116
  43.2 2.0 %collective-permute-done.12.refs_11_ = bf16[2,288,256]{2,1,0:T(8,128)(2,1)S(1)} collective-permute-done((bf16[2,288,256]{2,1,0:T(8,128)(2,1)S(1)}, bf16[2,288,256]{2,1,0:T(8,128)(2,1)S(1)}, u32[]{:S(2)}, u32[]{:S(2)}) %collective-permute-start.12) | collective-permute-done | bytes 294944 | tf_op jit(solution)/shard_map/ppermute | solution.py:116
  45.3 0.7 collective-permute-start.13
  46.0 1.3 %collective-permute-start.8 = (bf16[2,288,256]{2,1,0:T(8,128)(2,1)S(1)}, bf16[2,288,256]{2,1,0:T(8,128)(2,1)S(1)}, u32[]{:S(2)}, u32[]{:S(2)}) collective-permute-start(bf16[2,288,256]{2,1,0:T(8,128)(2,1)S(1)} %collective-permute-done.7.refs_6_), channel_id=1, source_target_pairs={{0,8},{1,17},{2,10},{3,19},{4,12},{5,21},{6,14},{7,23},{8,0},{9,25... | collective-permute-start | bytes 884744 | tf_op jit(solution)/shard_map/ppermute | solution.py:119
  47.7 1.6 %collective-permute-start.10 = (bf16[2,288,256]{2,1,0:T(8,128)(2,1)S(1)}, bf16[2,288,256]{2,1,0:T(8,128)(2,1)S(1)}, u32[]{:S(2)}, u32[]{:S(2)}) collective-permute-start(bf16[2,288,256]{2,1,0:T(8,128)(2,1)S(1)} %collective-permute-done.5.refs_4_), channel_id=1, source_target_pairs={{0,2},{1,3},{2,0},{3,1},{4,6},{5,7},{6,4},{7,5},{8,10},{9,11},{10,... | collective-permute-start | bytes 884744 | tf_op jit(solution)/shard_map/ppermute | solution.py:116
  49.3 3.4 %collective-permute-done.9.refs_8_ = bf16[2,288,256]{2,1,0:T(8,128)(2,1)S(1)} collective-permute-done((bf16[2,288,256]{2,1,0:T(8,128)(2,1)S(1)}, bf16[2,288,256]{2,1,0:T(8,128)(2,1)S(1)}, u32[]{:S(2)}, u32[]{:S(2)}) %collective-permute-start.9) | collective-permute-done | bytes 294944 | tf_op jit(solution)/shard_map/ppermute | solution.py:119
  52.9 1.9 %collective-permute-start.15 = (bf16[2,288,256]{2,1,0:T(8,128)(2,1)S(1)}, bf16[2,288,256]{2,1,0:T(8,128)(2,1)S(1)}, u32[]{:S(2)}, u32[]{:S(2)}) collective-permute-start(bf16[2,288,256]{2,1,0:T(8,128)(2,1)S(1)} %collective-permute-done.13.refs_12_), channel_id=1, source_target_pairs={{0,16},{1,9},{2,18},{3,11},{4,20},{5,13},{6,22},{7,15},{8,24},{9,1... | collective-permute-start | bytes 884744 | tf_op jit(solution)/shard_map/ppermute | solution.py:119
  54.9 4.1 %collective-permute-done.8.refs_7_ = bf16[2,288,256]{2,1,0:T(8,128)(2,1)S(1)} collective-permute-done((bf16[2,288,256]{2,1,0:T(8,128)(2,1)S(1)}, bf16[2,288,256]{2,1,0:T(8,128)(2,1)S(1)}, u32[]{:S(2)}, u32[]{:S(2)}) %collective-permute-start.8) | collective-permute-done | bytes 294944 | tf_op jit(solution)/shard_map/ppermute | solution.py:119
  59.0 0.8 collective-permute-start.19
  60.5 2.4 %collective-permute-start.18 = (bf16[2,288,256]{2,1,0:T(8,128)(2,1)S(1)}, bf16[2,288,256]{2,1,0:T(8,128)(2,1)S(1)}, u32[]{:S(2)}, u32[]{:S(2)}) collective-permute-start(bf16[2,288,256]{2,1,0:T(8,128)(2,1)S(1)} %collective-permute-done.17.refs_17_), channel_id=1, source_target_pairs={{0,8},{1,17},{2,10},{3,19},{4,12},{5,21},{6,14},{7,23},{8,0},{9,25... | collective-permute-start | bytes 884744 | tf_op jit(solution)/shard_map/ppermute | solution.py:119
  63.9 4.9 %collective-permute-done.19.refs_19_ = bf16[2,288,256]{2,1,0:T(8,128)(2,1)S(1)} collective-permute-done((bf16[2,288,256]{2,1,0:T(8,128)(2,1)S(1)}, bf16[2,288,256]{2,1,0:T(8,128)(2,1)S(1)}, u32[]{:S(2)}, u32[]{:S(2)}) %collective-permute-start.19) | collective-permute-done | bytes 294944 | tf_op jit(solution)/shard_map/ppermute | solution.py:119
  69.0 0.7 collective-permute-start.21
  69.7 6.0 %collective-permute-done.21.refs_20_ = bf16[2,288,256]{2,1,0:T(8,128)(2,1)S(1)} collective-permute-done((bf16[2,288,256]{2,1,0:T(8,128)(2,1)S(1)}, bf16[2,288,256]{2,1,0:T(8,128)(2,1)S(1)}, u32[]{:S(2)}, u32[]{:S(2)}) %collective-permute-start.21) | collective-permute-done | bytes 294944 | tf_op jit(solution)/shard_map/ppermute | solution.py:119
  75.7 1.6 %collective-permute-done.22.refs_16_ = bf16[2,288,256]{2,1,0:T(8,128)(2,1)S(1)} collective-permute-done((bf16[2,288,256]{2,1,0:T(8,128)(2,1)S(1)}, bf16[2,288,256]{2,1,0:T(8,128)(2,1)S(1)}, u32[]{:S(2)}, u32[]{:S(2)}) %collective-permute-start.22) | collective-permute-done | bytes 294944 | tf_op jit(solution)/shard_map/ppermute | solution.py:122
  77.4 12.3 %tower.1 = (f32[2,1,362]{2,1,0:T(1,128)}, f32[1,2]{1,0:T(1,128)}) custom-call(bf16[8,288,256]{2,1,0:T(8,128)(2,1)S(1)} %collective-permute-done.6.refs_0_, bf16[2,288,256]{2,1,0:T(8,128)(2,1)S(1)} %get-tuple-element.22.refs_1_, bf16[2,288,256]{2,1,0:T(8,128)(2,1)S(1)} %collective-permute-done.3.refs_2_, ...), custom_call_target="tpu_custom_call" | custom-call | tf_op jit(solution)/shard_map/tower/pallas_call | solution.py:275
  (70 shorter events, 4.6 us)
Async XLA Ops:
  1.7 10.9 %collective-permute-start.1 = (f32[2,288,256]{2,1,0:T(8,128)S(1)}, f32[2,288,256]{2,1,0:T(8,128)S(1)}, u32[]{:S(2)}, u32[]{:S(2)}) collective-permute-start(f32[2,288,256]{2,1,0:T(8,128)S(1)} %dynamic-slice_bitcast_fusion), channel_id=1, source_target_pairs={{0,8},{1,17},{2,10},{3,19},{4,12},{5,21},{6,14},{7,23},{8,0},{9,25... | collective-permute-start | bytes 1769480 | tf_op jit(solution)/shard_map/ppermute | solution.py:78
  4.8 1.7 %copy-start = (f32[1,4,2,288,256]{4,3,2,1,0:T(8,128)S(1)}, f32[1,4,2,288,256]{4,3,2,1,0:T(8,128)}, u32[]{:S(2)}) copy-start(f32[1,4,2,288,256]{4,3,2,1,0:T(8,128)} %param.14) | copy-start | bytes 7077892
  6.4 1.4 %copy-start.7 = (s32[2,1,361]{2,1,0:T(1,128)S(1)}, s32[2,1,361]{2,1,0:T(1,128)}, u32[]{:S(2)}) copy-start(s32[2,1,361]{2,1,0:T(1,128)} %param.10) | copy-start | bytes 8668
  6.4 1.5 %copy-start.9 = (s32[2,1]{0,1:T(1,128)S(1)}, s32[2,1]{0,1:T(1,128)}, u32[]{:S(2)}) copy-start(s32[2,1]{0,1:T(1,128)} %param.11) | copy-start | bytes 28
  7.6 14.6 %collective-permute-start = (f32[2,288,256]{2,1,0:T(8,128)}, f32[2,288,256]{2,1,0:T(8,128)S(1)}, u32[]{:S(2)}, u32[]{:S(2)}) collective-permute-start(f32[2,288,256]{2,1,0:T(8,128)} %get-tuple-element.16), channel_id=1, source_target_pairs={{0,8},{1,17},{2,10},{3,19},{4,12},{5,21},{6,14},{7,23},{8,0},{9,25... | collective-permute-start | bytes 1769480 | tf_op jit(solution)/shard_map/ppermute | solution.py:78
  12.6 4.0 %copy-start.6 = (bf16[36,256]{1,0:T(8,128)(2,1)S(1)}, bf16[36,256]{1,0:T(8,128)(2,1)}, u32[]{:S(2)}) copy-start(bf16[36,256]{1,0:T(8,128)(2,1)} %param.15) | copy-start | bytes 55300
  13.5 10.9 %collective-permute-start.2 = (f32[2,288,256]{2,1,0:T(8,128)}, f32[2,288,256]{2,1,0:T(8,128)S(1)}, u32[]{:S(2)}, u32[]{:S(2)}) collective-permute-start(f32[2,288,256]{2,1,0:T(8,128)} %add.17), channel_id=1, source_target_pairs={{0,16},{1,9},{2,18},{3,11},{4,20},{5,13},{6,22},{7,15},{8,24},{9,1... | collective-permute-start | bytes 1769480 | tf_op jit(solution)/shard_map/ppermute | solution.py:78
  20.4 4.1 %copy-start.1 = (f32[1,2,288,256]{3,2,1,0:T(8,128)S(1)}, f32[1,2,288,256]{3,2,1,0:T(8,128)}, u32[]{:S(2)}) copy-start(f32[1,2,288,256]{3,2,1,0:T(8,128)} %param.13) | copy-start | bytes 1769476
  25.4 7.4 %collective-permute-start.3 = (bf16[2,288,256]{2,1,0:T(8,128)(2,1)S(1)}, bf16[2,288,256]{2,1,0:T(8,128)(2,1)S(1)}, u32[]{:S(2)}, u32[]{:S(2)}) collective-permute-start(bf16[2,288,256]{2,1,0:T(8,128)(2,1)S(1)} %get-tuple-element.22.refs_1_), channel_id=1, source_target_pairs={{0,8},{1,17},{2,10},{3,19},{4,12},{5,21},{6,14},{7,23},{8,0},{9,25... | collective-permute-start | bytes 884744 | tf_op jit(solution)/shard_map/ppermute | solution.py:119
  27.1 15.8 %collective-permute-start.7 = (bf16[2,288,256]{2,1,0:T(8,128)(2,1)S(1)}, bf16[2,288,256]{2,1,0:T(8,128)(2,1)S(1)}, u32[]{:S(2)}, u32[]{:S(2)}) collective-permute-start(bf16[2,288,256]{2,1,0:T(8,128)(2,1)S(1)} %get-tuple-element.22.refs_1_), channel_id=1, source_target_pairs={{0,2},{1,3},{2,0},{3,1},{4,6},{5,7},{6,4},{7,5},{8,10},{9,11},{10,... | collective-permute-start | bytes 884744 | tf_op jit(solution)/shard_map/ppermute | solution.py:116
  28.6 16.6 %collective-permute-start.12 = (bf16[2,288,256]{2,1,0:T(8,128)(2,1)S(1)}, bf16[2,288,256]{2,1,0:T(8,128)(2,1)S(1)}, u32[]{:S(2)}, u32[]{:S(2)}) collective-permute-start(bf16[2,288,256]{2,1,0:T(8,128)(2,1)S(1)} %get-tuple-element.22.refs_1_), channel_id=1, source_target_pairs={{0,4},{1,5},{2,6},{3,7},{4,0},{5,1},{6,2},{7,3},{8,12},{9,13},{10,... | collective-permute-start | bytes 884744 | tf_op jit(solution)/shard_map/ppermute | solution.py:116
  31.2 16.1 %collective-permute-start.4 = (bf16[2,288,256]{2,1,0:T(8,128)(2,1)S(1)}, bf16[2,288,256]{2,1,0:T(8,128)(2,1)S(1)}, u32[]{:S(2)}, u32[]{:S(2)}) collective-permute-start(bf16[2,288,256]{2,1,0:T(8,128)(2,1)S(1)} %get-tuple-element.22.refs_1_), channel_id=1, source_target_pairs={{0,16},{1,9},{2,18},{3,11},{4,20},{5,13},{6,22},{7,15},{8,24},{9,1... | collective-permute-start | bytes 884744 | tf_op jit(solution)/shard_map/ppermute | solution.py:119
  32.8 15.0 %collective-permute-start.5 = (bf16[2,288,256]{2,1,0:T(8,128)(2,1)S(1)}, bf16[2,288,256]{2,1,0:T(8,128)(2,1)S(1)}, u32[]{:S(2)}, u32[]{:S(2)}) collective-permute-start(bf16[2,288,256]{2,1,0:T(8,128)(2,1)S(1)} %collective-permute-done.3.refs_2_), channel_id=1, source_target_pairs={{0,16},{1,9},{2,18},{3,11},{4,20},{5,13},{6,22},{7,15},{8,24},{9,1... | collective-permute-start | bytes 884744 | tf_op jit(solution)/shard_map/ppermute | solution.py:119
  42.9 9.9 %collective-permute-start.9 = (bf16[2,288,256]{2,1,0:T(8,128)(2,1)S(1)}, bf16[2,288,256]{2,1,0:T(8,128)(2,1)S(1)}, u32[]{:S(2)}, u32[]{:S(2)}) collective-permute-start(bf16[2,288,256]{2,1,0:T(8,128)(2,1)S(1)} %collective-permute-done.7.refs_6_), channel_id=1, source_target_pairs={{0,16},{1,9},{2,18},{3,11},{4,20},{5,13},{6,22},{7,15},{8,24},{9,1... | collective-permute-start | bytes 884744 | tf_op jit(solution)/shard_map/ppermute | solution.py:119
  45.3 7.6 %collective-permute-start.13 = (bf16[2,288,256]{2,1,0:T(8,128)(2,1)S(1)}, bf16[2,288,256]{2,1,0:T(8,128)(2,1)S(1)}, u32[]{:S(2)}, u32[]{:S(2)}) collective-permute-start(bf16[2,288,256]{2,1,0:T(8,128)(2,1)S(1)} %collective-permute-done.12.refs_11_), channel_id=1, source_target_pairs={{0,8},{1,17},{2,10},{3,19},{4,12},{5,21},{6,14},{7,23},{8,0},{9,25... | collective-permute-start | bytes 884744 | tf_op jit(solution)/shard_map/ppermute | solution.py:119
  46.0 13.0 %collective-permute-start.8 = (bf16[2,288,256]{2,1,0:T(8,128)(2,1)S(1)}, bf16[2,288,256]{2,1,0:T(8,128)(2,1)S(1)}, u32[]{:S(2)}, u32[]{:S(2)}) collective-permute-start(bf16[2,288,256]{2,1,0:T(8,128)(2,1)S(1)} %collective-permute-done.7.refs_6_), channel_id=1, source_target_pairs={{0,8},{1,17},{2,10},{3,19},{4,12},{5,21},{6,14},{7,23},{8,0},{9,25... | collective-permute-start | bytes 884744 | tf_op jit(solution)/shard_map/ppermute | solution.py:119
  47.3 11.7 %collective-permute-start.17 = (bf16[2,288,256]{2,1,0:T(8,128)(2,1)S(1)}, bf16[2,288,256]{2,1,0:T(8,128)(2,1)S(1)}, u32[]{:S(2)}, u32[]{:S(2)}) collective-permute-start(bf16[2,288,256]{2,1,0:T(8,128)(2,1)S(1)} %collective-permute-done.12.refs_11_), channel_id=1, source_target_pairs={{0,2},{1,3},{2,0},{3,1},{4,6},{5,7},{6,4},{7,5},{8,10},{9,11},{10,... | collective-permute-start | bytes 884744 | tf_op jit(solution)/shard_map/ppermute | solution.py:116
  47.7 12.7 %collective-permute-start.10 = (bf16[2,288,256]{2,1,0:T(8,128)(2,1)S(1)}, bf16[2,288,256]{2,1,0:T(8,128)(2,1)S(1)}, u32[]{:S(2)}, u32[]{:S(2)}) collective-permute-start(bf16[2,288,256]{2,1,0:T(8,128)(2,1)S(1)} %collective-permute-done.5.refs_4_), channel_id=1, source_target_pairs={{0,2},{1,3},{2,0},{3,1},{4,6},{5,7},{6,4},{7,5},{8,10},{9,11},{10,... | collective-permute-start | bytes 884744 | tf_op jit(solution)/shard_map/ppermute | solution.py:116
  52.7 10.3 %collective-permute-start.14 = (bf16[2,288,256]{2,1,0:T(8,128)(2,1)S(1)}, bf16[2,288,256]{2,1,0:T(8,128)(2,1)S(1)}, u32[]{:S(2)}, u32[]{:S(2)}) collective-permute-start(bf16[2,288,256]{2,1,0:T(8,128)(2,1)S(1)} %collective-permute-done.12.refs_11_), channel_id=1, source_target_pairs={{0,16},{1,9},{2,18},{3,11},{4,20},{5,13},{6,22},{7,15},{8,24},{9,1... | collective-permute-start | bytes 884744 | tf_op jit(solution)/shard_map/ppermute | solution.py:119
  52.9 10.2 %collective-permute-start.15 = (bf16[2,288,256]{2,1,0:T(8,128)(2,1)S(1)}, bf16[2,288,256]{2,1,0:T(8,128)(2,1)S(1)}, u32[]{:S(2)}, u32[]{:S(2)}) collective-permute-start(bf16[2,288,256]{2,1,0:T(8,128)(2,1)S(1)} %collective-permute-done.13.refs_12_), channel_id=1, source_target_pairs={{0,16},{1,9},{2,18},{3,11},{4,20},{5,13},{6,22},{7,15},{8,24},{9,1... | collective-permute-start | bytes 884744 | tf_op jit(solution)/shard_map/ppermute | solution.py:119
  59.0 18.3 %collective-permute-start.6 = (bf16[8,288,256]{2,1,0:T(8,128)(2,1)S(1)}, bf16[8,288,256]{2,1,0:T(8,128)(2,1)S(1)}, u32[]{:S(2)}, u32[]{:S(2)}) collective-permute-start(bf16[8,288,256]{2,1,0:T(8,128)(2,1)S(1)} %pad_maximum_fusion), channel_id=1, source_target_pairs={{0,1},{1,0},{2,3},{3,2},{4,5},{5,4},{6,7},{7,6},{8,9},{9,8},{10,11... | collective-permute-start | bytes 3538952 | tf_op jit(solution)/shard_map/ppermute | solution.py:122
  59.0 9.7 %collective-permute-start.19 = (bf16[2,288,256]{2,1,0:T(8,128)(2,1)S(1)}, bf16[2,288,256]{2,1,0:T(8,128)(2,1)S(1)}, u32[]{:S(2)}, u32[]{:S(2)}) collective-permute-start(bf16[2,288,256]{2,1,0:T(8,128)(2,1)S(1)} %collective-permute-done.17.refs_17_), channel_id=1, source_target_pairs={{0,16},{1,9},{2,18},{3,11},{4,20},{5,13},{6,22},{7,15},{8,24},{9,1... | collective-permute-start | bytes 884744 | tf_op jit(solution)/shard_map/ppermute | solution.py:119
  60.5 8.3 %collective-permute-start.18 = (bf16[2,288,256]{2,1,0:T(8,128)(2,1)S(1)}, bf16[2,288,256]{2,1,0:T(8,128)(2,1)S(1)}, u32[]{:S(2)}, u32[]{:S(2)}) collective-permute-start(bf16[2,288,256]{2,1,0:T(8,128)(2,1)S(1)} %collective-permute-done.17.refs_17_), channel_id=1, source_target_pairs={{0,8},{1,17},{2,10},{3,19},{4,12},{5,21},{6,14},{7,23},{8,0},{9,25... | collective-permute-start | bytes 884744 | tf_op jit(solution)/shard_map/ppermute | solution.py:119
  63.0 14.3 %collective-permute-start.11 = (bf16[8,288,256]{2,1,0:T(8,128)(2,1)S(1)}, bf16[8,288,256]{2,1,0:T(8,128)(2,1)S(1)}, u32[]{:S(2)}, u32[]{:S(2)}) collective-permute-start(bf16[8,288,256]{2,1,0:T(8,128)(2,1)S(1)} %pad_maximum_fusion.1), channel_id=1, source_target_pairs={{0,1},{1,0},{2,3},{3,2},{4,5},{5,4},{6,7},{7,6},{8,9},{9,8},{10,11... | collective-permute-start | bytes 3538952 | tf_op jit(solution)/shard_map/ppermute | solution.py:122
  63.3 14.1 %copy-start.2 = (bf16[760,384]{1,0:T(8,128)(2,1)S(1)}, bf16[760,384]{1,0:T(8,128)(2,1)}, u32[]{:S(2)}) copy-start(bf16[760,384]{1,0:T(8,128)(2,1)} %constant.36.clone.refs_26_) | copy-start | bytes 1751044
  63.3 14.1 %copy-start.3 = (f32[256]{0:T(256)S(1)}, f32[256]{0:T(256)}, u32[]{:S(2)}) copy-start(f32[256]{0:T(256)} %param.16) | copy-start | bytes 3076
  63.3 14.1 %copy-start.4 = (f32[256]{0:T(256)S(1)}, f32[256]{0:T(256)}, u32[]{:S(2)}) copy-start(f32[256]{0:T(256)} %param.17) | copy-start | bytes 3076
  63.3 14.1 %copy-start.5 = (f32[256]{0:T(256)S(1)}, f32[256]{0:T(256)}, u32[]{:S(2)}) copy-start(f32[256]{0:T(256)} %param.18) | copy-start | bytes 3076
  63.3 14.0 %collective-permute-start.16 = (bf16[8,288,256]{2,1,0:T(8,128)(2,1)S(1)}, bf16[8,288,256]{2,1,0:T(8,128)(2,1)S(1)}, u32[]{:S(2)}, u32[]{:S(2)}) collective-permute-start(bf16[8,288,256]{2,1,0:T(8,128)(2,1)S(1)} %pad_maximum_fusion.2), channel_id=1, source_target_pairs={{0,1},{1,0},{2,3},{3,2},{4,5},{5,4},{6,7},{7,6},{8,9},{9,8},{10,11... | collective-permute-start | bytes 3538952 | tf_op jit(solution)/shard_map/ppermute | solution.py:122
  68.8 8.5 %collective-permute-start.20 = (bf16[6,288,256]{2,1,0:T(8,128)(2,1)S(1)}, bf16[6,288,256]{2,1,0:T(8,128)(2,1)S(1)}, u32[]{:S(2)}, u32[]{:S(2)}) collective-permute-start(bf16[6,288,256]{2,1,0:T(8,128)(2,1)S(1)} %pad_maximum_fusion.3), channel_id=1, source_target_pairs={{0,1},{1,0},{2,3},{3,2},{4,5},{5,4},{6,7},{7,6},{8,9},{9,8},{10,11... | collective-permute-start | bytes 2654216 | tf_op jit(solution)/shard_map/ppermute | solution.py:122
  69.0 6.7 %collective-permute-start.21 = (bf16[2,288,256]{2,1,0:T(8,128)(2,1)S(1)}, bf16[2,288,256]{2,1,0:T(8,128)(2,1)S(1)}, u32[]{:S(2)}, u32[]{:S(2)}) collective-permute-start(bf16[2,288,256]{2,1,0:T(8,128)(2,1)S(1)} %collective-permute-done.18.refs_18_), channel_id=1, source_target_pairs={{0,16},{1,9},{2,18},{3,11},{4,20},{5,13},{6,22},{7,15},{8,24},{9,1... | collective-permute-start | bytes 884744 | tf_op jit(solution)/shard_map/ppermute | solution.py:119
  75.7 1.6 %collective-permute-start.22 = (bf16[2,288,256]{2,1,0:T(8,128)(2,1)S(1)}, bf16[2,288,256]{2,1,0:T(8,128)(2,1)S(1)}, u32[]{:S(2)}, u32[]{:S(2)}) collective-permute-start(bf16[2,288,256]{2,1,0:T(8,128)(2,1)S(1)} %collective-permute-done.21.refs_20_), channel_id=1, source_target_pairs={{0,1},{1,0},{2,3},{3,2},{4,5},{5,4},{6,7},{7,6},{8,9},{9,8},{10,11... | collective-permute-start | bytes 884744 | tf_op jit(solution)/shard_map/ppermute | solution.py:122
  (1 other events, 0.7 us)

commit v5 on v4

--- a/solution.py
+++ b/solution.py
@@ -158,8 +158,8 @@
 
 def tower(places, layers, rows, number, width, cuts, *refs):
     blocks = refs[: len(places)]
-    stem, legal, policy, passing, valuing, places_of_points, logp, worth = refs[len(places) : len(places) + 8]
-    weights, field, stream, mask, of_board, arrived = refs[len(places) + 8 :]
+    stem, legal, policy, passing, valuing, places_of_points, mask, of_board, owned, logp, worth = refs[len(places) : len(places) + 11]
+    weights, field, stream, arrived = refs[len(places) + 11 :]
     points = BOARD * width
     for labels, block in zip(places, blocks):
         if labels is None:
@@ -175,11 +175,6 @@
     for half in range(2):
         field[half, :width, :] = jnp.zeros((width, field.shape[2]), jnp.bfloat16)
         field[half, width + points :, :] = jnp.zeros((width, field.shape[2]), jnp.bfloat16)
-    column = lax.rem(lax.broadcasted_iota(jnp.int32, mask.shape, 0), width)
-    on_board = (lax.rem(column, PITCH) < BOARD) & (column < PITCH * number)
-    mask[...] = jnp.where(on_board, 1.0, 0.0)
-    for board in range(number):
-        of_board[board] = jnp.where((column >= board * PITCH) & (column < (board + 1) * PITCH), 1.0, 0.0)
 
     def rectified(low, high, values):
         keep = mask[low:high, :]
@@ -217,9 +212,7 @@
                 spread(0, low, high, values)
 
     trunk = stream[...]
-    column = lax.rem(lax.broadcasted_iota(jnp.int32, (8, points), 1), width)
-    owner = lax.broadcasted_iota(jnp.int32, (8, points), 0)
-    inside = (column >= owner * PITCH) & (column < owner * PITCH + BOARD) & (owner < number)
+    inside = owned[...] > 0
     exact = functools.partial(
         lax.dot_general, precision=lax.Precision.HIGHEST, preferred_element_type=jnp.float32
     )
@@ -265,6 +258,11 @@
     lanes = -(-(CELLS + 1) // 128) * 128
     target = np.where(known, cell, lanes)[:, None] == np.arange(lanes)[None]
     places_of_points = jnp.asarray(target.astype(jnp.bfloat16))
+    owner = np.where(known, column // PITCH, -1)
+    mask = jnp.asarray(np.repeat(known[:, None], 128, axis=1).astype(np.float32))
+    of_board = np.arange(number)[:, None] == owner[None]
+    of_board = jnp.asarray(np.repeat(of_board[:, :, None], 128, axis=2).astype(np.float32))
+    owned = jnp.asarray((np.arange(8)[:, None] == owner[None]).astype(np.float32))
     points = BOARD * width
     channels = stem.shape[1]
     places = [labels for _, labels in found]
@@ -278,19 +276,17 @@
             jax.ShapeDtypeStruct((steps_here, local_count, CELLS + 1), jnp.float32),
             jax.ShapeDtypeStruct((local_count, steps_here), jnp.float32),
         ),
-        in_specs=[anywhere] * len(found) + [inside] * 6,
+        in_specs=[anywhere] * len(found) + [inside] * 9,
         out_specs=(inside, inside),
         scratch_shapes=[
             pltpu.VMEM((layers, 2, depth, channels), jnp.bfloat16),
             pltpu.VMEM((2, points + 2 * width, 3 * channels), jnp.bfloat16),
             pltpu.VMEM((points, channels), jnp.float32),
-            pltpu.VMEM((points, 128), jnp.float32),
-            pltpu.VMEM((number, points, 128), jnp.float32),
             pltpu.SemaphoreType.DMA((layers,)),
         ],
         compiler_params=pltpu.CompilerParams(vmem_limit_bytes=36 * 2**20),
         name="tower",
-    )(*[block for block, _ in found], stem, legal, policy, passing, valuing, places_of_points)
+    )(*[block for block, _ in found], stem, legal, policy, passing, valuing, places_of_points, mask, of_board, owned)
 
 
 def padded_boards(rows, width):

time: 90 us -> 89.8 us (level)
    unnamed x21 -> x27, local copies, waits for them, and re-layouts: 2.37 us -> 2.39 us
where the time goes in v5:
time: 89.8 us; the launch traced here: 89.6 us
  waiting for transfers between devices  39.3 us (44%)
  starting transfers between devices  24.7 us (28%)
  Pallas kernels  14.1 us (16%)
  local copies, waits for them, and re-layouts  4.99 us (6%)
  matrix products  3.73 us (4%)
  other arithmetic  1.59 us (2%)
  between operations  1.16 us (1%)
    ppermute x11, waiting for transfers between devices, along_plane(): return lax.ppermute(block, AXES, plane_route(learners, actors, step))  18.4 us
    ppermute x11, starting transfers between devices, along_plane(): return lax.ppermute(block, AXES, plane_route(learners, actors, step))  12.6 us
    pallas_call x1, Pallas kernels, run_tower(): pl.pallas_call(functools.partial(tower, places, layers, rows, number, wid...  12 us
    ppermute x4, waiting for transfers between devices, along_z(): lax.ppermute(block, AXES, pairs(learners, actors, lambda l, a: (l, a ^ 2...  11.7 us
    ppermute x3, waiting for transfers between devices, reduce_gradients(): came = lax.ppermute(held.pop(subset), AXES, route)  7.57 us
    ppermute x4, starting transfers between devices, along_z(): lax.ppermute(block, AXES, pairs(learners, actors, lambda l, a: (l, a ^ 2...  6.19 us
    ppermute x3, starting transfers between devices, reduce_gradients(): came = lax.ppermute(held.pop(subset), AXES, route)  5.13 us
    conv_general_dilated x1, matrix products, stem_stream(): lax.conv_general_dilated(field, kernel, (1, 1), ((1, 1), (1, 1)), dimensi...  3.73 us
  transfers between devices with their start and end apart: 23, of which 11 were waited for; matrix products, arithmetic and copies ran while one was open for 8% of the time, Pallas kernels for 1%

profile of v5, /device:TPU:0, one launch (start us, length us, event | category | flops | bytes accessed | tf_op | source)
XLA Modules:
  0.0 89.6 jit_solution(15464293597536580342)
XLA Ops:
  0.6 1.1 %dynamic-slice_bitcast_fusion = f32[2,288,256]{2,1,0:T(8,128)S(1)} fusion(f32[1,4,2,288,256]{4,3,2,1,0:T(8,128)} %param.17, s32[]{:T(128)S(6)} %select_n.11), kind=kLoop, calls=%fused_computation.4 | loop fusion | bytes 1179652 | tf_op jit(solution)/shard_map/jit(dynamic_index_in_dim)/squeeze | solution.py:71
  1.7 3.0 %collective-permute-start.1 = (f32[2,288,256]{2,1,0:T(8,128)S(1)}, f32[2,288,256]{2,1,0:T(8,128)S(1)}, u32[]{:S(2)}, u32[]{:S(2)}) collective-permute-start(f32[2,288,256]{2,1,0:T(8,128)S(1)} %dynamic-slice_bitcast_fusion), channel_id=1, source_target_pairs={{0,8},{1,17},{2,10},{3,19},{4,12},{5,21},{6,14},{7,23},{8,0},{9,25... | collective-permute-start | bytes 1769480 | tf_op jit(solution)/shard_map/ppermute | solution.py:78
  4.8 1.7 %copy-done = f32[1,4,2,288,256]{4,3,2,1,0:T(8,128)S(1)} copy-done((f32[1,4,2,288,256]{4,3,2,1,0:T(8,128)S(1)}, f32[1,4,2,288,256]{4,3,2,1,0:T(8,128)}, u32[]{:S(2)}) %copy-start) | copy-done | bytes 2359320
  6.4 1.2 %pick.1 = (f32[2,288,256]{2,1,0:T(8,128)}, f32[2,288,256]{2,1,0:T(8,128)S(1)}, f32[2,288,256]{2,1,0:T(8,128)S(1)}) custom-call(f32[4,2,288,256]{3,2,1,0:T(8,128)S(1)} %bitcast.26), custom_call_target="tpu_custom_call" | custom-call | tf_op jit(solution)/shard_map/pick/pallas_call | solution.py:54
  8.2 4.4 %collective-permute-done.1 = f32[2,288,256]{2,1,0:T(8,128)S(1)} collective-permute-done((f32[2,288,256]{2,1,0:T(8,128)S(1)}, f32[2,288,256]{2,1,0:T(8,128)S(1)}, u32[]{:S(2)}, u32[]{:S(2)}) %collective-permute-start.1) | collective-permute-done | bytes 589856 | tf_op jit(solution)/shard_map/ppermute | solution.py:78
  12.6 0.9 add.17
  13.5 2.0 %collective-permute-start.2 = (f32[2,288,256]{2,1,0:T(8,128)}, f32[2,288,256]{2,1,0:T(8,128)S(1)}, u32[]{:S(2)}, u32[]{:S(2)}) collective-permute-start(f32[2,288,256]{2,1,0:T(8,128)} %add.17), channel_id=1, source_target_pairs={{0,16},{1,9},{2,18},{3,11},{4,20},{5,13},{6,22},{7,15},{8,24},{9,1... | collective-permute-start | bytes 1769480 | tf_op jit(solution)/shard_map/ppermute | solution.py:78
  15.8 0.8 copy.24
  16.6 3.7 %fusion.3 = f32[1,19,40,256]{3,0,2,1:T(1,128)S(1)} fusion(bf16[1,19,40,4]{3,0,2,1:T(2,128)(2,1)S(1)} %copy.24, bf16[3,3,4,256]{3,2,1,0:T(4,128)(2,1)S(1)} %reshape.52), kind=kOutput, calls=%fused_computation.18 | convolution fusion | flops 13291520 | bytes 802752 | tf_op jit(solution)/shard_map/conv_general_dilated | solution.py:305
  21.3 0.9 collective-permute-done.refs_1_
  22.2 2.2 %collective-permute-done.2.refs_2_ = f32[2,288,256]{2,1,0:T(8,128)S(1)} collective-permute-done((f32[2,288,256]{2,1,0:T(8,128)}, f32[2,288,256]{2,1,0:T(8,128)S(1)}, u32[]{:S(2)}, u32[]{:S(2)}) %collective-permute-start.2) | collective-permute-done | bytes 589856 | tf_op jit(solution)/shard_map/ppermute | solution.py:78
  24.4 0.9 %update.1 = (f32[2,288,256]{2,1,0:T(8,128)}, bf16[2,288,256]{2,1,0:T(8,128)(2,1)S(1)}) custom-call(f32[2,288,256]{2,1,0:T(8,128)S(1)} %get-tuple-element.18.refs_0_, f32[2,288,256]{2,1,0:T(8,128)S(1)} %collective-permute-done.refs_1_, f32[2,288,256]{2,1,0:T(8,128)S(1)} %collective-permute-done.2.refs_2_, f32[2,288,256]{2,1,0:T(8,128)S(1)} %bitcast.28), custom_call_target="tpu_custom_call" | custom-call | tf_op jit(solution)/shard_map/update/pallas_call | solution.py:98
  25.4 1.7 %collective-permute-start.3 = (bf16[2,288,256]{2,1,0:T(8,128)(2,1)S(1)}, bf16[2,288,256]{2,1,0:T(8,128)(2,1)S(1)}, u32[]{:S(2)}, u32[]{:S(2)}) collective-permute-start(bf16[2,288,256]{2,1,0:T(8,128)(2,1)S(1)} %get-tuple-element.22.refs_1_), channel_id=1, source_target_pairs={{0,8},{1,17},{2,10},{3,19},{4,12},{5,21},{6,14},{7,23},{8,0},{9,25... | collective-permute-start | bytes 884744 | tf_op jit(solution)/shard_map/ppermute | solution.py:119
  27.1 1.6 %collective-permute-start.7 = (bf16[2,288,256]{2,1,0:T(8,128)(2,1)S(1)}, bf16[2,288,256]{2,1,0:T(8,128)(2,1)S(1)}, u32[]{:S(2)}, u32[]{:S(2)}) collective-permute-start(bf16[2,288,256]{2,1,0:T(8,128)(2,1)S(1)} %get-tuple-element.22.refs_1_), channel_id=1, source_target_pairs={{0,2},{1,3},{2,0},{3,1},{4,6},{5,7},{6,4},{7,5},{8,10},{9,11},{10,... | collective-permute-start | bytes 884744 | tf_op jit(solution)/shard_map/ppermute | solution.py:116
  28.6 2.6 %collective-permute-start.12 = (bf16[2,288,256]{2,1,0:T(8,128)(2,1)S(1)}, bf16[2,288,256]{2,1,0:T(8,128)(2,1)S(1)}, u32[]{:S(2)}, u32[]{:S(2)}) collective-permute-start(bf16[2,288,256]{2,1,0:T(8,128)(2,1)S(1)} %get-tuple-element.22.refs_1_), channel_id=1, source_target_pairs={{0,4},{1,5},{2,6},{3,7},{4,0},{5,1},{6,2},{7,3},{8,12},{9,13},{10,... | collective-permute-start | bytes 884744 | tf_op jit(solution)/shard_map/ppermute | solution.py:116
  31.2 1.5 %collective-permute-start.4 = (bf16[2,288,256]{2,1,0:T(8,128)(2,1)S(1)}, bf16[2,288,256]{2,1,0:T(8,128)(2,1)S(1)}, u32[]{:S(2)}, u32[]{:S(2)}) collective-permute-start(bf16[2,288,256]{2,1,0:T(8,128)(2,1)S(1)} %get-tuple-element.22.refs_1_), channel_id=1, source_target_pairs={{0,16},{1,9},{2,18},{3,11},{4,20},{5,13},{6,22},{7,15},{8,24},{9,1... | collective-permute-start | bytes 884744 | tf_op jit(solution)/shard_map/ppermute | solution.py:119
  32.8 1.1 %collective-permute-start.5 = (bf16[2,288,256]{2,1,0:T(8,128)(2,1)S(1)}, bf16[2,288,256]{2,1,0:T(8,128)(2,1)S(1)}, u32[]{:S(2)}, u32[]{:S(2)}) collective-permute-start(bf16[2,288,256]{2,1,0:T(8,128)(2,1)S(1)} %collective-permute-done.3.refs_2_), channel_id=1, source_target_pairs={{0,16},{1,9},{2,18},{3,11},{4,20},{5,13},{6,22},{7,15},{8,24},{9,1... | collective-permute-start | bytes 884744 | tf_op jit(solution)/shard_map/ppermute | solution.py:119
  33.8 9.1 %collective-permute-done.7.refs_6_ = bf16[2,288,256]{2,1,0:T(8,128)(2,1)S(1)} collective-permute-done((bf16[2,288,256]{2,1,0:T(8,128)(2,1)S(1)}, bf16[2,288,256]{2,1,0:T(8,128)(2,1)S(1)}, u32[]{:S(2)}, u32[]{:S(2)}) %collective-permute-start.7) | collective-permute-done | bytes 294944 | tf_op jit(solution)/shard_map/ppermute | solution.py:116
  43.2 2.0 %collective-permute-done.12.refs_11_ = bf16[2,288,256]{2,1,0:T(8,128)(2,1)S(1)} collective-permute-done((bf16[2,288,256]{2,1,0:T(8,128)(2,1)S(1)}, bf16[2,288,256]{2,1,0:T(8,128)(2,1)S(1)}, u32[]{:S(2)}, u32[]{:S(2)}) %collective-permute-start.12) | collective-permute-done | bytes 294944 | tf_op jit(solution)/shard_map/ppermute | solution.py:116
  45.3 0.7 collective-permute-start.13
  46.0 1.3 %collective-permute-start.8 = (bf16[2,288,256]{2,1,0:T(8,128)(2,1)S(1)}, bf16[2,288,256]{2,1,0:T(8,128)(2,1)S(1)}, u32[]{:S(2)}, u32[]{:S(2)}) collective-permute-start(bf16[2,288,256]{2,1,0:T(8,128)(2,1)S(1)} %collective-permute-done.7.refs_6_), channel_id=1, source_target_pairs={{0,8},{1,17},{2,10},{3,19},{4,12},{5,21},{6,14},{7,23},{8,0},{9,25... | collective-permute-start | bytes 884744 | tf_op jit(solution)/shard_map/ppermute | solution.py:119
  47.7 1.6 %collective-permute-start.10 = (bf16[2,288,256]{2,1,0:T(8,128)(2,1)S(1)}, bf16[2,288,256]{2,1,0:T(8,128)(2,1)S(1)}, u32[]{:S(2)}, u32[]{:S(2)}) collective-permute-start(bf16[2,288,256]{2,1,0:T(8,128)(2,1)S(1)} %collective-permute-done.5.refs_4_), channel_id=1, source_target_pairs={{0,2},{1,3},{2,0},{3,1},{4,6},{5,7},{6,4},{7,5},{8,10},{9,11},{10,... | collective-permute-start | bytes 884744 | tf_op jit(solution)/shard_map/ppermute | solution.py:116
  49.3 3.4 %collective-permute-done.9.refs_8_ = bf16[2,288,256]{2,1,0:T(8,128)(2,1)S(1)} collective-permute-done((bf16[2,288,256]{2,1,0:T(8,128)(2,1)S(1)}, bf16[2,288,256]{2,1,0:T(8,128)(2,1)S(1)}, u32[]{:S(2)}, u32[]{:S(2)}) %collective-permute-start.9) | collective-permute-done | bytes 294944 | tf_op jit(solution)/shard_map/ppermute | solution.py:119
  52.9 1.9 %collective-permute-start.15 = (bf16[2,288,256]{2,1,0:T(8,128)(2,1)S(1)}, bf16[2,288,256]{2,1,0:T(8,128)(2,1)S(1)}, u32[]{:S(2)}, u32[]{:S(2)}) collective-permute-start(bf16[2,288,256]{2,1,0:T(8,128)(2,1)S(1)} %collective-permute-done.13.refs_12_), channel_id=1, source_target_pairs={{0,16},{1,9},{2,18},{3,11},{4,20},{5,13},{6,22},{7,15},{8,24},{9,1... | collective-permute-start | bytes 884744 | tf_op jit(solution)/shard_map/ppermute | solution.py:119
  54.9 4.1 %collective-permute-done.8.refs_7_ = bf16[2,288,256]{2,1,0:T(8,128)(2,1)S(1)} collective-permute-done((bf16[2,288,256]{2,1,0:T(8,128)(2,1)S(1)}, bf16[2,288,256]{2,1,0:T(8,128)(2,1)S(1)}, u32[]{:S(2)}, u32[]{:S(2)}) %collective-permute-start.8) | collective-permute-done | bytes 294944 | tf_op jit(solution)/shard_map/ppermute | solution.py:119
  59.0 0.8 collective-permute-start.19
  60.5 2.4 %collective-permute-start.18 = (bf16[2,288,256]{2,1,0:T(8,128)(2,1)S(1)}, bf16[2,288,256]{2,1,0:T(8,128)(2,1)S(1)}, u32[]{:S(2)}, u32[]{:S(2)}) collective-permute-start(bf16[2,288,256]{2,1,0:T(8,128)(2,1)S(1)} %collective-permute-done.17.refs_17_), channel_id=1, source_target_pairs={{0,8},{1,17},{2,10},{3,19},{4,12},{5,21},{6,14},{7,23},{8,0},{9,25... | collective-permute-start | bytes 884744 | tf_op jit(solution)/shard_map/ppermute | solution.py:119
  63.9 4.8 %collective-permute-done.19.refs_19_ = bf16[2,288,256]{2,1,0:T(8,128)(2,1)S(1)} collective-permute-done((bf16[2,288,256]{2,1,0:T(8,128)(2,1)S(1)}, bf16[2,288,256]{2,1,0:T(8,128)(2,1)S(1)}, u32[]{:S(2)}, u32[]{:S(2)}) %collective-permute-start.19) | collective-permute-done | bytes 294944 | tf_op jit(solution)/shard_map/ppermute | solution.py:119
  69.0 0.7 collective-permute-start.21
  69.7 6.0 %collective-permute-done.21.refs_20_ = bf16[2,288,256]{2,1,0:T(8,128)(2,1)S(1)} collective-permute-done((bf16[2,288,256]{2,1,0:T(8,128)(2,1)S(1)}, bf16[2,288,256]{2,1,0:T(8,128)(2,1)S(1)}, u32[]{:S(2)}, u32[]{:S(2)}) %collective-permute-start.21) | collective-permute-done | bytes 294944 | tf_op jit(solution)/shard_map/ppermute | solution.py:119
  75.7 1.6 %collective-permute-done.22.refs_16_ = bf16[2,288,256]{2,1,0:T(8,128)(2,1)S(1)} collective-permute-done((bf16[2,288,256]{2,1,0:T(8,128)(2,1)S(1)}, bf16[2,288,256]{2,1,0:T(8,128)(2,1)S(1)}, u32[]{:S(2)}, u32[]{:S(2)}) %collective-permute-start.22) | collective-permute-done | bytes 294944 | tf_op jit(solution)/shard_map/ppermute | solution.py:122
  77.4 12.0 %tower.1 = (f32[2,1,362]{2,1,0:T(1,128)}, f32[1,2]{1,0:T(1,128)}) custom-call(bf16[8,288,256]{2,1,0:T(8,128)(2,1)S(1)} %collective-permute-done.6.refs_0_, bf16[2,288,256]{2,1,0:T(8,128)(2,1)S(1)} %get-tuple-element.22.refs_1_, bf16[2,288,256]{2,1,0:T(8,128)(2,1)S(1)} %collective-permute-done.3.refs_2_, ...), custom_call_target="tpu_custom_call" | custom-call | tf_op jit(solution)/shard_map/tower/pallas_call | solution.py:273
  (76 shorter events, 4.6 us)
Async XLA Ops:
  1.7 10.9 %collective-permute-start.1 = (f32[2,288,256]{2,1,0:T(8,128)S(1)}, f32[2,288,256]{2,1,0:T(8,128)S(1)}, u32[]{:S(2)}, u32[]{:S(2)}) collective-permute-start(f32[2,288,256]{2,1,0:T(8,128)S(1)} %dynamic-slice_bitcast_fusion), channel_id=1, source_target_pairs={{0,8},{1,17},{2,10},{3,19},{4,12},{5,21},{6,14},{7,23},{8,0},{9,25... | collective-permute-start | bytes 1769480 | tf_op jit(solution)/shard_map/ppermute | solution.py:78
  7.6 14.6 %collective-permute-start = (f32[2,288,256]{2,1,0:T(8,128)}, f32[2,288,256]{2,1,0:T(8,128)S(1)}, u32[]{:S(2)}, u32[]{:S(2)}) collective-permute-start(f32[2,288,256]{2,1,0:T(8,128)} %get-tuple-element.16), channel_id=1, source_target_pairs={{0,8},{1,17},{2,10},{3,19},{4,12},{5,21},{6,14},{7,23},{8,0},{9,25... | collective-permute-start | bytes 1769480 | tf_op jit(solution)/shard_map/ppermute | solution.py:78
  12.6 4.0 %copy-start.9 = (bf16[36,256]{1,0:T(8,128)(2,1)S(1)}, bf16[36,256]{1,0:T(8,128)(2,1)}, u32[]{:S(2)}) copy-start(bf16[36,256]{1,0:T(8,128)(2,1)} %param.18) | copy-start | bytes 55300
  13.5 10.9 %collective-permute-start.2 = (f32[2,288,256]{2,1,0:T(8,128)}, f32[2,288,256]{2,1,0:T(8,128)S(1)}, u32[]{:S(2)}, u32[]{:S(2)}) collective-permute-start(f32[2,288,256]{2,1,0:T(8,128)} %add.17), channel_id=1, source_target_pairs={{0,16},{1,9},{2,18},{3,11},{4,20},{5,13},{6,22},{7,15},{8,24},{9,1... | collective-permute-start | bytes 1769480 | tf_op jit(solution)/shard_map/ppermute | solution.py:78
  20.4 4.1 %copy-start.2 = (f32[1,2,288,256]{3,2,1,0:T(8,128)S(1)}, f32[1,2,288,256]{3,2,1,0:T(8,128)}, u32[]{:S(2)}) copy-start(f32[1,2,288,256]{3,2,1,0:T(8,128)} %param.16) | copy-start | bytes 1769476
  25.4 7.4 %collective-permute-start.3 = (bf16[2,288,256]{2,1,0:T(8,128)(2,1)S(1)}, bf16[2,288,256]{2,1,0:T(8,128)(2,1)S(1)}, u32[]{:S(2)}, u32[]{:S(2)}) collective-permute-start(bf16[2,288,256]{2,1,0:T(8,128)(2,1)S(1)} %get-tuple-element.22.refs_1_), channel_id=1, source_target_pairs={{0,8},{1,17},{2,10},{3,19},{4,12},{5,21},{6,14},{7,23},{8,0},{9,25... | collective-permute-start | bytes 884744 | tf_op jit(solution)/shard_map/ppermute | solution.py:119
  27.1 15.8 %collective-permute-start.7 = (bf16[2,288,256]{2,1,0:T(8,128)(2,1)S(1)}, bf16[2,288,256]{2,1,0:T(8,128)(2,1)S(1)}, u32[]{:S(2)}, u32[]{:S(2)}) collective-permute-start(bf16[2,288,256]{2,1,0:T(8,128)(2,1)S(1)} %get-tuple-element.22.refs_1_), channel_id=1, source_target_pairs={{0,2},{1,3},{2,0},{3,1},{4,6},{5,7},{6,4},{7,5},{8,10},{9,11},{10,... | collective-permute-start | bytes 884744 | tf_op jit(solution)/shard_map/ppermute | solution.py:116
  28.6 16.6 %collective-permute-start.12 = (bf16[2,288,256]{2,1,0:T(8,128)(2,1)S(1)}, bf16[2,288,256]{2,1,0:T(8,128)(2,1)S(1)}, u32[]{:S(2)}, u32[]{:S(2)}) collective-permute-start(bf16[2,288,256]{2,1,0:T(8,128)(2,1)S(1)} %get-tuple-element.22.refs_1_), channel_id=1, source_target_pairs={{0,4},{1,5},{2,6},{3,7},{4,0},{5,1},{6,2},{7,3},{8,12},{9,13},{10,... | collective-permute-start | bytes 884744 | tf_op jit(solution)/shard_map/ppermute | solution.py:116
  31.2 16.1 %collective-permute-start.4 = (bf16[2,288,256]{2,1,0:T(8,128)(2,1)S(1)}, bf16[2,288,256]{2,1,0:T(8,128)(2,1)S(1)}, u32[]{:S(2)}, u32[]{:S(2)}) collective-permute-start(bf16[2,288,256]{2,1,0:T(8,128)(2,1)S(1)} %get-tuple-element.22.refs_1_), channel_id=1, source_target_pairs={{0,16},{1,9},{2,18},{3,11},{4,20},{5,13},{6,22},{7,15},{8,24},{9,1... | collective-permute-start | bytes 884744 | tf_op jit(solution)/shard_map/ppermute | solution.py:119
  32.8 15.0 %collective-permute-start.5 = (bf16[2,288,256]{2,1,0:T(8,128)(2,1)S(1)}, bf16[2,288,256]{2,1,0:T(8,128)(2,1)S(1)}, u32[]{:S(2)}, u32[]{:S(2)}) collective-permute-start(bf16[2,288,256]{2,1,0:T(8,128)(2,1)S(1)} %collective-permute-done.3.refs_2_), channel_id=1, source_target_pairs={{0,16},{1,9},{2,18},{3,11},{4,20},{5,13},{6,22},{7,15},{8,24},{9,1... | collective-permute-start | bytes 884744 | tf_op jit(solution)/shard_map/ppermute | solution.py:119
  42.9 9.9 %collective-permute-start.9 = (bf16[2,288,256]{2,1,0:T(8,128)(2,1)S(1)}, bf16[2,288,256]{2,1,0:T(8,128)(2,1)S(1)}, u32[]{:S(2)}, u32[]{:S(2)}) collective-permute-start(bf16[2,288,256]{2,1,0:T(8,128)(2,1)S(1)} %collective-permute-done.7.refs_6_), channel_id=1, source_target_pairs={{0,16},{1,9},{2,18},{3,11},{4,20},{5,13},{6,22},{7,15},{8,24},{9,1... | collective-permute-start | bytes 884744 | tf_op jit(solution)/shard_map/ppermute | solution.py:119
  45.3 7.6 %collective-permute-start.13 = (bf16[2,288,256]{2,1,0:T(8,128)(2,1)S(1)}, bf16[2,288,256]{2,1,0:T(8,128)(2,1)S(1)}, u32[]{:S(2)}, u32[]{:S(2)}) collective-permute-start(bf16[2,288,256]{2,1,0:T(8,128)(2,1)S(1)} %collective-permute-done.12.refs_11_), channel_id=1, source_target_pairs={{0,8},{1,17},{2,10},{3,19},{4,12},{5,21},{6,14},{7,23},{8,0},{9,25... | collective-permute-start | bytes 884744 | tf_op jit(solution)/shard_map/ppermute | solution.py:119
  46.0 13.0 %collective-permute-start.8 = (bf16[2,288,256]{2,1,0:T(8,128)(2,1)S(1)}, bf16[2,288,256]{2,1,0:T(8,128)(2,1)S(1)}, u32[]{:S(2)}, u32[]{:S(2)}) collective-permute-start(bf16[2,288,256]{2,1,0:T(8,128)(2,1)S(1)} %collective-permute-done.7.refs_6_), channel_id=1, source_target_pairs={{0,8},{1,17},{2,10},{3,19},{4,12},{5,21},{6,14},{7,23},{8,0},{9,25... | collective-permute-start | bytes 884744 | tf_op jit(solution)/shard_map/ppermute | solution.py:119
  47.3 11.7 %collective-permute-start.17 = (bf16[2,288,256]{2,1,0:T(8,128)(2,1)S(1)}, bf16[2,288,256]{2,1,0:T(8,128)(2,1)S(1)}, u32[]{:S(2)}, u32[]{:S(2)}) collective-permute-start(bf16[2,288,256]{2,1,0:T(8,128)(2,1)S(1)} %collective-permute-done.12.refs_11_), channel_id=1, source_target_pairs={{0,2},{1,3},{2,0},{3,1},{4,6},{5,7},{6,4},{7,5},{8,10},{9,11},{10,... | collective-permute-start | bytes 884744 | tf_op jit(solution)/shard_map/ppermute | solution.py:116
  47.7 12.7 %collective-permute-start.10 = (bf16[2,288,256]{2,1,0:T(8,128)(2,1)S(1)}, bf16[2,288,256]{2,1,0:T(8,128)(2,1)S(1)}, u32[]{:S(2)}, u32[]{:S(2)}) collective-permute-start(bf16[2,288,256]{2,1,0:T(8,128)(2,1)S(1)} %collective-permute-done.5.refs_4_), channel_id=1, source_target_pairs={{0,2},{1,3},{2,0},{3,1},{4,6},{5,7},{6,4},{7,5},{8,10},{9,11},{10,... | collective-permute-start | bytes 884744 | tf_op jit(solution)/shard_map/ppermute | solution.py:116
  52.7 10.3 %collective-permute-start.14 = (bf16[2,288,256]{2,1,0:T(8,128)(2,1)S(1)}, bf16[2,288,256]{2,1,0:T(8,128)(2,1)S(1)}, u32[]{:S(2)}, u32[]{:S(2)}) collective-permute-start(bf16[2,288,256]{2,1,0:T(8,128)(2,1)S(1)} %collective-permute-done.12.refs_11_), channel_id=1, source_target_pairs={{0,16},{1,9},{2,18},{3,11},{4,20},{5,13},{6,22},{7,15},{8,24},{9,1... | collective-permute-start | bytes 884744 | tf_op jit(solution)/shard_map/ppermute | solution.py:119
  52.9 10.2 %collective-permute-start.15 = (bf16[2,288,256]{2,1,0:T(8,128)(2,1)S(1)}, bf16[2,288,256]{2,1,0:T(8,128)(2,1)S(1)}, u32[]{:S(2)}, u32[]{:S(2)}) collective-permute-start(bf16[2,288,256]{2,1,0:T(8,128)(2,1)S(1)} %collective-permute-done.13.refs_12_), channel_id=1, source_target_pairs={{0,16},{1,9},{2,18},{3,11},{4,20},{5,13},{6,22},{7,15},{8,24},{9,1... | collective-permute-start | bytes 884744 | tf_op jit(solution)/shard_map/ppermute | solution.py:119
  59.0 18.3 %collective-permute-start.6 = (bf16[8,288,256]{2,1,0:T(8,128)(2,1)S(1)}, bf16[8,288,256]{2,1,0:T(8,128)(2,1)S(1)}, u32[]{:S(2)}, u32[]{:S(2)}) collective-permute-start(bf16[8,288,256]{2,1,0:T(8,128)(2,1)S(1)} %pad_maximum_fusion), channel_id=1, source_target_pairs={{0,1},{1,0},{2,3},{3,2},{4,5},{5,4},{6,7},{7,6},{8,9},{9,8},{10,11... | collective-permute-start | bytes 3538952 | tf_op jit(solution)/shard_map/ppermute | solution.py:122
  59.0 9.7 %collective-permute-start.19 = (bf16[2,288,256]{2,1,0:T(8,128)(2,1)S(1)}, bf16[2,288,256]{2,1,0:T(8,128)(2,1)S(1)}, u32[]{:S(2)}, u32[]{:S(2)}) collective-permute-start(bf16[2,288,256]{2,1,0:T(8,128)(2,1)S(1)} %collective-permute-done.17.refs_17_), channel_id=1, source_target_pairs={{0,16},{1,9},{2,18},{3,11},{4,20},{5,13},{6,22},{7,15},{8,24},{9,1... | collective-permute-start | bytes 884744 | tf_op jit(solution)/shard_map/ppermute | solution.py:119
  60.5 8.3 %collective-permute-start.18 = (bf16[2,288,256]{2,1,0:T(8,128)(2,1)S(1)}, bf16[2,288,256]{2,1,0:T(8,128)(2,1)S(1)}, u32[]{:S(2)}, u32[]{:S(2)}) collective-permute-start(bf16[2,288,256]{2,1,0:T(8,128)(2,1)S(1)} %collective-permute-done.17.refs_17_), channel_id=1, source_target_pairs={{0,8},{1,17},{2,10},{3,19},{4,12},{5,21},{6,14},{7,23},{8,0},{9,25... | collective-permute-start | bytes 884744 | tf_op jit(solution)/shard_map/ppermute | solution.py:119
  63.0 14.3 %collective-permute-start.11 = (bf16[8,288,256]{2,1,0:T(8,128)(2,1)S(1)}, bf16[8,288,256]{2,1,0:T(8,128)(2,1)S(1)}, u32[]{:S(2)}, u32[]{:S(2)}) collective-permute-start(bf16[8,288,256]{2,1,0:T(8,128)(2,1)S(1)} %pad_maximum_fusion.1), channel_id=1, source_target_pairs={{0,1},{1,0},{2,3},{3,2},{4,5},{5,4},{6,7},{7,6},{8,9},{9,8},{10,11... | collective-permute-start | bytes 3538952 | tf_op jit(solution)/shard_map/ppermute | solution.py:122
  63.1 14.2 %copy-start.5 = (f32[8,760]{1,0:T(8,128)S(1)}, f32[8,760]{1,0:T(8,128)}, u32[]{:S(2)}) copy-start(f32[8,760]{1,0:T(8,128)} %constant.45.clone.refs_29_) | copy-start | bytes 72964
  63.3 14.1 %copy-start.1 = (f32[2,760,128]{2,1,0:T(8,128)S(1)}, f32[2,760,128]{2,1,0:T(8,128)}, u32[]{:S(2)}) copy-start(f32[2,760,128]{2,1,0:T(8,128)} %constant.44.clone.refs_28_) | copy-start | bytes 2334724
  63.3 14.1 %copy-start.3 = (bf16[760,384]{1,0:T(8,128)(2,1)S(1)}, bf16[760,384]{1,0:T(8,128)(2,1)}, u32[]{:S(2)}) copy-start(bf16[760,384]{1,0:T(8,128)(2,1)} %constant.42.clone.refs_26_) | copy-start | bytes 1751044
  63.3 14.1 %copy-start.4 = (f32[760,128]{1,0:T(8,128)S(1)}, f32[760,128]{1,0:T(8,128)}, u32[]{:S(2)}) copy-start(f32[760,128]{1,0:T(8,128)} %constant.43.clone.refs_27_) | copy-start | bytes 1167364
  63.3 14.1 %copy-start.6 = (f32[256]{0:T(256)S(1)}, f32[256]{0:T(256)}, u32[]{:S(2)}) copy-start(f32[256]{0:T(256)} %param.19) | copy-start | bytes 3076
  63.3 14.1 %copy-start.7 = (f32[256]{0:T(256)S(1)}, f32[256]{0:T(256)}, u32[]{:S(2)}) copy-start(f32[256]{0:T(256)} %param.20) | copy-start | bytes 3076
  63.3 14.1 %copy-start.8 = (f32[256]{0:T(256)S(1)}, f32[256]{0:T(256)}, u32[]{:S(2)}) copy-start(f32[256]{0:T(256)} %param.21) | copy-start | bytes 3076
  63.4 14.0 %collective-permute-start.16 = (bf16[8,288,256]{2,1,0:T(8,128)(2,1)S(1)}, bf16[8,288,256]{2,1,0:T(8,128)(2,1)S(1)}, u32[]{:S(2)}, u32[]{:S(2)}) collective-permute-start(bf16[8,288,256]{2,1,0:T(8,128)(2,1)S(1)} %pad_maximum_fusion.2), channel_id=1, source_target_pairs={{0,1},{1,0},{2,3},{3,2},{4,5},{5,4},{6,7},{7,6},{8,9},{9,8},{10,11... | collective-permute-start | bytes 3538952 | tf_op jit(solution)/shard_map/ppermute | solution.py:122
  68.8 8.5 %collective-permute-start.20 = (bf16[6,288,256]{2,1,0:T(8,128)(2,1)S(1)}, bf16[6,288,256]{2,1,0:T(8,128)(2,1)S(1)}, u32[]{:S(2)}, u32[]{:S(2)}) collective-permute-start(bf16[6,288,256]{2,1,0:T(8,128)(2,1)S(1)} %pad_maximum_fusion.3), channel_id=1, source_target_pairs={{0,1},{1,0},{2,3},{3,2},{4,5},{5,4},{6,7},{7,6},{8,9},{9,8},{10,11... | collective-permute-start | bytes 2654216 | tf_op jit(solution)/shard_map/ppermute | solution.py:122
  69.0 6.7 %collective-permute-start.21 = (bf16[2,288,256]{2,1,0:T(8,128)(2,1)S(1)}, bf16[2,288,256]{2,1,0:T(8,128)(2,1)S(1)}, u32[]{:S(2)}, u32[]{:S(2)}) collective-permute-start(bf16[2,288,256]{2,1,0:T(8,128)(2,1)S(1)} %collective-permute-done.18.refs_18_), channel_id=1, source_target_pairs={{0,16},{1,9},{2,18},{3,11},{4,20},{5,13},{6,22},{7,15},{8,24},{9,1... | collective-permute-start | bytes 884744 | tf_op jit(solution)/shard_map/ppermute | solution.py:119
  75.7 1.6 %collective-permute-start.22 = (bf16[2,288,256]{2,1,0:T(8,128)(2,1)S(1)}, bf16[2,288,256]{2,1,0:T(8,128)(2,1)S(1)}, u32[]{:S(2)}, u32[]{:S(2)}) collective-permute-start(bf16[2,288,256]{2,1,0:T(8,128)(2,1)S(1)} %collective-permute-done.21.refs_20_), channel_id=1, source_target_pairs={{0,1},{1,0},{2,3},{3,2},{4,5},{5,4},{6,7},{7,6},{8,9},{9,8},{10,11... | collective-permute-start | bytes 884744 | tf_op jit(solution)/shard_map/ppermute | solution.py:122
  (4 other events, 5.3 us)
